TPU v7x, 32 devices: a whole 2x2x4 slice. The times are simulated.
32 devices in a mesh: parts: 2 (over x), tile: 8 (over z, y), chan: 2 (over core).
Axes of the slice: x: 2, y: 2, z: 4, core: 2. Of those that a mesh axis runs over, the one named last changes fastest.
Arguments:
- activations: bfloat16 [384, 16, 16, 128], P(('parts', 'tile')), parts along dimension 0, may hold values from -6 to 6
- cotangent: bfloat16 [384, 16, 16, 128], P(('parts', 'tile')), parts along dimension 0, may hold values from -6 to 6
- neighbours: int32 [192, 4], P('tile'), may hold values from 0 to 191, as said below
- rotations: int32 [192, 4], P('tile'), may hold values from 0 to 3, as said below
- kernels: bfloat16 [2, 7, 7, 128], replicated, may hold values from -0.875 to 0.875
- gains: float32 [2, 128], replicated, may hold values from 0.1 to 1.9
- w_in: bfloat16 [2, 128, 512], P(None, None, 'chan'), may hold values from -0.5 to 0.5
- w_out: bfloat16 [2, 512, 128], P(None, 'chan'), may hold values from -0.25 to 0.25
Outputs:
- input_grads: bfloat16 [384, 16, 16, 128], P(('parts', 'tile')), parts along dimension 0
- kernel_grads: float32 [4, 7, 7, 128], P('parts'), parts along dimension 0
- gain_grads: float32 [4, 128], P('parts'), parts along dimension 0
- w_in_grads: float32 [4, 128, 512], P('parts', None, 'chan'), parts along dimension 0
- w_out_grads: float32 [4, 512, 128], P('parts', 'chan'), parts along dimension 0
There are 2 independent parts, one for each index of `parts`. A program takes and returns all parts, laid end to end along the dimension named above; an argument that names none is the same for every part. Nothing has to cross between parts.
Inputs may be any that keep to these rules, and one draw needn't show every extreme that they name: `neighbours`: tile g lies in block g // 24; the tile across any side of a tile lies in the same block or in the block just before or after it (cyclically, 8 blocks); adjacency is mutual. The rotations of the two sides of a seam add up to 0 mod 4.
All inputs are finite; a program needn't handle non-finite values.
Results may differ from a plain program's by a relative error of at most 0.02.
Values may be sent and summed in bfloat16 or wider, within the bound.
A program may use at most 384 MiB of HBM per device.

v0:
```python
import jax
import jax.numpy as jnp
from jax import lax
from jax.sharding import PartitionSpec as P


def shortened(value):
    return jax.tree.map(lambda a: a.astype(jnp.bfloat16) if a.dtype == jnp.float32 else a, value)


def with_halo(cells, sides, width):
    for axis, dim in sides:
        count = lax.axis_size(axis)
        head = lax.slice_in_dim(cells, 0, width, axis=dim)
        tail = lax.slice_in_dim(cells, cells.shape[dim] - width, cells.shape[dim], axis=dim)
        cells = jnp.concatenate(
            [
                lax.ppermute(tail, axis, [(i, (i + 1) % count) for i in range(count)]),
                cells,
                lax.ppermute(head, axis, [((i + 1) % count, i) for i in range(count)]),
            ],
            axis=dim,
        )
    return cells


def shifted(value, axis, steps):
    count = lax.axis_size(axis)
    pairs = [(source, (source + steps) % count) for source in range(count)]
    return lax.ppermute(value, axis, pairs)


def edge_strips(tile_data, pad_depth):
    return jnp.stack(
        [jnp.rot90(tile_data, quarter, axes=(1, 2))[:, :pad_depth] for quarter in range(4)], 1
    )


def assemble(tile_data, chosen, pad_depth):
    regions = [
        jnp.rot90(chosen[:, side_index], -((side_index + 2) % 4), axes=(1, 2))
        for side_index in range(4)
    ]
    corner = jnp.zeros(
        (tile_data.shape[0], pad_depth, pad_depth, tile_data.shape[3]), tile_data.dtype
    )
    middle = jnp.concatenate([regions[3], tile_data, regions[1]], 2)
    upper_rows = jnp.concatenate([corner, regions[0], corner], 2)
    lower_rows = jnp.concatenate([corner, regions[2], corner], 2)
    return jnp.concatenate([upper_rows, middle, lower_rows], 1)


def slot_index(neighbours, rotations, tile_count):
    groups = lax.axis_size("tile")
    position = lax.axis_index("tile")
    offset = (neighbours // tile_count - position + 1) % groups
    sources = (jnp.arange(4, dtype=jnp.int32)[None, :] + 2 + rotations) % 4
    return (offset * tile_count + neighbours % tile_count) * 4 + sources


def gather_rims(tile_data, neighbours, rotations, pad_depth):
    tile_count = tile_data.shape[0]
    strips = edge_strips(tile_data, pad_depth)
    extended = with_halo(shortened(strips), (("tile", 0),), tile_count).astype(strips.dtype)
    flattened = extended.reshape((extended.shape[0] * 4,) + extended.shape[2:])
    selected = slot_index(neighbours, rotations, tile_count).reshape(-1)
    chosen = jnp.take(flattened, selected, axis=0).reshape((tile_count, 4) + extended.shape[2:])
    return assemble(tile_data, chosen, pad_depth)


def depthwise(padded, kernel):
    kernel_size = kernel.shape[0]
    out_side = padded.shape[1] - kernel_size + 1
    running = jnp.zeros((padded.shape[0], out_side, out_side, padded.shape[3]), jnp.float32)
    for kernel_row in range(kernel_size):
        for kernel_column in range(kernel_size):
            window = padded[
                :, kernel_row : kernel_row + out_side, kernel_column : kernel_column + out_side
            ]
            running = running + window.astype(jnp.float32) * kernel[
                kernel_row, kernel_column
            ].astype(jnp.float32)
    return running


def depthwise_back(padded, grad_hidden, kernel):
    kernel_size = kernel.shape[0]
    out_side = grad_hidden.shape[1]
    grad_padded = jnp.zeros(padded.shape, jnp.float32)
    rows_grad = []
    for kernel_row in range(kernel_size):
        column_grad = []
        for kernel_column in range(kernel_size):
            window = padded[
                :, kernel_row : kernel_row + out_side, kernel_column : kernel_column + out_side
            ]
            column_grad.append(jnp.sum(window.astype(jnp.float32) * grad_hidden, axis=(0, 1, 2)))
            spread = grad_hidden * kernel[kernel_row, kernel_column].astype(jnp.float32)
            grad_padded = grad_padded + jnp.pad(
                spread,
                (
                    (0, 0),
                    (kernel_row, kernel_size - 1 - kernel_row),
                    (kernel_column, kernel_size - 1 - kernel_column),
                    (0, 0),
                ),
            )
        rows_grad.append(jnp.stack(column_grad))
    return (jnp.stack(rows_grad), grad_padded)


def return_rims(grad_padded, neighbours, rotations, pad_depth):
    tile_count = grad_padded.shape[0]
    tile_side = grad_padded.shape[1] - 2 * pad_depth
    inner_end = pad_depth + tile_side
    regions = [
        grad_padded[:, :pad_depth, pad_depth:inner_end],
        grad_padded[:, pad_depth:inner_end, inner_end:],
        grad_padded[:, inner_end:, pad_depth:inner_end],
        grad_padded[:, pad_depth:inner_end, :pad_depth],
    ]
    canon = jnp.stack(
        [
            jnp.rot90(regions[side_index], (side_index + 2) % 4, axes=(1, 2))
            for side_index in range(4)
        ],
        1,
    )
    selected = slot_index(neighbours, rotations, tile_count).reshape(-1)
    slot_ids = jnp.arange(12 * tile_count, dtype=jnp.int32)
    onehot = (slot_ids[:, None] == selected[None, :]).astype(jnp.float32)
    routed = jnp.dot(onehot, canon.reshape(4 * tile_count, -1), precision=lax.Precision.HIGHEST)
    routed = routed.reshape((3, tile_count, 4) + canon.shape[2:])
    from_before = shifted(shortened(routed[2]), "tile", 1)
    from_after = shifted(shortened(routed[0]), "tile", -1)
    grad_strips = routed[1] + from_before + from_after
    running = grad_padded[:, pad_depth:inner_end, pad_depth:inner_end]
    for quarter in range(4):
        placed = jnp.pad(
            grad_strips[:, quarter], ((0, 0), (0, tile_side - pad_depth), (0, 0), (0, 0))
        )
        running = running + jnp.rot90(placed, -quarter, axes=(1, 2))
    return running


def norm_parts(hidden, gain_vector):
    centered = hidden - jnp.mean(hidden, -1, keepdims=True)
    inverse_scale = lax.rsqrt(jnp.mean(centered * centered, -1, keepdims=True) + 1e-06)
    standard = centered * inverse_scale
    return (standard, inverse_scale, (standard * gain_vector).astype(jnp.bfloat16))


def norm_back(grad_normed, standard, inverse_scale, gain_vector):
    scaled = grad_normed * gain_vector
    gain_grad = jnp.sum(grad_normed * standard, 0)
    grad_hidden = inverse_scale * (
        scaled
        - jnp.mean(scaled, -1, keepdims=True)
        - standard * jnp.mean(scaled * standard, -1, keepdims=True)
    )
    return (grad_hidden, gain_grad)


def local(activations, cotangent, neighbours, rotations, kernels, gains, w_in, w_out):
    pad_depth = kernels.shape[1] // 2
    layer_count = kernels.shape[0]
    tile_count, tile_side, _, channels = activations.shape
    pixels = tile_count * tile_side * tile_side
    current = activations
    caches = []
    for layer_index in range(layer_count):
        padded = gather_rims(current, neighbours, rotations, pad_depth)
        hidden = depthwise(padded, kernels[layer_index]).reshape(pixels, channels)
        standard, inverse_scale, normed = norm_parts(hidden, gains[layer_index])
        linear_out = jnp.dot(normed, w_in[layer_index], preferred_element_type=jnp.float32)
        activated = jax.nn.gelu(linear_out).astype(jnp.bfloat16)
        caches.append((padded, standard, inverse_scale, normed, linear_out, activated))
        if layer_index + 1 < layer_count:
            partial_value = jnp.dot(
                activated, w_out[layer_index], preferred_element_type=jnp.float32
            )
            mixed_sum = lax.psum(partial_value.astype(jnp.bfloat16), "chan").astype(jnp.float32)
            current = (current.astype(jnp.float32) + mixed_sum.reshape(current.shape)).astype(
                jnp.bfloat16
            )
    gradient = cotangent.astype(jnp.float32).reshape(pixels, channels)
    layer_grads = [None] * layer_count
    for layer_index in reversed(range(layer_count)):
        padded, standard, inverse_scale, normed, linear_out, activated = caches[layer_index]
        gradient_low = gradient.astype(jnp.bfloat16)
        grad_activated = jnp.dot(
            gradient_low, w_out[layer_index].T, preferred_element_type=jnp.float32
        )
        out_grad = jnp.dot(activated.T, gradient_low, preferred_element_type=jnp.float32)
        gelu_back = jax.vjp(jax.nn.gelu, linear_out)[1]
        grad_linear = gelu_back(grad_activated)[0].astype(jnp.bfloat16)
        in_grad = jnp.dot(normed.T, grad_linear, preferred_element_type=jnp.float32)
        normed_partial = jnp.dot(
            grad_linear, w_in[layer_index].T, preferred_element_type=jnp.float32
        )
        grad_normed = lax.psum(normed_partial.astype(jnp.bfloat16), "chan").astype(jnp.float32)
        grad_hidden, gain_grad = norm_back(grad_normed, standard, inverse_scale, gains[layer_index])
        grad_hidden = grad_hidden.reshape(tile_count, tile_side, tile_side, channels)
        kernel_grad, grad_padded = depthwise_back(padded, grad_hidden, kernels[layer_index])
        returned = return_rims(grad_padded, neighbours, rotations, pad_depth)
        gradient = (gradient.reshape(returned.shape) + returned).reshape(pixels, channels)
        block_terms = (kernel_grad, gain_grad, in_grad, out_grad)
        block_terms = (
            lax.psum(block_terms[0].astype(jnp.bfloat16), "tile").astype(jnp.float32),
            lax.psum(block_terms[1].astype(jnp.bfloat16), "tile").astype(jnp.float32),
            lax.psum(block_terms[2].astype(jnp.bfloat16), "tile").astype(jnp.float32),
            lax.psum(block_terms[3].astype(jnp.bfloat16), "tile").astype(jnp.float32),
        )
        layer_grads[layer_index] = block_terms
    input_grads = gradient.reshape(tile_count, tile_side, tile_side, channels).astype(jnp.bfloat16)
    kernel_grads = jnp.stack([layer_grads[layer_index][0] for layer_index in range(layer_count)])
    gain_grads = jnp.stack([layer_grads[layer_index][1] for layer_index in range(layer_count)])
    w_in_grads = jnp.stack([layer_grads[layer_index][2] for layer_index in range(layer_count)])
    w_out_grads = jnp.stack([layer_grads[layer_index][3] for layer_index in range(layer_count)])
    return (input_grads, kernel_grads, gain_grads, w_in_grads, w_out_grads)


def solution(mesh):
    placed = (
        P(("parts", "tile"), None, None, None),
        P(("parts", "tile"), None, None, None),
        P("tile", None),
        P("tile", None),
        P(),
        P(),
        P(None, None, "chan"),
        P(None, "chan", None),
    )
    return jax.shard_map(
        local,
        mesh=mesh,
        in_specs=placed,
        out_specs=(
            P(("parts", "tile"), None, None, None),
            P("parts", None, None, None),
            P("parts", None),
            P("parts", None, "chan"),
            P("parts", "chan", None),
        ),
        check_vma=False,
    )
```

profile of v0, /device:TPU:0, one launch (start us, length us, event | category | flops | bytes accessed | tf_op | source)
XLA Modules:
  0.0 868.2 jit_solution(14555066360481025918)
XLA Ops:
  14.8 6.0 collective-permute-start.1
  24.9 44.3 %collective-permute-done.1 = bf16[24,4,3,16,128]{4,3,2,1,0:T(8,128)(2,1)S(1)} collective-permute-done((bf16[24,4,3,16,128]{4,3,2,1,0:T(8,128)(2,1)}, bf16[24,4,3,16,128]{4,3,2,1,0:T(8,128)(2,1)S(1)}, u32[]{:S(2)}, u32[]{:S(2)}) %collective-permute-start.1) | collective-permute-done | bytes 1179680 | tf_op jit(solution)/shard_map/ppermute | solution.py:20
  84.5 24.7 %fusion.383 = (f32[24,16,16]{2,1,0:T(8,128)S(1)}, f32[24,16,16,128]{3,2,1,0:T(8,128)S(1)}) fusion(f32[128]{0:T(128)S(1)} %copy-done.74, bf16[24,19,22,128]{3,2,1,0:T(8,128)(2,1)S(1)} %get-tuple-element.294, f32[128]{0:T(128)S(1)} %copy-done.76, f32[128]{0:T(128)S(1)} %copy-done.80, f32[128]{0:T(128)S(1)} %copy-done.82, f32[128]{0:T(128)S(1)} %copy-done.84, ...), kind=kLoop, calls=%fused_computation.1028 | loop fusion | flops 129755136 | bytes 71418368 | tf_op jit(solution)/shard_map/reduce_sum | solution.py:147
  119.9 20.8 %all-reduce.113.cloned.1.call-done = bf16[24,16,16,128]{3,2,1,0:T(8,128)(2,1)} async-done(((bf16[24,16,16,128]{3,2,1,0:T(8,128)(2,1)}), bf16[24,16,16,128]{3,2,1,0:T(8,128)(2,1)}) %all-reduce.113.cloned.1.call-update) | async-done | bytes 1572880 | tf_op jit(solution)/shard_map/psum | solution.py:182
  157.6 47.0 %collective-permute-done.3 = bf16[24,4,3,16,128]{4,3,2,1,0:T(8,128)(2,1)S(1)} collective-permute-done((bf16[24,4,3,16,128]{4,3,2,1,0:T(8,128)(2,1)S(1)}, bf16[24,4,3,16,128]{4,3,2,1,0:T(8,128)(2,1)S(1)}, u32[]{:S(2)}, u32[]{:S(2)}) %collective-permute-start.3) | collective-permute-done | bytes 1179680 | tf_op jit(solution)/shard_map/ppermute | solution.py:20
  206.3 13.8 %pad_maximum_fusion = bf16[72,4,3,16,128]{4,2,3,0,1:T(4,128)(2,1)S(1)} fusion(bf16[24,4,3,16,128]{4,2,3,0,1:T(4,128)(2,1)S(1)} %copy.1091, bf16[24,1,3,16,128]{4,2,3,0,1:T(4,128)(2,1)S(1)} %reverse_bitcast_fusion.4, bf16[24,1,3,16,128]{4,2,3,0,1:T(4,128)(2,1)S(1)} %bitcast.1078, bf16[24,1,3,16,128]{4,2,3,0,1:T(4,128)(2,1)S(1)} %slice_bitcast_fusion.14, ...), kind=kLoop, calls=%fused_computation.30 | loop fusion | flops 8847360 | bytes 7077888 | tf_op jit(solution)/shard_map/concatenate | solution.py:16
  233.5 24.7 %fusion.381 = (f32[24,16,16]{2,1,0:T(8,128)S(1)}, f32[24,16,16,128]{3,2,1,0:T(8,128)S(1)}) fusion(f32[128]{0:T(128)S(1)} %copy-done.78, bf16[24,19,22,128]{3,2,1,0:T(8,128)(2,1)S(1)} %get-tuple-element.292, f32[128]{0:T(128)S(1)} %copy-done.79, f32[128]{0:T(128)S(1)} %copy-done.110, f32[128]{0:T(128)S(1)} %copy-done.111, f32[128]{0:T(128)S(1)} %copy-done.112, ...), kind=kLoop, calls=%fused_computation.1027 | loop fusion | flops 129755136 | bytes 71418368 | tf_op jit(solution)/shard_map/reduce_sum | solution.py:147
  276.8 6.7 fusion.250
  283.5 10.0 %all-reduce.115.cloned.1.call-done = bf16[6144,128]{1,0:T(8,128)(2,1)} async-done(((bf16[6144,128]{1,0:T(8,128)(2,1)}), bf16[6144,128]{1,0:T(8,128)(2,1)}) %all-reduce.115.cloned.1.call-update) | async-done | bytes 1572880 | tf_op jit(solution)/shard_map/psum | solution.py:201
  293.5 7.1 fusion.216
  306.2 8.4 fusion.161
  314.7 6.9 fusion.194
  321.8 14.2 %broadcast_multiply_fusion.47 = (f32[24,16,16,128]{3,2,1,0:T(8,128)}, f32[24,16,16,128]{3,2,1,0:T(8,128)}, f32[24,16,16,128]{3,2,1,0:T(8,128)}, f32[24,16,16,128...) fusion(f32[24,16,16,128]{3,2,1,0:T(8,128)S(1)} %bitcast.1053, ...), kind=kLoop, calls=%fused_computation.558 | loop fusion | flops 11010048 | bytes 47193088 | tf_op jit(solution)/shard_map/mul | solution.py:98
  336.1 17.7 %fusion.143 = (bf16[128]{0:T(256)(128)(2,1)S(1)}, bf16[128]{0:T(256)(128)(2,1)S(1)}, bf16[128]{0:T(256)(128)(2,1)S(1)}, f32[24,16,16,128]{3,2,1,0:T(8,128)}, f32...) fusion(f32[24,16,16,128]{3,2,1,0:T(8,128)} %bitcast.1054, ...), kind=kLoop, calls=%fused_computation.367 | loop fusion | flops 18873984 | bytes 55058688 | tf_op jit(solution)/shard_map/reduce_sum | solution.py:97
  354.0 19.4 %broadcast_multiply_fusion.48 = (f32[24,16,16,128]{3,2,1,0:T(8,128)}, f32[24,16,16,128]{3,2,1,0:T(8,128)}, f32[24,16,16,128]{3,2,1,0:T(8,128)}, f32[24,16,16,128...) fusion(f32[24,16,16,128]{3,2,1,0:T(8,128)} %bitcast.1055, ...), kind=kLoop, calls=%fused_computation.559 | loop fusion | flops 14155776 | bytes 59778048 | tf_op jit(solution)/shard_map/mul | solution.py:98
  373.4 49.0 %pad_add_fusion.1 = f32[24,22,22,128]{3,2,1,0:T(8,128)S(1)} fusion(f32[24,16,16,128]{3,2,1,0:T(8,128)} %get-tuple-element.210, f32[24,16,16,128]{3,2,1,0:T(8,128)} %get-tuple-element.211, f32[24,16,16,128]{3,2,1,0:T(8,128)} %get-tuple-element.212, f32[24,16,16,128]{3,2,1,0:T(8,128)} %get-tuple-element.213, f32[24,16,16,128]{3,2,1,0:T(8,128)} %get-tuple-element.214, ...), kind=kLoop, calls=%fused_computation.10 | loop fusion | flops 71368704 | bytes 160088064 | tf_op jit(solution)/shard_map/add | solution.py:99
  457.3 8.0 fusion.212
  466.4 40.1 %collective-permute-done.5 = bf16[24,4,3,16,128]{4,3,2,1,0:T(8,128)(2,1)} collective-permute-done((bf16[24,4,3,16,128]{4,3,2,1,0:T(8,128)(2,1)}, bf16[24,4,3,16,128]{4,3,2,1,0:T(8,128)(2,1)}, u32[]{:S(2)}, u32[]{:S(2)}) %collective-permute-start.5) | collective-permute-done | bytes 1179680 | tf_op jit(solution)/shard_map/ppermute | solution.py:30
  525.2 6.2 rev.110
  539.4 6.5 fusion.6
  557.0 14.6 %all-reduce.117.cloned.1.call-done = bf16[6144,128]{1,0:T(8,128)(2,1)} async-done(((bf16[6144,128]{1,0:T(8,128)(2,1)}), bf16[6144,128]{1,0:T(8,128)(2,1)}) %all-reduce.117.cloned.1.call-update) | async-done | bytes 1572880 | tf_op jit(solution)/shard_map/psum | solution.py:201
  571.6 7.0 fusion.220
  578.7 5.5 multiply_convert_fusion.3
  584.2 8.4 fusion.65
  592.6 8.5 fusion.115
  601.2 7.5 fusion.97
  609.1 14.2 %broadcast_multiply_fusion.96 = (f32[24,16,16,128]{3,2,1,0:T(8,128)}, f32[24,16,16,128]{3,2,1,0:T(8,128)}, f32[24,16,16,128]{3,2,1,0:T(8,128)}, f32[24,16,16,128...) fusion(f32[24,16,16,128]{3,2,1,0:T(8,128)S(1)} %bitcast.1060, ...), kind=kLoop, calls=%fused_computation.607 | loop fusion | flops 11010048 | bytes 47193088 | tf_op jit(solution)/shard_map/mul | solution.py:98
  623.6 16.6 %fusion.47 = (bf16[128]{0:T(256)(128)(2,1)S(1)}, bf16[128]{0:T(256)(128)(2,1)S(1)}, bf16[128]{0:T(256)(128)(2,1)S(1)}, f32[24,16,16,128]{3,2,1,0:T(8,128)}, f32[...) fusion(f32[24,16,16,128]{3,2,1,0:T(8,128)} %bitcast.1061, ...), kind=kLoop, calls=%fused_computation.271 | loop fusion | flops 18873984 | bytes 55058688 | tf_op jit(solution)/shard_map/reduce_sum | solution.py:97
  640.4 18.5 %broadcast_multiply_fusion.97 = (f32[24,16,16,128]{3,2,1,0:T(8,128)S(1)}, f32[24,16,16,128]{3,2,1,0:T(8,128)}, f32[24,16,16,128]{3,2,1,0:T(8,128)}, f32[24,16,16...) fusion(f32[24,16,16,128]{3,2,1,0:T(8,128)} %bitcast.1062, ...), kind=kLoop, calls=%fused_computation.608 | loop fusion | flops 14155776 | bytes 59778048 | tf_op jit(solution)/shard_map/mul | solution.py:98
  658.9 48.0 %pad_add_fusion = f32[24,22,22,128]{3,2,1,0:T(8,128)S(1)} fusion(f32[24,16,16,128]{3,2,1,0:T(8,128)} %get-tuple-element.193, f32[24,16,16,128]{3,2,1,0:T(8,128)} %get-tuple-element.194, f32[24,16,16,128]{3,2,1,0:T(8,128)} %get-tuple-element.195, f32[24,16,16,128]{3,2,1,0:T(8,128)} %get-tuple-element.196, f32[24,16,16,128]{3,2,1,0:T(8,128)} %get-tuple-element.197, ...), kind=kLoop, calls=%fused_computation.9 | loop fusion | flops 71368704 | bytes 160088064 | tf_op jit(solution)/shard_map/add | solution.py:99
  741.2 76.0 %all-reduce.106 = (bf16[1,7,7,128]{3,2,1,0:T(8,128)(2,1)S(1)}, bf16[1,7,7,128]{3,2,1,0:T(8,128)(2,1)S(1)}, bf16[1,128]{1,0:T(2,128)(2,1)}, bf16[1,128]{1,0:T(2,128)(2,1)}) all-reduce(bf16[1,7,7,128]{3,2,1,0:T(8,128)(2,1)S(1)} %bitcast.1098, ...), channel_id=1, replica_groups=mesh['parts'=2,'tile'=8,'chan'=2] {'tile'}, use_global_device_ids=true, to_apply=%region_110.112 | all-reduce | flops 12800 | bytes 51200 | tf_op jit(solution)/shard_map/psum | solution.py:209
  820.5 8.5 all-reduce.119.cloned.1.call-done
  (763 shorter events, 234.7 us)
Async XLA Ops:
  7.2 133.5 %all-reduce.113.cloned.1.call-start = ((), (), s32[]{:S(2)}) async-start(), calls=%async_computation | async-start | bytes 3145728 | tf_op jit(solution)/shard_map/psum | solution.py:182
  12.5 56.7 %copy-start.50 = (bf16[24,3,16,128]{3,2,1,0:T(8,128)(2,1)}, bf16[24,3,16,128]{3,2,1,0:T(8,128)(2,1)S(1)}, u32[]{:S(2)}) copy-start(bf16[24,3,16,128]{3,2,1,0:T(8,128)(2,1)S(1)} %slice.1050) | copy-start | bytes 884740
  13.6 55.6 %copy-start.51 = (bf16[24,1,3,16,128]{4,3,2,1,0:T(8,128)(2,1)}, bf16[24,1,3,16,128]{4,3,2,1,0:T(8,128)(2,1)S(1)}, u32[]{:S(2)}) copy-start(bf16[24,1,3,16,128]{4,3,2,1,0:T(8,128)(2,1)S(1)} %slice_bitcast_fusion.19) | copy-start | bytes 884740
  14.8 54.4 %collective-permute-start.1 = (bf16[24,4,3,16,128]{4,3,2,1,0:T(8,128)(2,1)}, bf16[24,4,3,16,128]{4,3,2,1,0:T(8,128)(2,1)S(1)}, u32[]{:S(2)}, u32[]{:S(2)}) collective-permute-start(bf16[24,4,3,16,128]{4,3,2,1,0:T(8,128)(2,1)} %pad_maximum_fusion.17), channel_id=1, source_target_pairs={{2,0},{4,2},{6,4},{8,6},{10,8},{12,10},{14,12},{0,14},{3,1},{5,3},... | collective-permute-start | bytes 3538952 | tf_op jit(solution)/shard_map/ppermute | solution.py:20
  20.8 49.4 %collective-permute-start = (bf16[24,4,3,16,128]{4,3,2,1,0:T(8,128)(2,1)}, bf16[24,4,3,16,128]{4,3,2,1,0:T(8,128)(2,1)}, u32[]{:S(2)}, u32[]{:S(2)}) collective-permute-start(bf16[24,4,3,16,128]{4,3,2,1,0:T(8,128)(2,1)} %pad_maximum_fusion.17), channel_id=1, source_target_pairs={{0,2},{2,4},{4,6},{6,8},{8,10},{10,12},{12,14},{14,0},{1,3},{3,5},... | collective-permute-start | bytes 3538952 | tf_op jit(solution)/shard_map/ppermute | solution.py:18
  84.1 25.2 %copy-start = (bf16[24,19,22,128]{3,2,1,0:T(8,128)(2,1)}, bf16[24,19,22,128]{3,2,1,0:T(8,128)(2,1)S(1)}, u32[]{:S(2)}) copy-start(bf16[24,19,22,128]{3,2,1,0:T(8,128)(2,1)S(1)} %get-tuple-element.293) | copy-start | bytes 7704580
  84.1 25.2 %copy-start.2 = (bf16[24,19,22,128]{3,2,1,0:T(8,128)(2,1)}, bf16[24,19,22,128]{3,2,1,0:T(8,128)(2,1)S(1)}, u32[]{:S(2)}) copy-start(bf16[24,19,22,128]{3,2,1,0:T(8,128)(2,1)S(1)} %get-tuple-element.294) | copy-start | bytes 7704580
  119.4 174.1 %all-reduce.115.cloned.1.call-start = ((), (), s32[]{:S(2)}) async-start(), calls=%async_computation.1 | async-start | bytes 3145728 | tf_op jit(solution)/shard_map/psum | solution.py:201
  151.0 53.5 %collective-permute-start.3 = (bf16[24,4,3,16,128]{4,3,2,1,0:T(8,128)(2,1)S(1)}, bf16[24,4,3,16,128]{4,3,2,1,0:T(8,128)(2,1)S(1)}, u32[]{:S(2)}, u32[]{:S(2)}) collective-permute-start(bf16[24,4,3,16,128]{4,3,2,1,0:T(8,128)(2,1)S(1)} %copy.1088), channel_id=1, source_target_pairs={{2,0},{4,2},{6,4},{8,6},{10,8},{12,10},{14,12},{0,14},{3,1},{5,3},... | collective-permute-start | bytes 3538952 | tf_op jit(solution)/shard_map/ppermute | solution.py:20
  155.6 49.8 %collective-permute-start.2 = (bf16[24,4,3,16,128]{4,3,2,1,0:T(8,128)(2,1)S(1)}, bf16[24,4,3,16,128]{4,3,2,1,0:T(8,128)(2,1)S(1)}, u32[]{:S(2)}, u32[]{:S(2)}) collective-permute-start(bf16[24,4,3,16,128]{4,3,2,1,0:T(8,128)(2,1)S(1)} %copy.1088), channel_id=1, source_target_pairs={{0,2},{2,4},{4,6},{6,8},{8,10},{10,12},{12,14},{14,0},{1,3},{3,5},... | collective-permute-start | bytes 3538952 | tf_op jit(solution)/shard_map/ppermute | solution.py:18
  233.1 25.2 %copy-start.4 = (bf16[24,19,22,128]{3,2,1,0:T(8,128)(2,1)}, bf16[24,19,22,128]{3,2,1,0:T(8,128)(2,1)S(1)}, u32[]{:S(2)}) copy-start(bf16[24,19,22,128]{3,2,1,0:T(8,128)(2,1)S(1)} %get-tuple-element.291) | copy-start | bytes 7704580
  272.3 299.2 %all-reduce.117.cloned.1.call-start = ((), (), s32[]{:S(2)}) async-start(), calls=%async_computation.2 | async-start | bytes 3145728 | tf_op jit(solution)/shard_map/psum | solution.py:201
  336.0 17.9 %copy-start.181 = (f32[128]{0:T(128)S(1)}, f32[128]{0:T(128)}, u32[]{:S(2)}) copy-start(f32[128]{0:T(128)} %get-tuple-element.339) | copy-start | bytes 1540
  336.0 17.9 %copy-start.183 = (f32[128]{0:T(128)S(1)}, f32[128]{0:T(128)}, u32[]{:S(2)}) copy-start(f32[128]{0:T(128)} %get-tuple-element.340) | copy-start | bytes 1540
  336.0 17.9 %copy-start.185 = (f32[128]{0:T(128)S(1)}, f32[128]{0:T(128)}, u32[]{:S(2)}) copy-start(f32[128]{0:T(128)} %get-tuple-element.341) | copy-start | bytes 1540
  336.0 17.9 %copy-start.187 = (f32[128]{0:T(128)S(1)}, f32[128]{0:T(128)}, u32[]{:S(2)}) copy-start(f32[128]{0:T(128)} %get-tuple-element.342) | copy-start | bytes 1540
  336.0 17.9 %copy-start.189 = (f32[128]{0:T(128)S(1)}, f32[128]{0:T(128)}, u32[]{:S(2)}) copy-start(f32[128]{0:T(128)} %get-tuple-element.343) | copy-start | bytes 1540
  336.0 17.9 %copy-start.191 = (f32[128]{0:T(128)S(1)}, f32[128]{0:T(128)}, u32[]{:S(2)}) copy-start(f32[128]{0:T(128)} %get-tuple-element.344) | copy-start | bytes 1540
  336.0 17.9 %copy-start.193 = (f32[128]{0:T(128)S(1)}, f32[128]{0:T(128)}, u32[]{:S(2)}) copy-start(f32[128]{0:T(128)} %get-tuple-element.345) | copy-start | bytes 1540
  336.0 17.9 %copy-start.195 = (f32[128]{0:T(128)S(1)}, f32[128]{0:T(128)}, u32[]{:S(2)}) copy-start(f32[128]{0:T(128)} %get-tuple-element.346) | copy-start | bytes 1540
  336.1 17.9 %copy-start.197 = (f32[128]{0:T(128)S(1)}, f32[128]{0:T(128)}, u32[]{:S(2)}) copy-start(f32[128]{0:T(128)} %get-tuple-element.347) | copy-start | bytes 1540
  336.1 17.9 %copy-start.199 = (f32[128]{0:T(128)S(1)}, f32[128]{0:T(128)}, u32[]{:S(2)}) copy-start(f32[128]{0:T(128)} %get-tuple-element.348) | copy-start | bytes 1540
  452.8 53.8 %collective-permute-start.5 = (bf16[24,4,3,16,128]{4,3,2,1,0:T(8,128)(2,1)}, bf16[24,4,3,16,128]{4,3,2,1,0:T(8,128)(2,1)}, u32[]{:S(2)}, u32[]{:S(2)}) collective-permute-start(bf16[24,4,3,16,128]{4,3,2,1,0:T(8,128)(2,1)} %bitcast.410), channel_id=1, source_target_pairs={{0,14},{2,0},{4,2},{6,4},{8,6},{10,8},{12,10},{14,12},{1,15},{3,1}... | collective-permute-start | bytes 3538952 | tf_op jit(solution)/shard_map/ppermute | solution.py:30
  457.3 49.4 %collective-permute-start.4 = (bf16[24,4,3,16,128]{4,3,2,1,0:T(8,128)(2,1)}, bf16[24,4,3,16,128]{4,3,2,1,0:T(8,128)(2,1)}, u32[]{:S(2)}, u32[]{:S(2)}) collective-permute-start(bf16[24,4,3,16,128]{4,3,2,1,0:T(8,128)(2,1)} %bitcast.407), channel_id=1, source_target_pairs={{0,2},{2,4},{4,6},{6,8},{8,10},{10,12},{12,14},{14,0},{1,3},{3,5},... | collective-permute-start | bytes 3538952 | tf_op jit(solution)/shard_map/ppermute | solution.py:30
  549.7 279.2 %all-reduce.119.cloned.1.call-start = ((), (), s32[]{:S(2)}) async-start(), calls=%async_computation.3 | async-start | bytes 524288 | tf_op jit(solution)/shard_map/psum | solution.py:211
  553.3 18.3 %copy-start.10 = (f32[24,16,16,128]{3,2,1,0:T(8,128)S(1)}, f32[24,16,16,128]{3,2,1,0:T(8,128)}, u32[]{:S(2)}) copy-start(f32[24,16,16,128]{3,2,1,0:T(8,128)} %copy-done.9) | copy-start | bytes 9437188
  553.3 18.3 %copy-start.60 = (f32[6144]{0:T(1024)S(1)}, f32[6144]{0:T(1024)}, u32[]{:S(2)}) copy-start(f32[6144]{0:T(1024)} %div.49) | copy-start | bytes 73732
  553.3 18.3 %copy-start.61 = (f32[6144]{0:T(1024)S(1)}, f32[6144]{0:T(1024)}, u32[]{:S(2)}) copy-start(f32[6144]{0:T(1024)} %rsqrt.27) | copy-start | bytes 73732
  553.3 18.3 %copy-start.72 = (f32[128]{0:T(128)S(1)}, f32[128]{0:T(128)}, u32[]{:S(2)}) copy-start(f32[128]{0:T(128)} %get-tuple-element.418) | copy-start | bytes 1540
  584.2 24.6 %copy-start.8 = (f32[6144,128]{1,0:T(8,128)}, f32[6144,128]{1,0:T(8,128)S(1)}, u32[]{:S(2)}) copy-start(f32[6144,128]{1,0:T(8,128)S(1)} %get-tuple-element.190) | copy-start | bytes 9437188
  731.9 100.3 %collective-permute-start.6 = (bf16[24,4,3,16,128]{4,3,2,1,0:T(8,128)(2,1)}, bf16[24,4,3,16,128]{4,3,2,1,0:T(8,128)(2,1)S(1)}, u32[]{:S(2)}, u32[]{:S(2)}) collective-permute-start(bf16[24,4,3,16,128]{4,3,2,1,0:T(8,128)(2,1)} %bitcast.417), channel_id=1, source_target_pairs={{0,2},{2,4},{4,6},{6,8},{8,10},{10,12},{12,14},{14,0},{1,3},{3,5},... | collective-permute-start | bytes 3538952 | tf_op jit(solution)/shard_map/ppermute | solution.py:30
  733.6 98.5 %collective-permute-start.7 = (bf16[24,4,3,16,128]{4,3,2,1,0:T(8,128)(2,1)}, bf16[24,4,3,16,128]{4,3,2,1,0:T(8,128)(2,1)}, u32[]{:S(2)}, u32[]{:S(2)}) collective-permute-start(bf16[24,4,3,16,128]{4,3,2,1,0:T(8,128)(2,1)} %bitcast.420), channel_id=1, source_target_pairs={{0,14},{2,0},{4,2},{6,4},{8,6},{10,8},{12,10},{14,12},{1,15},{3,1}... | collective-permute-start | bytes 3538952 | tf_op jit(solution)/shard_map/ppermute | solution.py:30
  (266 other events, 1977.0 us)
Sparse Core Ops, SparseCore 0:
  119.5 21.1 all-reduce.112
  272.5 20.9 all-reduce.114
  549.9 21.6 all-reduce.116
  737.8 91.0 all-reduce.118
where the time goes:
time: 878 us; the launch traced here: 868 us
  other arithmetic  392 us (45%)
  waiting for transfers between devices  186 us (21%)
  local copies, waits for them, and re-layouts  129 us (15%)
  blocking collectives  76 us (9%)
  matrix products  46.9 us (5%)
  starting transfers between devices  20.4 us (2%)
  between operations  18.5 us (2%)
    add x2, other arithmetic, depthwise_back(): grad_padded + jnp.pad(spread, ((0, 0), (kernel_row, kernel_size - 1 - ker...  97.1 us
    ppermute x2, waiting for transfers between devices, with_halo(): lax.ppermute(head, axis, [((i + 1) % count, i) for i in range(count)])  91.3 us
    reduce_sum x8, other arithmetic, depthwise_back(): jnp.sum(window.astype(jnp.float32) * grad_hidden, axis=(0, 1, 2))  82.1 us
    psum x1, blocking collectives, local(): lax.psum(block_terms[0].astype(jnp.bfloat16), 'tile').astype(jnp.float32)  76 us
    mul x4, other arithmetic, depthwise_back(): spread = grad_hidden * kernel[kernel_row, kernel_column].astype(jnp.float32)  66.3 us
    reduce_sum x2, other arithmetic, norm_parts(): centered = hidden - jnp.mean(hidden, -1, keepdims=True)  49.5 us
    ppermute x4, waiting for transfers between devices, shifted(): return lax.ppermute(value, axis, pairs)  40.3 us
    unnamed x607, local copies, waits for them, and re-layouts  35.7 us
  transfers between devices with their start and end apart: 12, of which 8 were waited for; matrix products, arithmetic and copies ran while one was open for 5% of the time, Pallas kernels for 0%

commit v1 on v0

v1 whole, which is shorter than its diff:
```python
import jax
import jax.numpy as jnp
import numpy as np
from jax import lax
from jax.experimental import pallas as pl
from jax.experimental.pallas import tpu as pltpu
from jax.sharding import PartitionSpec as P

BF = jnp.bfloat16
F32 = jnp.float32
KS = 7
PAD = 3
S = 16
EDGE = PAD * S
LANES = 128


def permutation_tables():
    pixel = np.arange(S * S).reshape(S, S)
    extract = np.zeros((4 * EDGE, S * S), np.float32)
    for quarter in range(4):
        source = np.rot90(pixel, quarter)[:PAD].reshape(-1)
        extract[quarter * EDGE + np.arange(EDGE), source] = 1
    strip = np.arange(EDGE).reshape(PAD, S)
    top = np.zeros((EDGE, EDGE), np.float32)
    top[np.arange(EDGE), np.rot90(strip, -2).reshape(-1)] = 1
    right = np.zeros((S, 8, EDGE), np.float32)
    left = np.zeros((S, 8, EDGE), np.float32)
    for i in range(S):
        for j in range(PAD):
            right[i, j, np.rot90(strip, -3)[i, j]] = 1
            left[i, 8 - PAD + j, np.rot90(strip, -1)[i, j]] = 1
    return extract, top, right.reshape(S * 8, EDGE), left.reshape(S * 8, EDGE)


def mm(a, b):
    return jnp.dot(a, b, preferred_element_type=F32)


def fill_shifted(x_ref, strips_ref, top_ref, right_ref, left_ref, pad_ref, sh_ref):
    @pl.when(pl.program_id(0) == 0)
    def _():
        pad_ref[...] = jnp.zeros_like(pad_ref)

    end = PAD + S
    pad_ref[PAD:end, 8:24] = x_ref[0].astype(F32)
    pad_ref[0:PAD, 8:24] = mm(top_ref[...], strips_ref[0, 0]).reshape(PAD, S, LANES)
    pad_ref[end:, 8:24] = strips_ref[0, 2].astype(F32).reshape(PAD, S, LANES)
    pad_ref[PAD:end, 24:32] = mm(right_ref[...], strips_ref[0, 1]).reshape(S, 8, LANES)
    pad_ref[PAD:end, 0:8] = mm(left_ref[...], strips_ref[0, 3]).reshape(S, 8, LANES)
    for b in range(KS):
        sh_ref[b] = pad_ref[:, 5 + b : 21 + b, :].reshape(S + 2 * PAD, 2, 8, LANES)


def depthwise(sh_ref, kern_ref, hid_ref):
    def body(block, carry):
        row = block * 4
        acc = jnp.zeros((4, 2, 8, LANES), F32)
        for b in range(KS):
            col = sh_ref[b, pl.ds(row, 4 + KS - 1)]
            for a in range(KS):
                acc = acc + col[a : a + 4] * kern_ref[b * KS + a][None, None]
        hid_ref[pl.ds(row, 4)] = acc
        return carry

    lax.fori_loop(0, S // 4, body, 0)


def normalise(hidden, gain):
    centered = hidden - jnp.mean(hidden, -1, keepdims=True)
    inverse = lax.rsqrt(jnp.mean(centered * centered, -1, keepdims=True) + 1e-06)
    standard = centered * inverse
    return standard, inverse, (standard * gain).astype(BF)


ROOT = 0.7978845608028654
CUBE = 0.044715


def forward_kernel(
    off_ref, x_ref, strips_ref, top_ref, right_ref, left_ref, extract_ref, kern_ref, gain_ref, w_in_ref, w_out_ref,
    hidden_ref, next_ref, next_strips_ref, pad_ref, sh_ref, hid_ref,
):
    fill_shifted(x_ref, strips_ref, top_ref, right_ref, left_ref, pad_ref, sh_ref)
    depthwise(sh_ref, kern_ref, hid_ref)
    hidden = hid_ref[...].reshape(S * S, LANES)
    hidden_ref[0] = hidden
    _, _, normed = normalise(hidden, gain_ref[...])
    linear = mm(normed, w_in_ref[...])
    act = 0.5 * linear * (1.0 + jnp.tanh(ROOT * (linear + CUBE * linear * linear * linear)))
    mixed = mm(act.astype(BF), w_out_ref[...])
    current = (x_ref[0].reshape(S * S, LANES).astype(F32) + mixed).astype(BF)
    next_ref[0] = current.reshape(S, S, LANES)
    next_strips_ref[0] = mm(extract_ref[...], current).astype(BF).reshape(4, EDGE, LANES)


def backward_kernel(
    first, x_ref, strips_ref, grad_ref, extra_ref, top_ref, right_ref, left_ref, place_ref, top_t_ref,
    right_t_ref, left_t_ref, kern_ref, gain_ref, w_in_ref, w_in_t_ref, w_out_t_ref,
    base_ref, canon_ref, kg_ref, gg_ref, wi_ref, wo_ref,
    pad_ref, sh_ref, hid_ref, gsh_ref, gh_ref, sum_ref, bl_ref, br_ref,
):
    @pl.when(pl.program_id(0) == 0)
    def _():
        kg_ref[...] = jnp.zeros_like(kg_ref)
        gg_ref[...] = jnp.zeros_like(gg_ref)
        wi_ref[...] = jnp.zeros_like(wi_ref)
        wo_ref[...] = jnp.zeros_like(wo_ref)
        gsh_ref[...] = jnp.zeros_like(gsh_ref)

    fill_shifted(x_ref, strips_ref, top_ref, right_ref, left_ref, pad_ref, sh_ref)
    if first:
        depthwise(sh_ref, kern_ref, hid_ref)
        hidden = hid_ref[...].reshape(S * S, LANES)
        gradient = grad_ref[0].reshape(S * S, LANES).astype(F32)
    else:
        hidden = extra_ref[0][0]
        gradient = grad_ref[0].reshape(S * S, LANES) + mm(
            place_ref[...], extra_ref[1][0].reshape(4 * EDGE, LANES)
        )
    sum_ref[...] = gradient.reshape(S, S, LANES)
    low = gradient.astype(BF)
    gain = gain_ref[...]
    standard, inverse, normed = normalise(hidden, gain)
    linear = mm(normed, w_in_ref[...])
    square = linear * linear
    tanh = jnp.tanh(ROOT * linear * (1.0 + CUBE * square))
    half = 0.5 * (1.0 + tanh)
    act = (linear * half).astype(BF)
    slope = half + linear * (0.5 * ROOT) * (1.0 - tanh * tanh) * (1.0 + (3.0 * CUBE) * square)
    grad_act = mm(low, w_out_t_ref[...])
    grad_linear = (slope * grad_act).astype(BF)
    over_pixels = (((0,), (0,)), ((), ()))
    wo_ref[...] += lax.dot_general(low, act, over_pixels, preferred_element_type=F32)
    wi_ref[...] += lax.dot_general(normed, grad_linear, over_pixels, preferred_element_type=F32)
    grad_normed = mm(grad_linear, w_in_t_ref[...])
    scaled = grad_normed * gain
    gg_ref[...] += jnp.sum((grad_normed * standard).reshape(S * S // 8, 8, LANES), 0)
    grad_hidden = inverse * (
        scaled
        - jnp.mean(scaled, -1, keepdims=True)
        - standard * jnp.mean(scaled * standard, -1, keepdims=True)
    )
    gh_ref[...] = grad_hidden.reshape(S, 2, 8, LANES)

    def column(b, carry):
        gh = gh_ref[...]
        for a in range(KS):
            kg_ref[b * KS + a] += jnp.sum(sh_ref[b, a : a + S] * gh, axis=(0, 1))
        taps = [kern_ref[b * KS + a][None] for a in range(KS)]
        for r in range(S + 2 * PAD):
            total = None
            for a in range(KS):
                if 0 <= r - a < S:
                    term = gh[r - a] * taps[a]
                    total = term if total is None else total + term
            gsh_ref[b, r, 16:32, :] = total.reshape(S, LANES)
        return carry

    lax.fori_loop(0, KS, column, 0)

    def rows(block, carry):
        row = block * 4
        total = gsh_ref[0, pl.ds(PAD + row, 4), 11:43, :]
        for b in range(1, KS):
            total = total + gsh_ref[b, pl.ds(PAD + row, 4), 11 - b : 43 - b, :]
        base_ref[0, pl.ds(row, 4)] = sum_ref[pl.ds(row, 4)] + total[:, 8:24]
        bl_ref[pl.ds(row, 4)] = total[:, 0:8]
        br_ref[pl.ds(row, 4)] = total[:, 24:32]
        return carry

    lax.fori_loop(0, S // 4, rows, 0)

    def outer(start):
        total = gsh_ref[0, start : start + PAD, 19:35, :]
        for b in range(1, KS):
            total = total + gsh_ref[b, start : start + PAD, 19 - b : 35 - b, :]
        return total.reshape(EDGE, LANES).astype(BF)

    canon_ref[0, 0] = mm(top_t_ref[...], outer(0)).astype(BF)
    canon_ref[0, 2] = outer(PAD + S)
    canon_ref[0, 1] = mm(right_t_ref[...], br_ref[...].reshape(S * 8, LANES).astype(BF)).astype(BF)
    canon_ref[0, 3] = mm(left_t_ref[...], bl_ref[...].reshape(S * 8, LANES).astype(BF)).astype(BF)


def whole(shape):
    return pl.BlockSpec(shape, lambda t, off: (0,) * len(shape))


def own_tile(shape, count):
    return pl.BlockSpec((1,) + shape, lambda t, off: (off[0] * count + t,) + (0,) * len(shape))


def each_tile(shape):
    return pl.BlockSpec((1,) + shape, lambda t, off: (t,) + (0,) * len(shape))


def shift_scratch():
    return [
        pltpu.VMEM((S + 2 * PAD, 32, LANES), F32),
        pltpu.VMEM((KS, S + 2 * PAD, 2, 8, LANES), F32),
        pltpu.VMEM((S, 2, 8, LANES), F32),
    ]


PARAMS = pltpu.CompilerParams(vmem_limit_bytes=40 * 1024 * 1024)


def forward_call(offset, count, x, strips, tables, kern, gain, w_in, w_out):
    hidden_units = w_in.shape[1]
    return pl.pallas_call(
        forward_kernel,
        grid_spec=pltpu.PrefetchScalarGridSpec(
            num_scalar_prefetch=1,
            grid=(count,),
            in_specs=[
                own_tile((S, S, LANES), count),
                each_tile((4, EDGE, LANES)),
                whole((EDGE, EDGE)),
                whole((S * 8, EDGE)),
                whole((S * 8, EDGE)),
                whole((4 * EDGE, S * S)),
                whole((KS * KS, 8, LANES)),
                whole((1, LANES)),
                whole((LANES, hidden_units)),
                whole((hidden_units, LANES)),
            ],
            out_specs=[
                each_tile((S * S, LANES)),
                each_tile((S, S, LANES)),
                each_tile((4, EDGE, LANES)),
            ],
            scratch_shapes=shift_scratch(),
        ),
        out_shape=[
            jax.ShapeDtypeStruct((count, S * S, LANES), F32),
            jax.ShapeDtypeStruct((count, S, S, LANES), BF),
            jax.ShapeDtypeStruct((count, 4, EDGE, LANES), BF),
        ],
        compiler_params=PARAMS,
        name="block_forward",
    )(offset, x, strips, *tables, kern, gain, w_in, w_out)


def first_backward(off_ref, x_ref, strips_ref, grad_ref, *rest):
    backward_kernel(True, x_ref, strips_ref, grad_ref, None, *rest)


def second_backward(off_ref, x_ref, strips_ref, grad_ref, hidden_ref, returned_ref, *rest):
    backward_kernel(False, x_ref, strips_ref, grad_ref, (hidden_ref, returned_ref), *rest)


def backward_call(first, offset, count, x, strips, grad, extra, tables, kern, gain, w_in, w_in_t, w_out_t):
    hidden_units = w_in.shape[1]
    x_spec = each_tile((S, S, LANES)) if first else own_tile((S, S, LANES), count)
    grad_spec = own_tile((S, S, LANES), count) if first else each_tile((S, S, LANES))
    extra_specs = [] if first else [each_tile((S * S, LANES)), each_tile((4, EDGE, LANES))]
    return pl.pallas_call(
        first_backward if first else second_backward,
        grid_spec=pltpu.PrefetchScalarGridSpec(
            num_scalar_prefetch=1,
            grid=(count,),
            in_specs=[x_spec, each_tile((4, EDGE, LANES)), grad_spec]
            + extra_specs
            + [whole(table.shape) for table in tables]
            + [
                whole((KS * KS, 8, LANES)),
                whole((1, LANES)),
                whole((LANES, hidden_units)),
                whole((hidden_units, LANES)),
                whole((LANES, hidden_units)),
            ],
            out_specs=[
                each_tile((S, S, LANES)),
                each_tile((4, EDGE, LANES)),
                whole((KS * KS, 8, LANES)),
                whole((8, LANES)),
                whole((LANES, hidden_units)),
                whole((LANES, hidden_units)),
            ],
            scratch_shapes=shift_scratch()
            + [
                pltpu.VMEM((KS, S + 2 * PAD, 48, LANES), F32),
                pltpu.VMEM((S, 2, 8, LANES), F32),
                pltpu.VMEM((S, S, LANES), F32),
                pltpu.VMEM((S, 8, LANES), F32),
                pltpu.VMEM((S, 8, LANES), F32),
            ],
        ),
        out_shape=[
            jax.ShapeDtypeStruct((count, S, S, LANES), F32),
            jax.ShapeDtypeStruct((count, 4, EDGE, LANES), BF),
            jax.ShapeDtypeStruct((KS * KS, 8, LANES), F32),
            jax.ShapeDtypeStruct((8, LANES), F32),
            jax.ShapeDtypeStruct((LANES, hidden_units), F32),
            jax.ShapeDtypeStruct((LANES, hidden_units), F32),
        ],
        compiler_params=PARAMS,
        name="block_backward",
    )(offset, x, strips, grad, *extra, *tables, kern, gain, w_in, w_in_t, w_out_t)


def shifted(value, axis, steps):
    count = lax.axis_size(axis)
    return lax.ppermute(value, axis, [(i, (i + steps) % count) for i in range(count)])


def swapped(value):
    return lax.ppermute(value, "chan", [(0, 1), (1, 0)])


def around(value):
    return shifted(value, "tile", 1), value, shifted(value, "tile", -1)


def exchange(strips):
    count = strips.shape[0]
    rows = strips.reshape(count * 4, EDGE * LANES)
    before, own, after = around(rows)
    mine = jnp.concatenate([before, own, after], 0)
    other = swapped(mine)
    return mine, other


def reduced(value, axis):
    count = lax.axis_size(axis)
    if count & (count - 1):
        return lax.psum(value.astype(BF), axis).astype(F32)
    step = 1
    while step < count:
        got = lax.ppermute(value.astype(BF), axis, [(i, i ^ step) for i in range(count)])
        value = value.astype(BF).astype(F32) + got.astype(F32)
        step *= 2
    return value


def local(activations, cotangent, neighbours, rotations, kernels, gains, w_in, w_out):
    tile_count = activations.shape[0]
    count = tile_count // 2
    chan = lax.axis_index("chan")
    position = lax.axis_index("tile")
    groups = lax.axis_size("tile")
    half_units = w_in.shape[2]
    offset = chan.astype(jnp.int32).reshape(1)

    extract, top, right, left = [jnp.asarray(table, BF) for table in permutation_tables()]
    forward_tables = (top, right, left, extract)
    backward_tables = (top, right, left, extract.T, top.T, right.T, left.T)

    seams = jnp.concatenate([neighbours, rotations], 1)
    seams_all = jnp.stack(around(seams), 0)

    own_first = lax.dynamic_slice_in_dim(activations, chan * count, count, 0)
    start_strips = jnp.einsum(
        "pk,tkc->tpc", extract, own_first.reshape(count, S * S, LANES), preferred_element_type=F32
    ).astype(BF)
    mine0, other0 = exchange(start_strips)

    joined = jnp.stack([w_in[0].T, w_in[1].T, w_out[0], w_out[1]], 0)
    gathered = lax.all_gather(joined, "chan", axis=1, tiled=True)
    in_t = [gathered[0], gathered[1]]
    out_w = [gathered[2], gathered[3]]
    in_w = [value.T for value in in_t]
    out_t = [value.T for value in out_w]
    taps = jnp.broadcast_to(
        kernels.astype(F32).transpose(0, 2, 1, 3).reshape(2, KS * KS, 1, LANES), (2, KS * KS, 8, LANES)
    )

    own_seams = lax.dynamic_slice_in_dim(seams, chan * count, count, 0)
    side = jnp.arange(4, dtype=jnp.int32)
    from_tile = own_seams[:, :4]
    source = (side[None, :] + 2 + own_seams[:, 4:]) % 4
    block_offset = (from_tile // tile_count - position + 1) % groups
    inner = from_tile % tile_count
    is_mine = (inner // count == chan).reshape(-1, 1)
    read_index = ((block_offset * count + inner % count) * 4 + source).reshape(-1)

    def choose(mine, other):
        picked = jnp.where(is_mine, jnp.take(mine, read_index, axis=0), jnp.take(other, read_index, axis=0))
        return picked.reshape(count, 4, EDGE, LANES)

    targets = seams_all[:, :, :4] * 4 + (side[None, None, :] + 2 + seams_all[:, :, 4:]) % 4
    targets_mine = lax.dynamic_slice_in_dim(targets, chan * count, count, 1).reshape(-1)
    targets_other = lax.dynamic_slice_in_dim(targets, (1 - chan) * count, count, 1).reshape(-1)
    slots = (position * tile_count + chan * count) * 4 + jnp.arange(count * 4, dtype=jnp.int32)
    hot_mine = (slots[:, None] == targets_mine[None, :]).astype(BF)
    hot_other = (slots[:, None] == targets_other[None, :]).astype(BF)

    def returned(canon):
        mine, other = exchange(canon)
        total = mm(hot_mine, mine) + mm(hot_other, other)
        return total.astype(BF).reshape(count, 4, EDGE, LANES)

    chosen0 = choose(mine0, other0)
    hidden0, current, strips1 = forward_call(
        offset, count, activations, chosen0, forward_tables, taps[0], gains[0:1], in_w[0], out_w[0]
    )
    chosen1 = choose(*exchange(strips1))
    base1, canon1, *grads1 = backward_call(
        True, offset, count, current, chosen1, cotangent, (), backward_tables,
        taps[1], gains[1:2], in_w[1], in_t[1], out_t[1],
    )

    def split(parts):
        kernel_part, gain_part, in_part, out_part = parts
        small = jnp.concatenate(
            [
                kernel_part.sum(1),
                gain_part.sum(0, keepdims=True),
            ],
            0,
        )
        stacked = jnp.stack([in_part, out_part], 0)

        def half(which):
            piece = lax.dynamic_slice_in_dim(stacked, which * half_units, half_units, 2)
            return jnp.concatenate([piece.reshape(-1, LANES), small], 0)

        total = half(chan) + swapped(half(1 - chan).astype(BF)).astype(F32)
        total = reduced(total, "tile")
        size = LANES * half_units // LANES
        kernel_sum = total[2 * size : 2 * size + KS * KS].reshape(KS, KS, LANES).transpose(1, 0, 2)
        return (
            kernel_sum,
            total[2 * size + KS * KS],
            total[:size].reshape(LANES, half_units),
            total[size : 2 * size].reshape(LANES, half_units).T,
        )

    sums1 = split(grads1)
    returned1 = returned(canon1)
    base0, canon0, *grads0 = backward_call(
        False, offset, count, activations, chosen0, base1, (hidden0, returned1), backward_tables,
        taps[0], gains[0:1], in_w[0], in_t[0], out_t[0],
    )
    returned0 = returned(canon0)
    sums0 = split(grads0)
    placed = jnp.einsum(
        "kp,tpc->tkc", extract.T, returned0.reshape(count, 4 * EDGE, LANES), preferred_element_type=F32
    )
    own_out = (base0 + placed.reshape(base0.shape)).astype(BF)
    input_grads = lax.all_gather(own_out, "chan", axis=0, tiled=True)
    stacked = [jnp.stack([a, b], 0) for a, b in zip(sums0, sums1)]
    return (input_grads, *stacked)


def solution(mesh):
    placed = (
        P(("parts", "tile"), None, None, None),
        P(("parts", "tile"), None, None, None),
        P("tile", None),
        P("tile", None),
        P(),
        P(),
        P(None, None, "chan"),
        P(None, "chan", None),
    )
    return jax.shard_map(
        local,
        mesh=mesh,
        in_specs=placed,
        out_specs=(
            P(("parts", "tile"), None, None, None),
            P("parts", None, None, None),
            P("parts", None),
            P("parts", None, "chan"),
            P("parts", "chan", None),
        ),
        check_vma=False,
    )
```

time: 878 us -> 308 us (0.35); the launches traced: 868 us -> 308 us
  other arithmetic: 392 us -> 12.8 us
  local copies, waits for them, and re-layouts: 129 us -> 40.4 us
  Pallas kernels: 0 us -> 86.7 us
  waiting for transfers between devices: 186 us -> 110 us
  blocking collectives: 76 us -> 2.76 us
  matrix products: 46.9 us -> 7.99 us
  starting transfers between devices: 20.4 us -> 32 us
    reduce_sum x14 -> x4, other arithmetic: 149 us -> 1.08 us  [the longest x2 1.04 us: split(): kernel_part.sum(1)]
    add x8 -> x6, other arithmetic: 111 us -> 1.14 us  [the longest x2 0.97 us: reduced(): value = value.astype(BF).astype(F32) + got.astype(F32)]
    pallas_call x0 -> x3, Pallas kernels: none -> 86.7 us  [the longest x2 66.6 us: backward_call(): pl.pallas_call(first_backward if first else second_backward, grid_spec=pl...]
    psum x1 -> x0, blocking collectives: 76 us -> none  [local(): lax.psum(block_terms[0].astype(jnp.bfloat16), 'tile').astype(jnp.float32)]
    mul x4 -> x0, other arithmetic: 66.3 us -> none  [depthwise_back(): spread = grad_hidden * kernel[kernel_row, kernel_column].astype(jnp.float32)]
    psum x4 -> x0, waiting for transfers between devices: 53.9 us -> none  [the longest x2 24.6 us: local(): lax.psum(normed_partial.astype(jnp.bfloat16), 'chan').astype(jnp.float32)]
    rev x15 -> x0, local copies, waits for them, and re-layouts: 42.8 us -> none  [the longest x6 24.5 us: return_rims(): running = running + jnp.rot90(placed, -quarter, axes=(1, 2))]
    dot_general x13 -> x6, matrix products: 46.9 us -> 7.99 us  [the longest x4 6.35 us: mm(): return jnp.dot(a, b, preferred_element_type=F32)]
  transfers between devices with their start and end apart: 12 -> 23, of which waited for: 8 -> 15; matrix products, arithmetic and copies ran while one was open for 5% -> 11% of each run, Pallas kernels for 0% -> 0%
where the time goes in v1:
time: 308 us
  waiting for transfers between devices  110 us (36%)
  Pallas kernels  86.7 us (28%)
  local copies, waits for them, and re-layouts  40.4 us (13%)
  starting transfers between devices  32 us (10%)
  between operations  15.2 us (5%)
  other arithmetic  12.8 us (4%)
  matrix products  7.99 us (3%)
    ppermute x10, waiting for transfers between devices, shifted(): lax.ppermute(value, axis, [(i, (i + steps) % count) for i in range(count)])  94.4 us
    pallas_call x2, Pallas kernels, backward_call(): pl.pallas_call(first_backward if first else second_backward, grid_spec=pl...  66.6 us
    ppermute x10, starting transfers between devices, shifted(): lax.ppermute(value, axis, [(i, (i + steps) % count) for i in range(count)])  26 us
    pallas_call x1, Pallas kernels, forward_call(): pl.pallas_call(forward_kernel, grid_spec=pltpu.PrefetchScalarGridSpec(num...  20.1 us
    unnamed x142, local copies, waits for them, and re-layouts  17 us
    ppermute x6, waiting for transfers between devices, reduced(): lax.ppermute(value.astype(BF), axis, [(i, i ^ step) for i in range(count)])  13.3 us
    gather x2, local copies, waits for them, and re-layouts, choose(): jnp.take(other, read_index, axis=0)  7.27 us
    dot_general x4, matrix products, mm(): return jnp.dot(a, b, preferred_element_type=F32)  6.35 us
  transfers between devices with their start and end apart: 23, of which 15 were waited for; matrix products, arithmetic and copies ran while one was open for 11% of the time, Pallas kernels for 0%

profile of v1, /device:TPU:0, one launch (start us, length us, event | category | flops | bytes accessed | tf_op | source)
XLA Modules:
  0.0 307.9 jit_solution(5085603502375616946)
XLA Ops:
  10.0 3.0 collective-permute-start
  13.1 3.1 %collective-permute-start.1 = (bf16[48,6144]{1,0:T(8,128)(2,1)S(1)}, bf16[48,6144]{1,0:T(8,128)(2,1)S(1)}, u32[]{:S(2)}, u32[]{:S(2)}) collective-permute-start(bf16[48,6144]{1,0:T(8,128)(2,1)S(1)} %reshape.102), channel_id=1, source_target_pairs={{0,14},{2,0},{4,2},{6,4},{8,6},{10,8},{12,10},{14,12},{1,15},{3,1}... | collective-permute-start | bytes 1769480 | tf_op jit(solution)/shard_map/ppermute | solution.py:305
  17.5 20.8 %collective-permute-done = bf16[48,6144]{1,0:T(8,128)(2,1)} collective-permute-done((bf16[48,6144]{1,0:T(8,128)(2,1)S(1)}, bf16[48,6144]{1,0:T(8,128)(2,1)}, u32[]{:S(2)}, u32[]{:S(2)}) %collective-permute-start) | collective-permute-done | bytes 589856 | tf_op jit(solution)/shard_map/ppermute | solution.py:305
  41.9 2.8 all_gather.6
  47.2 3.2 %gather_fusion.1 = bf16[48,6144]{1,0:T(8,128)(2,1)S(1)} fusion(bf16[144,6144]{1,0:T(8,128)(2,1)} %collective-permute-done.2, s32[1024]{0:T(1024)S(1)} %pad_clamp_fusion), kind=kCustom, calls=%fused_computation.1.clone | custom fusion | bytes 1179840 | tf_op jit(solution)/shard_map/jit(_take)/gather | solution.py:379
  51.8 20.1 %block_forward.1 = (f32[12,256,128]{2,1,0:T(8,128)S(1)}, bf16[12,16,16,128]{3,2,1,0:T(8,128)(2,1)S(1)}, bf16[12,4,48,128]{3,2,1,0:T(8,128)(2,1)S(1)}) custom-call(s32[1]{0:T(128)} %bitcast.off_ref, bf16[24,16,16,128]{3,2,1,0:T(8,128)(2,1)S(1)} %copy-done, bf16[12,4,48,128]{3,2,1,0:T(8,128)(2,1)S(1)} %bitcast.108, bf16[48,48]{1,0:T(8,128)(2,1)S(1)} %copy-done.20, ...), custom_call_target="tpu_custom_call" | custom-call | tf_op jit(solution)/shard_map/block_forward/pallas_call | solution.py:211
  73.7 3.2 %collective-permute-start.4 = (bf16[48,6144]{1,0:T(8,128)(2,1)S(1)}, bf16[48,6144]{1,0:T(8,128)(2,1)S(1)}, u32[]{:S(2)}, u32[]{:S(2)}) collective-permute-start(bf16[48,6144]{1,0:T(8,128)(2,1)S(1)} %bitcast.131), channel_id=1, source_target_pairs={{0,14},{2,0},{4,2},{6,4},{8,6},{10,8},{12,10},{14,12},{1,15},{3,1}... | collective-permute-start | bytes 1769480 | tf_op jit(solution)/shard_map/ppermute | solution.py:305
  76.9 22.4 %collective-permute-done.3 = bf16[48,6144]{1,0:T(8,128)(2,1)S(1)} collective-permute-done((bf16[48,6144]{1,0:T(8,128)(2,1)S(1)}, bf16[48,6144]{1,0:T(8,128)(2,1)S(1)}, u32[]{:S(2)}, u32[]{:S(2)}) %collective-permute-start.3) | collective-permute-done | bytes 589856 | tf_op jit(solution)/shard_map/ppermute | solution.py:305
  103.1 4.1 %gather_fusion.2 = bf16[48,6144]{1,0:T(8,128)(2,1)} fusion(bf16[144,6144]{1,0:T(8,128)(2,1)} %constant_dynamic-update-slice_fusion.3, s32[1024]{0:T(1024)} %copy-done.52), kind=kCustom, calls=%fused_computation.2.clone | custom fusion | bytes 1179840 | tf_op jit(solution)/shard_map/jit(_take)/gather | solution.py:379
  107.2 4.1 %gather_fusion.3 = bf16[48,6144]{1,0:T(8,128)(2,1)} fusion(bf16[144,6144]{1,0:T(8,128)(2,1)} %collective-permute-done.5, s32[1024]{0:T(1024)} %copy-done.52), kind=kCustom, calls=%fused_computation.3.clone | custom fusion | bytes 1179840 | tf_op jit(solution)/shard_map/jit(_take)/gather | solution.py:379
  113.2 37.9 %block_backward.2 = (f32[12,16,16,128]{3,2,1,0:T(8,128)S(1)}, bf16[12,4,48,128]{3,2,1,0:T(8,128)(2,1)S(1)}, f32[49,8,128]{2,1,0:T(8,128)S(1)}, f32[8,128]{1,0:T(...) custom-call(s32[1]{0:T(128)} %bitcast.off_ref, bf16[12,16,16,128]{3,2,1,0:T(8,128)(2,1)S(1)} %get-tuple-element.21.x_ref, ...), custom_call_target="tpu_custom_call" | custom-call | tf_op jit(solution)/shard_map/block_backward/pallas_call | solution.py:258
  151.4 2.1 collective-permute-start.8
  153.5 3.1 %collective-permute-start.9 = (bf16[48,6144]{1,0:T(8,128)(2,1)S(1)}, bf16[48,6144]{1,0:T(8,128)(2,1)S(1)}, u32[]{:S(2)}, u32[]{:S(2)}) collective-permute-start(bf16[48,6144]{1,0:T(8,128)(2,1)S(1)} %bitcast.133), channel_id=1, source_target_pairs={{0,14},{2,0},{4,2},{6,4},{8,6},{10,8},{12,10},{14,12},{1,15},{3,1}... | collective-permute-start | bytes 1769480 | tf_op jit(solution)/shard_map/ppermute | solution.py:305
  156.6 22.8 %collective-permute-done.8 = bf16[48,6144]{1,0:T(8,128)(2,1)S(1)} collective-permute-done((bf16[48,6144]{1,0:T(8,128)(2,1)S(1)}, bf16[48,6144]{1,0:T(8,128)(2,1)S(1)}, u32[]{:S(2)}, u32[]{:S(2)}) %collective-permute-start.8) | collective-permute-done | bytes 589856 | tf_op jit(solution)/shard_map/ppermute | solution.py:305
  182.5 5.1 %collective-permute-start.7 = (s32[24,8]{0,1:T(8,128)S(1)}, s32[24,8]{0,1:T(8,128)S(1)}, u32[]{:S(2)}, u32[]{:S(2)}) collective-permute-start(s32[24,8]{0,1:T(8,128)S(1)} %copy-done.50), channel_id=1, source_target_pairs={{0,14},{2,0},{4,2},{6,4},{8,6},{10,8},{12,10},{14,12},{1,15},{3,1}... | collective-permute-start | bytes 2312 | tf_op jit(solution)/shard_map/ppermute | solution.py:305
  188.9 5.0 %collective-permute-done.6 = s32[24,8]{0,1:T(8,128)S(1)} collective-permute-done((s32[24,8]{0,1:T(8,128)S(1)}, s32[24,8]{0,1:T(8,128)S(1)}, u32[]{:S(2)}, u32[]{:S(2)}) %collective-permute-start.6) | collective-permute-done | bytes 800 | tf_op jit(solution)/shard_map/ppermute | solution.py:305
  194.5 1.9 fusion.16
  196.5 2.1 fusion.3
  198.9 28.7 %block_backward.3 = (f32[12,16,16,128]{3,2,1,0:T(8,128)S(1)}, bf16[12,4,48,128]{3,2,1,0:T(8,128)(2,1)S(1)}, f32[49,8,128]{2,1,0:T(8,128)S(1)}, f32[8,128]{1,0:T(...) custom-call(s32[1]{0:T(128)} %bitcast.off_ref, bf16[24,16,16,128]{3,2,1,0:T(8,128)(2,1)S(1)} %copy-done, ...), custom_call_target="tpu_custom_call" | custom-call | tf_op jit(solution)/shard_map/block_backward/pallas_call | solution.py:258
  233.7 4.7 %collective-permute-start.12 = (bf16[48,6144]{1,0:T(8,128)(2,1)S(1)}, bf16[48,6144]{1,0:T(8,128)(2,1)S(1)}, u32[]{:S(2)}, u32[]{:S(2)}) collective-permute-start(bf16[48,6144]{1,0:T(8,128)(2,1)S(1)} %bitcast.129), channel_id=1, source_target_pairs={{0,14},{2,0},{4,2},{6,4},{8,6},{10,8},{12,10},{14,12},{1,15},{3,1}... | collective-permute-start | bytes 1769480 | tf_op jit(solution)/shard_map/ppermute | solution.py:305
  238.5 17.3 %collective-permute-done.11 = bf16[48,6144]{1,0:T(8,128)(2,1)S(1)} collective-permute-done((bf16[48,6144]{1,0:T(8,128)(2,1)S(1)}, bf16[48,6144]{1,0:T(8,128)(2,1)S(1)}, u32[]{:S(2)}, u32[]{:S(2)}) %collective-permute-start.11) | collective-permute-done | bytes 589856 | tf_op jit(solution)/shard_map/ppermute | solution.py:305
  257.5 3.1 %collective-permute-done.12 = bf16[48,6144]{1,0:T(8,128)(2,1)S(1)} collective-permute-done((bf16[48,6144]{1,0:T(8,128)(2,1)S(1)}, bf16[48,6144]{1,0:T(8,128)(2,1)S(1)}, u32[]{:S(2)}, u32[]{:S(2)}) %collective-permute-start.12) | collective-permute-done | bytes 589856 | tf_op jit(solution)/shard_map/ppermute | solution.py:305
  263.8 2.2 collective-permute-done.18
  267.0 2.1 collective-permute-start.15
  269.1 4.5 %collective-permute-done.19 = bf16[562,128]{1,0:T(8,128)(2,1)S(1)} collective-permute-done((bf16[562,128]{1,0:T(8,128)(2,1)S(1)}, bf16[562,128]{1,0:T(8,128)(2,1)S(1)}, u32[]{:S(2)}, u32[]{:S(2)}) %collective-permute-start.19) | collective-permute-done | bytes 143904 | tf_op jit(solution)/shard_map/ppermute | solution.py:331
  273.7 2.2 collective-permute-done.15
  276.1 3.7 %collective-permute-done.20 = bf16[562,128]{1,0:T(8,128)(2,1)S(1)} collective-permute-done((bf16[562,128]{1,0:T(8,128)(2,1)S(1)}, bf16[562,128]{1,0:T(8,128)(2,1)S(1)}, u32[]{:S(2)}, u32[]{:S(2)}) %collective-permute-start.20) | collective-permute-done | bytes 143904 | tf_op jit(solution)/shard_map/ppermute | solution.py:331
  280.4 1.9 fusion.1
  284.7 2.5 add_convert_fusion
  288.1 3.0 collective-permute-start.17
  292.1 2.8 collective-permute-done.17
  298.1 3.0 copy.100
  (260 shorter events, 44.3 us)
Async XLA Ops:
  7.2 290.9 %all-gather.2.cloned.1.call-start = ((), (), s32[]{:S(2)}) async-start(), calls=%async_computation | async-start | bytes 2359296 | tf_op jit(solution)/shard_map/all_gather | solution.py:442
  10.0 28.2 %collective-permute-start = (bf16[48,6144]{1,0:T(8,128)(2,1)S(1)}, bf16[48,6144]{1,0:T(8,128)(2,1)}, u32[]{:S(2)}, u32[]{:S(2)}) collective-permute-start(bf16[48,6144]{1,0:T(8,128)(2,1)S(1)} %reshape.102), channel_id=1, source_target_pairs={{0,2},{2,4},{4,6},{6,8},{8,10},{10,12},{12,14},{14,0},{1,3},{3,5},... | collective-permute-start | bytes 1769480 | tf_op jit(solution)/shard_map/ppermute | solution.py:305
  13.1 27.4 %collective-permute-start.1 = (bf16[48,6144]{1,0:T(8,128)(2,1)S(1)}, bf16[48,6144]{1,0:T(8,128)(2,1)S(1)}, u32[]{:S(2)}, u32[]{:S(2)}) collective-permute-start(bf16[48,6144]{1,0:T(8,128)(2,1)S(1)} %reshape.102), channel_id=1, source_target_pairs={{0,14},{2,0},{4,2},{6,4},{8,6},{10,8},{12,10},{14,12},{1,15},{3,1}... | collective-permute-start | bytes 1769480 | tf_op jit(solution)/shard_map/ppermute | solution.py:305
  40.5 6.6 %collective-permute-start.2 = (bf16[144,6144]{1,0:T(8,128)(2,1)S(1)}, bf16[144,6144]{1,0:T(8,128)(2,1)}, u32[]{:S(2)}, u32[]{:S(2)}) collective-permute-start(bf16[144,6144]{1,0:T(8,128)(2,1)S(1)} %constant_dynamic-update-slice_fusion), channel_id=1, source_target_pairs={{0,1},{1,0},{2,3},{3,2},{4,5},{5,4},{6,7},{7,6},{8,9},{9,8},{10,11... | collective-permute-start | bytes 5308424 | tf_op jit(solution)/shard_map/ppermute | solution.py:309
  72.1 30.2 %copy-start.47 = (f32[1,7,7,128]{3,0,1,2:T(1,128)S(1)}, f32[1,7,7,128]{3,0,1,2:T(1,128)}, u32[]{:S(2)}) copy-start(f32[1,7,7,128]{3,0,1,2:T(1,128)} %get-tuple-element.64) | copy-start | bytes 75268
  72.1 30.2 %copy-start.43 = (bf16[512,128]{0,1:T(8,128)(2,1)S(1)}, bf16[512,128]{0,1:T(8,128)(2,1)}, u32[]{:S(2)}) copy-start(bf16[512,128]{0,1:T(8,128)(2,1)} %get-tuple-element.55) | copy-start | bytes 393220
  72.1 27.1 %collective-permute-start.3 = (bf16[48,6144]{1,0:T(8,128)(2,1)S(1)}, bf16[48,6144]{1,0:T(8,128)(2,1)S(1)}, u32[]{:S(2)}, u32[]{:S(2)}) collective-permute-start(bf16[48,6144]{1,0:T(8,128)(2,1)S(1)} %bitcast.130), channel_id=1, source_target_pairs={{0,2},{2,4},{4,6},{6,8},{8,10},{10,12},{12,14},{14,0},{1,3},{3,5},... | collective-permute-start | bytes 1769480 | tf_op jit(solution)/shard_map/ppermute | solution.py:305
  73.7 27.7 %collective-permute-start.4 = (bf16[48,6144]{1,0:T(8,128)(2,1)S(1)}, bf16[48,6144]{1,0:T(8,128)(2,1)S(1)}, u32[]{:S(2)}, u32[]{:S(2)}) collective-permute-start(bf16[48,6144]{1,0:T(8,128)(2,1)S(1)} %bitcast.131), channel_id=1, source_target_pairs={{0,14},{2,0},{4,2},{6,4},{8,6},{10,8},{12,10},{14,12},{1,15},{3,1}... | collective-permute-start | bytes 1769480 | tf_op jit(solution)/shard_map/ppermute | solution.py:305
  102.3 4.9 %collective-permute-start.5 = (bf16[144,6144]{1,0:T(8,128)(2,1)}, bf16[144,6144]{1,0:T(8,128)(2,1)}, u32[]{:S(2)}, u32[]{:S(2)}) collective-permute-start(bf16[144,6144]{1,0:T(8,128)(2,1)} %constant_dynamic-update-slice_fusion.3), channel_id=1, source_target_pairs={{0,1},{1,0},{2,3},{3,2},{4,5},{5,4},{6,7},{7,6},{8,9},{9,8},{10,11... | collective-permute-start | bytes 5308424 | tf_op jit(solution)/shard_map/ppermute | solution.py:309
  151.2 30.0 %copy-start.6 = (f32[12,16,16,128]{3,2,1,0:T(8,128)}, f32[12,16,16,128]{3,2,1,0:T(8,128)S(1)}, u32[]{:S(2)}) copy-start(f32[12,16,16,128]{3,2,1,0:T(8,128)S(1)} %get-tuple-element.23.grad_ref) | copy-start | bytes 4718596
  151.2 30.0 %copy-start.8 = (f32[128,512]{1,0:T(8,128)}, f32[128,512]{1,0:T(8,128)S(1)}, u32[]{:S(2)}) copy-start(f32[128,512]{1,0:T(8,128)S(1)} %get-tuple-element.33) | copy-start | bytes 786436
  151.4 31.1 %copy-start.50 = (s32[24,8]{0,1:T(8,128)S(1)}, s32[24,8]{0,1:T(8,128)}, u32[]{:S(2)}) copy-start(s32[24,8]{0,1:T(8,128)} %copy-done.49) | copy-start | bytes 2308
  151.4 36.2 %copy-start.42 = (bf16[512,128]{0,1:T(8,128)(2,1)S(1)}, bf16[512,128]{0,1:T(8,128)(2,1)}, u32[]{:S(2)}) copy-start(bf16[512,128]{0,1:T(8,128)(2,1)} %get-tuple-element.57) | copy-start | bytes 393220
  151.4 42.5 %copy-start.51 = (s32[1,24,8]{1,2,0:T(8,128)S(1)}, s32[1,24,8]{1,2,0:T(8,128)}, u32[]{:S(2)}) copy-start(s32[1,24,8]{1,2,0:T(8,128)} %get-tuple-element.68) | copy-start | bytes 2308
  151.4 42.5 %copy-start.58 = (s32[4]{0:T(128)S(1)}, s32[4]{0:T(128)}, u32[]{:S(2)}) copy-start(s32[4]{0:T(128)} %copy-done.57) | copy-start | bytes 52
  151.4 28.0 %collective-permute-start.8 = (bf16[48,6144]{1,0:T(8,128)(2,1)S(1)}, bf16[48,6144]{1,0:T(8,128)(2,1)S(1)}, u32[]{:S(2)}, u32[]{:S(2)}) collective-permute-start(bf16[48,6144]{1,0:T(8,128)(2,1)S(1)} %bitcast.132), channel_id=1, source_target_pairs={{0,2},{2,4},{4,6},{6,8},{8,10},{10,12},{12,14},{14,0},{1,3},{3,5},... | collective-permute-start | bytes 1769480 | tf_op jit(solution)/shard_map/ppermute | solution.py:305
  153.5 28.1 %collective-permute-start.9 = (bf16[48,6144]{1,0:T(8,128)(2,1)S(1)}, bf16[48,6144]{1,0:T(8,128)(2,1)S(1)}, u32[]{:S(2)}, u32[]{:S(2)}) collective-permute-start(bf16[48,6144]{1,0:T(8,128)(2,1)S(1)} %bitcast.133), channel_id=1, source_target_pairs={{0,14},{2,0},{4,2},{6,4},{8,6},{10,8},{12,10},{14,12},{1,15},{3,1}... | collective-permute-start | bytes 1769480 | tf_op jit(solution)/shard_map/ppermute | solution.py:305
  182.5 12.0 %collective-permute-start.10 = (bf16[144,6144]{1,0:T(8,128)(2,1)}, bf16[144,6144]{1,0:T(8,128)(2,1)}, u32[]{:S(2)}, u32[]{:S(2)}) collective-permute-start(bf16[144,6144]{1,0:T(8,128)(2,1)} %constant_dynamic-update-slice_fusion.6), channel_id=1, source_target_pairs={{0,1},{1,0},{2,3},{3,2},{4,5},{5,4},{6,7},{7,6},{8,9},{9,8},{10,11... | collective-permute-start | bytes 5308424 | tf_op jit(solution)/shard_map/ppermute | solution.py:309
  182.5 6.4 %collective-permute-start.7 = (s32[24,8]{0,1:T(8,128)S(1)}, s32[24,8]{0,1:T(8,128)S(1)}, u32[]{:S(2)}, u32[]{:S(2)}) collective-permute-start(s32[24,8]{0,1:T(8,128)S(1)} %copy-done.50), channel_id=1, source_target_pairs={{0,14},{2,0},{4,2},{6,4},{8,6},{10,8},{12,10},{14,12},{1,15},{3,1}... | collective-permute-start | bytes 2312 | tf_op jit(solution)/shard_map/ppermute | solution.py:305
  187.6 6.3 %collective-permute-start.6 = (s32[24,8]{0,1:T(8,128)S(1)}, s32[24,8]{0,1:T(8,128)S(1)}, u32[]{:S(2)}, u32[]{:S(2)}) collective-permute-start(s32[24,8]{0,1:T(8,128)S(1)} %copy-done.50), channel_id=1, source_target_pairs={{0,2},{2,4},{4,6},{6,8},{8,10},{10,12},{12,14},{14,0},{1,3},{3,5},... | collective-permute-start | bytes 2312 | tf_op jit(solution)/shard_map/ppermute | solution.py:305
  198.9 32.1 %copy-start.38 = (f32[8,128]{1,0:T(8,128)S(1)}, f32[8,128]{1,0:T(8,128)}, u32[]{:S(2)}) copy-start(f32[8,128]{1,0:T(8,128)} %copy-done.37) | copy-start | bytes 12292
  230.9 24.8 %collective-permute-start.11 = (bf16[48,6144]{1,0:T(8,128)(2,1)S(1)}, bf16[48,6144]{1,0:T(8,128)(2,1)S(1)}, u32[]{:S(2)}, u32[]{:S(2)}) collective-permute-start(bf16[48,6144]{1,0:T(8,128)(2,1)S(1)} %bitcast.128), channel_id=1, source_target_pairs={{0,2},{2,4},{4,6},{6,8},{8,10},{10,12},{12,14},{14,0},{1,3},{3,5},... | collective-permute-start | bytes 1769480 | tf_op jit(solution)/shard_map/ppermute | solution.py:305
  233.7 26.9 %collective-permute-start.12 = (bf16[48,6144]{1,0:T(8,128)(2,1)S(1)}, bf16[48,6144]{1,0:T(8,128)(2,1)S(1)}, u32[]{:S(2)}, u32[]{:S(2)}) collective-permute-start(bf16[48,6144]{1,0:T(8,128)(2,1)S(1)} %bitcast.129), channel_id=1, source_target_pairs={{0,14},{2,0},{4,2},{6,4},{8,6},{10,8},{12,10},{14,12},{1,15},{3,1}... | collective-permute-start | bytes 1769480 | tf_op jit(solution)/shard_map/ppermute | solution.py:305
  261.5 18.4 %collective-permute-start.13 = (bf16[144,6144]{1,0:T(8,128)(2,1)}, bf16[144,6144]{1,0:T(8,128)(2,1)S(1)}, u32[]{:S(2)}, u32[]{:S(2)}) collective-permute-start(bf16[144,6144]{1,0:T(8,128)(2,1)} %constant_dynamic-update-slice_fusion.9), channel_id=1, source_target_pairs={{0,1},{1,0},{2,3},{3,2},{4,5},{5,4},{6,7},{7,6},{8,9},{9,8},{10,11... | collective-permute-start | bytes 5308424 | tf_op jit(solution)/shard_map/ppermute | solution.py:309
  263.0 3.0 collective-permute-start.18
  263.7 3.3 %collective-permute-start.14 = (bf16[562,128]{1,0:T(8,128)(2,1)S(1)}, bf16[562,128]{1,0:T(8,128)(2,1)S(1)}, u32[]{:S(2)}, u32[]{:S(2)}) collective-permute-start(bf16[562,128]{1,0:T(8,128)(2,1)S(1)} %pad_maximum_fusion.3), channel_id=1, source_target_pairs={{0,1},{1,0},{2,3},{3,2},{4,5},{5,4},{6,7},{7,6},{8,9},{9,8},{10,11... | collective-permute-start | bytes 431624 | tf_op jit(solution)/shard_map/ppermute | solution.py:309
  266.9 6.7 %collective-permute-start.19 = (bf16[562,128]{1,0:T(8,128)(2,1)S(1)}, bf16[562,128]{1,0:T(8,128)(2,1)S(1)}, u32[]{:S(2)}, u32[]{:S(2)}) collective-permute-start(bf16[562,128]{1,0:T(8,128)(2,1)S(1)} %fusion.7), channel_id=1, source_target_pairs={{0,2},{2,0},{4,6},{6,4},{8,10},{10,8},{12,14},{14,12},{1,3},{3,1},... | collective-permute-start | bytes 431624 | tf_op jit(solution)/shard_map/ppermute | solution.py:331
  267.0 8.9 %collective-permute-start.15 = (bf16[562,128]{1,0:T(8,128)(2,1)S(1)}, bf16[562,128]{1,0:T(8,128)(2,1)S(1)}, u32[]{:S(2)}, u32[]{:S(2)}) collective-permute-start(bf16[562,128]{1,0:T(8,128)(2,1)S(1)} %fusion.6), channel_id=1, source_target_pairs={{0,2},{2,0},{4,6},{6,4},{8,10},{10,8},{12,14},{14,12},{1,3},{3,1},... | collective-permute-start | bytes 431624 | tf_op jit(solution)/shard_map/ppermute | solution.py:331
  273.7 6.1 %collective-permute-start.20 = (bf16[562,128]{1,0:T(8,128)(2,1)S(1)}, bf16[562,128]{1,0:T(8,128)(2,1)S(1)}, u32[]{:S(2)}, u32[]{:S(2)}) collective-permute-start(bf16[562,128]{1,0:T(8,128)(2,1)S(1)} %add_convert_fusion.2), channel_id=1, source_target_pairs={{0,4},{2,6},{4,0},{6,2},{8,12},{10,14},{12,8},{14,10},{1,5},{3,7},... | collective-permute-start | bytes 431624 | tf_op jit(solution)/shard_map/ppermute | solution.py:331
  276.0 11.2 %collective-permute-start.16 = (bf16[562,128]{1,0:T(8,128)(2,1)S(1)}, bf16[562,128]{1,0:T(8,128)(2,1)}, u32[]{:S(2)}, u32[]{:S(2)}) collective-permute-start(bf16[562,128]{1,0:T(8,128)(2,1)S(1)} %add_convert_fusion.4), channel_id=1, source_target_pairs={{0,4},{2,6},{4,0},{6,2},{8,12},{10,14},{12,8},{14,10},{1,5},{3,7},... | collective-permute-start | bytes 431624 | tf_op jit(solution)/shard_map/ppermute | solution.py:331
  279.8 11.3 %collective-permute-start.21 = (bf16[562,128]{1,0:T(8,128)(2,1)S(1)}, bf16[562,128]{1,0:T(8,128)(2,1)}, u32[]{:S(2)}, u32[]{:S(2)}) collective-permute-start(bf16[562,128]{1,0:T(8,128)(2,1)S(1)} %add_convert_fusion.1), channel_id=1, source_target_pairs={{0,8},{2,10},{4,12},{6,14},{8,0},{10,2},{12,4},{14,6},{1,9},{3,11}... | collective-permute-start | bytes 431624 | tf_op jit(solution)/shard_map/ppermute | solution.py:331
  288.1 6.8 %collective-permute-start.17 = (bf16[562,128]{1,0:T(8,128)(2,1)S(1)}, bf16[562,128]{1,0:T(8,128)(2,1)S(1)}, u32[]{:S(2)}, u32[]{:S(2)}) collective-permute-start(bf16[562,128]{1,0:T(8,128)(2,1)S(1)} %add_convert_fusion.3), channel_id=1, source_target_pairs={{0,8},{2,10},{4,12},{6,14},{8,0},{10,2},{12,4},{14,6},{1,9},{3,11}... | collective-permute-start | bytes 431624 | tf_op jit(solution)/shard_map/ppermute | solution.py:331
  (53 other events, 370.7 us)
Sparse Core Ops, SparseCore 0:
  287.3 9.3 all-gather.1

commit v2 on v1

--- a/solution.py
+++ b/solution.py
@@ -313,13 +313,22 @@
     return shifted(value, "tile", 1), value, shifted(value, "tile", -1)
 
 
-def exchange(strips):
-    count = strips.shape[0]
-    rows = strips.reshape(count * 4, EDGE * LANES)
-    before, own, after = around(rows)
-    mine = jnp.concatenate([before, own, after], 0)
-    other = swapped(mine)
-    return mine, other
+def ranked(mask):
+    return jnp.cumsum(mask.astype(jnp.int32)) - 1
+
+
+def picked(mask, values, first, width, empty):
+    wanted = first + jnp.arange(width, dtype=jnp.int32)
+    select = mask[None, :] & (ranked(mask)[None, :] == wanted[:, None])
+    return jnp.max(jnp.where(select, values[None, :], empty), 1)
+
+
+def in_rounds(rounds, body, state):
+    return lax.while_loop(
+        lambda carry: carry[0] < rounds,
+        lambda carry: (carry[0] + 1, body(carry[0], carry[1])),
+        (jnp.int32(1), state),
+    )[1]
 
 
 def reduced(value, axis):
@@ -348,13 +357,92 @@
     backward_tables = (top, right, left, extract.T, top.T, right.T, left.T)
 
     seams = jnp.concatenate([neighbours, rotations], 1)
-    seams_all = jnp.stack(around(seams), 0)
-
-    own_first = lax.dynamic_slice_in_dim(activations, chan * count, count, 0)
-    start_strips = jnp.einsum(
-        "pk,tkc->tpc", extract, own_first.reshape(count, S * S, LANES), preferred_element_type=F32
-    ).astype(BF)
-    mine0, other0 = exchange(start_strips)
+    side = jnp.arange(4, dtype=jnp.int32)
+
+    def sides_of(block_seams):
+        part = lax.dynamic_slice_in_dim(block_seams, chan * count, count, 0)
+        source = (side[None, :] + 2 + part[:, 4:]) % 4
+        owner = part[:, :4] // tile_count
+        slot = (part[:, :4] % tile_count) * 4 + source
+        return owner.reshape(-1), slot.reshape(-1)
+
+    def mine_first(slot):
+        return slot % (count * 4) + jnp.where(slot // (count * 4) == chan, 0, count * 4)
+
+    seams_before, _, seams_after = around(seams)
+    owner, slot = sides_of(seams)
+    owner_before, slot_before = sides_of(seams_before)
+    owner_after, slot_after = sides_of(seams_after)
+    to_before = owner == (position - 1) % groups
+    to_after = owner == (position + 1) % groups
+    within = owner == position
+    from_before = owner_before == position
+    from_after = owner_after == position
+    most = jnp.maximum(jnp.sum(to_before.astype(jnp.int32)), jnp.sum(to_after.astype(jnp.int32)))
+    rounds = (lax.pmax(most, ("parts", "tile", "chan")) + count - 1) // count
+
+    strips0 = jnp.einsum(
+        "pk,tkc->tpc", extract, activations.reshape(tile_count, S * S, LANES), preferred_element_type=F32
+    ).astype(BF).reshape(tile_count * 4, EDGE * LANES)
+
+    def fetch(full, place):
+        def ask(index):
+            for_after = picked(from_after, place(slot_after), index * count, count, 0)
+            for_before = picked(from_before, place(slot_before), index * count, count, 0)
+            return (
+                shifted(jnp.take(full, for_after, axis=0), "tile", 1),
+                shifted(jnp.take(full, for_before, axis=0), "tile", -1),
+            )
+
+        got_before, got_after = ask(0)
+        table = jnp.concatenate([full, got_before, got_after], 0)
+        last = count - 1
+        base = full.shape[0]
+        where_before = base + jnp.minimum(ranked(to_before), last)
+        where_after = base + count + jnp.minimum(ranked(to_after), last)
+        index = jnp.where(within, place(slot), jnp.where(to_before, where_before, where_after))
+        chosen = jnp.take(table, index, axis=0)
+
+        def more(index, chosen):
+            got_before, got_after = ask(index)
+            for mask, got in ((to_before, got_before), (to_after, got_after)):
+                rank = ranked(mask) - index * count
+                here = mask & (rank >= 0) & (rank < count)
+                chosen = jnp.where(
+                    here[:, None], jnp.take(got, jnp.clip(rank, 0, last), axis=0), chosen
+                )
+            return chosen
+
+        return in_rounds(rounds, more, chosen).reshape(count, 4, EDGE, LANES)
+
+    rows = jnp.arange(tile_count * 4, dtype=jnp.int32)[:, None]
+    hot_within = (rows == jnp.where(within, mine_first(slot), -1)[None, :]).astype(BF)
+
+    def returned(canon):
+        canon = canon.reshape(count * 4, EDGE * LANES)
+        numbers = jnp.arange(count * 4, dtype=jnp.int32)
+
+        def send(index):
+            for_before = picked(to_before, numbers, index * count, count, 0)
+            for_after = picked(to_after, numbers, index * count, count, 0)
+            aim_before = picked(from_before, mine_first(slot_before), index * count, count, -1)
+            aim_after = picked(from_after, mine_first(slot_after), index * count, count, -1)
+            got_before = shifted(jnp.take(canon, for_after, axis=0), "tile", 1)
+            got_after = shifted(jnp.take(canon, for_before, axis=0), "tile", -1)
+            aims = jnp.concatenate([aim_before, aim_after])
+            return (rows == aims[None, :]).astype(BF), got_before, got_after
+
+        hot, *got = send(0)
+        total = mm(jnp.concatenate([hot_within, hot], 1), jnp.concatenate([canon, *got], 0))
+
+        def more(index, total):
+            hot, *got = send(index)
+            return total + mm(hot, jnp.concatenate(got, 0))
+
+        total = in_rounds(rounds, more, total)
+        own, other = total[: count * 4], total[count * 4 :]
+        total = own + swapped(other.astype(BF)).astype(F32)
+        return total.astype(BF).reshape(count, 4, EDGE, LANES)
 
     joined = jnp.stack([w_in[0].T, w_in[1].T, w_out[0], w_out[1]], 0)
     gathered = lax.all_gather(joined, "chan", axis=1, tiled=True)
@@ -366,36 +454,12 @@
         kernels.astype(F32).transpose(0, 2, 1, 3).reshape(2, KS * KS, 1, LANES), (2, KS * KS, 8, LANES)
     )
 
-    own_seams = lax.dynamic_slice_in_dim(seams, chan * count, count, 0)
-    side = jnp.arange(4, dtype=jnp.int32)
-    from_tile = own_seams[:, :4]
-    source = (side[None, :] + 2 + own_seams[:, 4:]) % 4
-    block_offset = (from_tile // tile_count - position + 1) % groups
-    inner = from_tile % tile_count
-    is_mine = (inner // count == chan).reshape(-1, 1)
-    read_index = ((block_offset * count + inner % count) * 4 + source).reshape(-1)
-
-    def choose(mine, other):
-        picked = jnp.where(is_mine, jnp.take(mine, read_index, axis=0), jnp.take(other, read_index, axis=0))
-        return picked.reshape(count, 4, EDGE, LANES)
-
-    targets = seams_all[:, :, :4] * 4 + (side[None, None, :] + 2 + seams_all[:, :, 4:]) % 4
-    targets_mine = lax.dynamic_slice_in_dim(targets, chan * count, count, 1).reshape(-1)
-    targets_other = lax.dynamic_slice_in_dim(targets, (1 - chan) * count, count, 1).reshape(-1)
-    slots = (position * tile_count + chan * count) * 4 + jnp.arange(count * 4, dtype=jnp.int32)
-    hot_mine = (slots[:, None] == targets_mine[None, :]).astype(BF)
-    hot_other = (slots[:, None] == targets_other[None, :]).astype(BF)
-
-    def returned(canon):
-        mine, other = exchange(canon)
-        total = mm(hot_mine, mine) + mm(hot_other, other)
-        return total.astype(BF).reshape(count, 4, EDGE, LANES)
-
-    chosen0 = choose(mine0, other0)
+    chosen0 = fetch(strips0, lambda value: value)
     hidden0, current, strips1 = forward_call(
         offset, count, activations, chosen0, forward_tables, taps[0], gains[0:1], in_w[0], out_w[0]
     )
-    chosen1 = choose(*exchange(strips1))
+    strips1 = strips1.reshape(count * 4, EDGE * LANES)
+    chosen1 = fetch(jnp.concatenate([strips1, swapped(strips1)], 0), mine_first)
     base1, canon1, *grads1 = backward_call(
         True, offset, count, current, chosen1, cotangent, (), backward_tables,
         taps[1], gains[1:2], in_w[1], in_t[1], out_t[1],

time: 308 us -> 321 us (1.042)
  waiting for transfers between devices: 110 us -> 37.3 us
  blocking collectives: 2.76 us -> 40.2 us
  other arithmetic: 12.8 us -> 36.9 us
  local copies, waits for them, and re-layouts: 40.4 us -> 64.2 us
    ppermute x10, waiting for transfers between devices: 94.4 us -> 18.9 us  [shifted(): lax.ppermute(value, axis, [(i, (i + steps) % count) for i in range(count)])]
    pmax x0 -> x1, blocking collectives: none -> 38 us  [local(): rounds = (lax.pmax(most, ('parts', 'tile', 'chan')) + count - 1) // count]
    gather x4 -> x10, local copies, waits for them, and re-layouts: 12.3 us -> 23.4 us  [the longest x2 6.04 us: fetch(): chosen = jnp.take(table, index, axis=0)]
    select_n x1 -> x16, other arithmetic: 0.01 us -> 7.68 us  [the longest x2 1.87 us: fetch(): chosen = jnp.take(table, index, axis=0)]
    concatenate x0 -> x4, other arithmetic: none -> 6.19 us  [the longest x2 4.86 us: fetch(): table = jnp.concatenate([full, got_before, got_after], 0)]
    unnamed x142 -> x149, local copies, waits for them, and re-layouts: 17 us -> 21.8 us
    ppermute x6, waiting for transfers between devices: 13.3 us -> 17.6 us  [reduced(): lax.ppermute(value.astype(BF), axis, [(i, i ^ step) for i in range(count)])]
    convert_element_type x6, other arithmetic: 2.07 us -> 5.69 us  [reduced(): value = value.astype(BF).astype(F32) + got.astype(F32)]
  transfers between devices with their start and end apart: 23 -> 22, of which waited for: 15 -> 12; matrix products, arithmetic and copies ran while one was open for 11% -> 17% of each run, Pallas kernels for 0% -> 9%
where the time goes in v2:
time: 321 us; the launch traced here: 320 us
  Pallas kernels  86.8 us (27%)
  local copies, waits for them, and re-layouts  64.2 us (20%)
  blocking collectives  40.2 us (13%)
  waiting for transfers between devices  37.3 us (12%)
  other arithmetic  36.9 us (11%)
  starting transfers between devices  30.3 us (9%)
  between operations  17.2 us (5%)
  matrix products  6.64 us (2%)
    pallas_call x2, Pallas kernels, backward_call(): pl.pallas_call(first_backward if first else second_backward, grid_spec=pl...  66.6 us
    pmax x1, blocking collectives, local(): rounds = (lax.pmax(most, ('parts', 'tile', 'chan')) + count - 1) // count  38 us
    ppermute x10, starting transfers between devices, shifted(): lax.ppermute(value, axis, [(i, (i + steps) % count) for i in range(count)])  25.4 us
    unnamed x149, local copies, waits for them, and re-layouts  21.8 us
    pallas_call x1, Pallas kernels, forward_call(): pl.pallas_call(forward_kernel, grid_spec=pltpu.PrefetchScalarGridSpec(num...  20.1 us
    ppermute x10, waiting for transfers between devices, shifted(): lax.ppermute(value, axis, [(i, (i + steps) % count) for i in range(count)])  18.9 us
    ppermute x6, waiting for transfers between devices, reduced(): lax.ppermute(value.astype(BF), axis, [(i, i ^ step) for i in range(count)])  17.6 us
  transfers between devices with their start and end apart: 22, of which 12 were waited for; matrix products, arithmetic and copies ran while one was open for 17% of the time, Pallas kernels for 9%

profile of v2, /device:TPU:0, one launch (start us, length us, event | category | flops | bytes accessed | tf_op | source)
XLA Modules:
  0.0 319.7 jit_solution(12265563006832539118)
XLA Ops:
  7.9 3.0 collective-permute-start.10
  10.9 3.1 collective-permute-start.8
  16.6 38.0 %pmax.7 = s32[]{:T(128)} all-reduce(s32[]{:T(128)S(6)} %max.15), channel_id=1, replica_groups=mesh['parts'=2,'tile'=8,'chan'=2] {'parts','tile','chan'}, use_global_device_ids=true, to_apply=%region_8.11 | all-reduce | flops 1 | bytes 8 | tf_op jit(solution)/shard_map/pmax | solution.py:382
  69.1 2.4 reshape.1307
  78.8 2.5 collective-permute-start.9
  81.4 2.3 collective-permute-start.11
  84.9 5.1 %collective-permute-done.9 = bf16[12,6144]{1,0:T(8,128)(2,1)S(1)} collective-permute-done((bf16[12,6144]{1,0:T(8,128)(2,1)S(1)}, bf16[12,6144]{1,0:T(8,128)(2,1)S(1)}, u32[]{:S(2)}, u32[]{:S(2)}) %collective-permute-start.9) | collective-permute-done | bytes 147488 | tf_op jit(solution)/shard_map/ppermute | solution.py:305
  90.0 2.3 collective-permute-done.11
  92.3 2.5 pad_maximum_fusion
  94.9 3.0 gather_fusion.14
  100.1 20.1 %block_forward.1 = (f32[12,256,128]{2,1,0:T(8,128)S(1)}, bf16[12,16,16,128]{3,2,1,0:T(8,128)(2,1)S(1)}, bf16[12,4,48,128]{3,2,1,0:T(8,128)(2,1)S(1)}) custom-call(s32[1]{0:T(128)} %bitcast.10.off_ref, bf16[24,16,16,128]{3,2,1,0:T(8,128)(2,1)S(1)} %copy-done, bf16[12,4,48,128]{3,2,1,0:T(8,128)(2,1)S(1)} %bitcast.192, bf16[48,48]{1,0:T(8,128)(2,1)S(1)} %copy-done.12, ...), custom_call_target="tpu_custom_call" | custom-call | tf_op jit(solution)/shard_map/block_forward/pallas_call | solution.py:211
  124.2 2.9 gather_fusion.16
  127.1 2.9 gather_fusion.15
  132.2 4.8 %collective-permute-start.14 = (bf16[12,6144]{1,0:T(8,128)(2,1)S(1)}, bf16[12,6144]{1,0:T(8,128)(2,1)S(1)}, u32[]{:S(2)}, u32[]{:S(2)}) collective-permute-start(bf16[12,6144]{1,0:T(8,128)(2,1)S(1)} %broadcast_select_fusion.14), channel_id=1, source_target_pairs={{0,14},{2,0},{4,2},{6,4},{8,6},{10,8},{12,10},{14,12},{1,15},{3,1}... | collective-permute-start | bytes 442376 | tf_op jit(solution)/shard_map/ppermute | solution.py:305
  137.6 3.2 collective-permute-done.13
  140.8 2.7 collective-permute-done.14
  143.5 2.3 pad_maximum_fusion.1
  145.8 3.0 gather_fusion.17
  157.8 37.9 %block_backward.2 = (f32[12,16,16,128]{3,2,1,0:T(8,128)S(1)}, bf16[12,4,48,128]{3,2,1,0:T(8,128)(2,1)S(1)}, f32[49,8,128]{2,1,0:T(8,128)S(1)}, f32[8,128]{1,0:T(...) custom-call(s32[1]{0:T(128)} %bitcast.10.off_ref, bf16[12,16,16,128]{3,2,1,0:T(8,128)(2,1)S(1)} %copy-done.9, ...), custom_call_target="tpu_custom_call" | custom-call | tf_op jit(solution)/shard_map/block_backward/pallas_call | solution.py:258
  199.1 2.7 gather_fusion.19
  201.8 2.8 gather_fusion.18
  208.0 4.7 %collective-permute-start.16 = (bf16[12,6144]{1,0:T(8,128)(2,1)}, bf16[12,6144]{1,0:T(8,128)(2,1)}, u32[]{:S(2)}, u32[]{:S(2)}) collective-permute-start(bf16[12,6144]{1,0:T(8,128)(2,1)} %broadcast_select_fusion.11), channel_id=1, source_target_pairs={{0,14},{2,0},{4,2},{6,4},{8,6},{10,8},{12,10},{14,12},{1,15},{3,1}... | collective-permute-start | bytes 442376 | tf_op jit(solution)/shard_map/ppermute | solution.py:305
  218.8 3.2 fusion.37
  225.7 6.2 %collective-permute-done.26 = bf16[562,128]{1,0:T(8,128)(2,1)} collective-permute-done((bf16[562,128]{1,0:T(8,128)(2,1)S(1)}, bf16[562,128]{1,0:T(8,128)(2,1)}, u32[]{:S(2)}, u32[]{:S(2)}) %collective-permute-start.26) | collective-permute-done | bytes 143904 | tf_op jit(solution)/shard_map/ppermute | solution.py:340
  236.0 28.7 %block_backward.3 = (f32[12,16,16,128]{3,2,1,0:T(8,128)S(1)}, bf16[12,4,48,128]{3,2,1,0:T(8,128)(2,1)S(1)}, f32[49,8,128]{2,1,0:T(8,128)S(1)}, f32[8,128]{1,0:T(...) custom-call(s32[1]{0:T(128)} %bitcast.10.off_ref, bf16[24,16,16,128]{3,2,1,0:T(8,128)(2,1)S(1)} %copy-done, ...), custom_call_target="tpu_custom_call" | custom-call | tf_op jit(solution)/shard_map/block_backward/pallas_call | solution.py:258
  268.9 4.4 %collective-permute-start.19 = (bf16[12,6144]{1,0:T(8,128)(2,1)S(1)}, bf16[12,6144]{1,0:T(8,128)(2,1)}, u32[]{:S(2)}, u32[]{:S(2)}) collective-permute-start(bf16[12,6144]{1,0:T(8,128)(2,1)S(1)} %broadcast_select_fusion.10), channel_id=1, source_target_pairs={{0,14},{2,0},{4,2},{6,4},{8,6},{10,8},{12,10},{14,12},{1,15},{3,1}... | collective-permute-start | bytes 442376 | tf_op jit(solution)/shard_map/ppermute | solution.py:305
  275.0 3.0 collective-permute-done.18
  284.4 2.5 collective-permute-start.28
  286.9 2.2 collective-permute-done.22
  292.5 2.5 add_convert_fusion
  298.9 8.0 %collective-permute-done.24 = bf16[562,128]{1,0:T(8,128)(2,1)S(1)} collective-permute-done((bf16[562,128]{1,0:T(8,128)(2,1)S(1)}, bf16[562,128]{1,0:T(8,128)(2,1)S(1)}, u32[]{:S(2)}, u32[]{:S(2)}) %collective-permute-start.24) | collective-permute-done | bytes 143904 | tf_op jit(solution)/shard_map/ppermute | solution.py:340
  309.9 3.0 copy.290
  (343 shorter events, 84.6 us)
Async XLA Ops:
  7.2 302.7 %all-gather.2.cloned.1.call-start = ((), (), s32[]{:S(2)}) async-start(), calls=%async_computation | async-start | bytes 2359296 | tf_op jit(solution)/shard_map/all_gather | solution.py:506
  7.9 63.6 %collective-permute-start.10 = (s32[24,8]{0,1:T(8,128)S(1)}, s32[24,8]{0,1:T(8,128)S(1)}, u32[]{:S(2)}, u32[]{:S(2)}) collective-permute-start(s32[24,8]{0,1:T(8,128)S(1)} %pad_add_fusion.3), channel_id=1, source_target_pairs={{0,2},{2,4},{4,6},{6,8},{8,10},{10,12},{12,14},{14,0},{1,3},{3,5},... | collective-permute-start | bytes 2312 | tf_op jit(solution)/shard_map/ppermute | solution.py:305
  10.9 60.7 %collective-permute-start.8 = (s32[24,8]{0,1:T(8,128)S(1)}, s32[24,8]{0,1:T(8,128)S(1)}, u32[]{:S(2)}, u32[]{:S(2)}) collective-permute-start(s32[24,8]{0,1:T(8,128)S(1)} %pad_add_fusion.3), channel_id=1, source_target_pairs={{0,14},{2,0},{4,2},{6,4},{8,6},{10,8},{12,10},{14,12},{1,15},{3,1}... | collective-permute-start | bytes 2312 | tf_op jit(solution)/shard_map/ppermute | solution.py:305
  58.6 41.5 %copy-start.28 = (f32[1,128]{1,0:T(1,128)}, f32[1,128]{1,0:T(1,128)S(1)}, u32[]{:S(2)}) copy-start(f32[1,128]{1,0:T(1,128)S(1)} %get-tuple-element.1216.gain_ref.rest_8_) | copy-start | bytes 1540
  72.1 12.2 %copy-start.67 = (s32[12,4]{1,0:T(8,128)}, s32[12,4]{1,0:T(8,128)S(1)}, u32[]{:S(2)}) copy-start(s32[12,4]{1,0:T(8,128)S(1)} %copy.183) | copy-start | bytes 580
  72.3 12.1 %copy-start.68 = (s32[12,4]{1,0:T(8,128)}, s32[12,4]{1,0:T(8,128)S(1)}, u32[]{:S(2)}) copy-start(s32[12,4]{1,0:T(8,128)S(1)} %copy.187) | copy-start | bytes 580
  78.8 11.2 %collective-permute-start.9 = (bf16[12,6144]{1,0:T(8,128)(2,1)S(1)}, bf16[12,6144]{1,0:T(8,128)(2,1)S(1)}, u32[]{:S(2)}, u32[]{:S(2)}) collective-permute-start(bf16[12,6144]{1,0:T(8,128)(2,1)S(1)} %broadcast_select_fusion.17), channel_id=1, source_target_pairs={{0,2},{2,4},{4,6},{6,8},{8,10},{10,12},{12,14},{14,0},{1,3},{3,5},... | collective-permute-start | bytes 442376 | tf_op jit(solution)/shard_map/ppermute | solution.py:305
  81.4 10.9 %collective-permute-start.11 = (bf16[12,6144]{1,0:T(8,128)(2,1)S(1)}, bf16[12,6144]{1,0:T(8,128)(2,1)S(1)}, u32[]{:S(2)}, u32[]{:S(2)}) collective-permute-start(bf16[12,6144]{1,0:T(8,128)(2,1)S(1)} %broadcast_select_fusion.16), channel_id=1, source_target_pairs={{0,14},{2,0},{4,2},{6,4},{8,6},{10,8},{12,10},{14,12},{1,15},{3,1}... | collective-permute-start | bytes 442376 | tf_op jit(solution)/shard_map/ppermute | solution.py:305
  120.5 2.1 collective-permute-start.12
  127.1 9.9 %copy-start.77 = (s32[24]{0:T(128)S(1)}, s32[24]{0:T(128)}, u32[]{:S(2)}) copy-start(s32[24]{0:T(128)} %pad_add_fusion.4) | copy-start | bytes 292
  131.0 9.8 %collective-permute-start.13 = (bf16[12,6144]{1,0:T(8,128)(2,1)S(1)}, bf16[12,6144]{1,0:T(8,128)(2,1)S(1)}, u32[]{:S(2)}, u32[]{:S(2)}) collective-permute-start(bf16[12,6144]{1,0:T(8,128)(2,1)S(1)} %broadcast_select_fusion.15), channel_id=1, source_target_pairs={{0,2},{2,4},{4,6},{6,8},{8,10},{10,12},{12,14},{14,0},{1,3},{3,5},... | collective-permute-start | bytes 442376 | tf_op jit(solution)/shard_map/ppermute | solution.py:305
  132.2 11.3 %collective-permute-start.14 = (bf16[12,6144]{1,0:T(8,128)(2,1)S(1)}, bf16[12,6144]{1,0:T(8,128)(2,1)S(1)}, u32[]{:S(2)}, u32[]{:S(2)}) collective-permute-start(bf16[12,6144]{1,0:T(8,128)(2,1)S(1)} %broadcast_select_fusion.14), channel_id=1, source_target_pairs={{0,14},{2,0},{4,2},{6,4},{8,6},{10,8},{12,10},{14,12},{1,15},{3,1}... | collective-permute-start | bytes 442376 | tf_op jit(solution)/shard_map/ppermute | solution.py:305
  201.8 12.3 %copy-start.22 = (f32[49,8,128]{2,1,0:T(8,128)S(1)}, f32[49,8,128]{2,1,0:T(8,128)}, u32[]{:S(2)}) copy-start(f32[49,8,128]{2,1,0:T(8,128)} %copy-done.21) | copy-start | bytes 602116
  206.3 11.3 %collective-permute-start.15 = (bf16[12,6144]{1,0:T(8,128)(2,1)}, bf16[12,6144]{1,0:T(8,128)(2,1)}, u32[]{:S(2)}, u32[]{:S(2)}) collective-permute-start(bf16[12,6144]{1,0:T(8,128)(2,1)} %broadcast_select_fusion.13), channel_id=1, source_target_pairs={{0,2},{2,4},{4,6},{6,8},{8,10},{10,12},{12,14},{14,0},{1,3},{3,5},... | collective-permute-start | bytes 442376 | tf_op jit(solution)/shard_map/ppermute | solution.py:305
  206.3 12.5 %copy-start.63 = (pred[96,48]{1,0:T(32,128)(4,1)S(1)}, pred[96,48]{1,0:T(32,128)(4,1)}, u32[]{:S(2)}) copy-start(pred[96,48]{1,0:T(32,128)(4,1)} %iota_compare_fusion.5) | copy-start | bytes 13828
  206.3 12.5 %copy-start.65 = (pred[96,24]{1,0:T(32,128)(4,1)S(1)}, pred[96,24]{1,0:T(32,128)(4,1)}, u32[]{:S(2)}) copy-start(pred[96,24]{1,0:T(32,128)(4,1)} %iota_compare_fusion.4) | copy-start | bytes 6916
  208.0 10.8 %collective-permute-start.16 = (bf16[12,6144]{1,0:T(8,128)(2,1)}, bf16[12,6144]{1,0:T(8,128)(2,1)}, u32[]{:S(2)}, u32[]{:S(2)}) collective-permute-start(bf16[12,6144]{1,0:T(8,128)(2,1)} %broadcast_select_fusion.11), channel_id=1, source_target_pairs={{0,14},{2,0},{4,2},{6,4},{8,6},{10,8},{12,10},{14,12},{1,15},{3,1}... | collective-permute-start | bytes 442376 | tf_op jit(solution)/shard_map/ppermute | solution.py:305
  217.5 7.0 %collective-permute-start.25 = (bf16[562,128]{1,0:T(8,128)(2,1)}, bf16[562,128]{1,0:T(8,128)(2,1)}, u32[]{:S(2)}, u32[]{:S(2)}) collective-permute-start(bf16[562,128]{1,0:T(8,128)(2,1)} %pad_maximum_fusion.6), channel_id=1, source_target_pairs={{0,1},{1,0},{2,3},{3,2},{4,5},{5,4},{6,7},{7,6},{8,9},{9,8},{10,11... | collective-permute-start | bytes 431624 | tf_op jit(solution)/shard_map/ppermute | solution.py:309
  224.5 9.2 %collective-permute-start.17 = (bf16[48,6144]{1,0:T(8,128)(2,1)}, bf16[48,6144]{1,0:T(8,128)(2,1)}, u32[]{:S(2)}, u32[]{:S(2)}) collective-permute-start(bf16[48,6144]{1,0:T(8,128)(2,1)} %slice.217), channel_id=1, source_target_pairs={{0,1},{1,0},{2,3},{3,2},{4,5},{5,4},{6,7},{7,6},{8,9},{9,8},{10,11... | collective-permute-start | bytes 1769480 | tf_op jit(solution)/shard_map/ppermute | solution.py:309
  225.5 6.4 %collective-permute-start.26 = (bf16[562,128]{1,0:T(8,128)(2,1)S(1)}, bf16[562,128]{1,0:T(8,128)(2,1)}, u32[]{:S(2)}, u32[]{:S(2)}) collective-permute-start(bf16[562,128]{1,0:T(8,128)(2,1)S(1)} %fusion.51), channel_id=1, source_target_pairs={{0,2},{2,0},{4,6},{6,4},{8,10},{10,8},{12,14},{14,12},{1,3},{3,1},... | collective-permute-start | bytes 431624 | tf_op jit(solution)/shard_map/ppermute | solution.py:340
  233.6 49.8 %collective-permute-start.27 = (bf16[562,128]{1,0:T(8,128)(2,1)}, bf16[562,128]{1,0:T(8,128)(2,1)}, u32[]{:S(2)}, u32[]{:S(2)}) collective-permute-start(bf16[562,128]{1,0:T(8,128)(2,1)} %add_convert_fusion.4), channel_id=1, source_target_pairs={{0,4},{2,6},{4,0},{6,2},{8,12},{10,14},{12,8},{14,10},{1,5},{3,7},... | collective-permute-start | bytes 431624 | tf_op jit(solution)/shard_map/ppermute | solution.py:340
  268.5 11.6 %copy-start.64 = (pred[96,48]{1,0:T(32,128)(4,1)S(1)}, pred[96,48]{1,0:T(32,128)(4,1)}, u32[]{:S(2)}) copy-start(pred[96,48]{1,0:T(32,128)(4,1)} %iota_compare_fusion.5) | copy-start | bytes 13828
  268.5 11.6 %copy-start.66 = (pred[96,24]{1,0:T(32,128)(4,1)S(1)}, pred[96,24]{1,0:T(32,128)(4,1)}, u32[]{:S(2)}) copy-start(pred[96,24]{1,0:T(32,128)(4,1)} %iota_compare_fusion.4) | copy-start | bytes 6916
  268.6 9.4 %collective-permute-start.18 = (bf16[12,6144]{1,0:T(8,128)(2,1)S(1)}, bf16[12,6144]{1,0:T(8,128)(2,1)S(1)}, u32[]{:S(2)}, u32[]{:S(2)}) collective-permute-start(bf16[12,6144]{1,0:T(8,128)(2,1)S(1)} %broadcast_select_fusion.12), channel_id=1, source_target_pairs={{0,2},{2,4},{4,6},{6,8},{8,10},{10,12},{12,14},{14,0},{1,3},{3,5},... | collective-permute-start | bytes 442376 | tf_op jit(solution)/shard_map/ppermute | solution.py:305
  268.9 11.2 %collective-permute-start.19 = (bf16[12,6144]{1,0:T(8,128)(2,1)S(1)}, bf16[12,6144]{1,0:T(8,128)(2,1)}, u32[]{:S(2)}, u32[]{:S(2)}) collective-permute-start(bf16[12,6144]{1,0:T(8,128)(2,1)S(1)} %broadcast_select_fusion.10), channel_id=1, source_target_pairs={{0,14},{2,0},{4,2},{6,4},{8,6},{10,8},{12,10},{14,12},{1,15},{3,1}... | collective-permute-start | bytes 442376 | tf_op jit(solution)/shard_map/ppermute | solution.py:305
  273.5 8.1 %copy-start.45 = (f32[49,128]{1,0:T(8,128)}, f32[49,128]{1,0:T(8,128)S(1)}, u32[]{:S(2)}) copy-start(f32[49,128]{1,0:T(8,128)S(1)} %reduce_sum.56) | copy-start | bytes 75268
  275.0 6.9 %collective-permute-start.21 = (bf16[562,128]{1,0:T(8,128)(2,1)}, bf16[562,128]{1,0:T(8,128)(2,1)}, u32[]{:S(2)}, u32[]{:S(2)}) collective-permute-start(bf16[562,128]{1,0:T(8,128)(2,1)} %pad_maximum_fusion.5), channel_id=1, source_target_pairs={{0,1},{1,0},{2,3},{3,2},{4,5},{5,4},{6,7},{7,6},{8,9},{9,8},{10,11... | collective-permute-start | bytes 431624 | tf_op jit(solution)/shard_map/ppermute | solution.py:309
  281.7 8.3 %collective-permute-start.20 = (bf16[48,6144]{1,0:T(8,128)(2,1)S(1)}, bf16[48,6144]{1,0:T(8,128)(2,1)S(1)}, u32[]{:S(2)}, u32[]{:S(2)}) collective-permute-start(bf16[48,6144]{1,0:T(8,128)(2,1)S(1)} %slice.216), channel_id=1, source_target_pairs={{0,1},{1,0},{2,3},{3,2},{4,5},{5,4},{6,7},{7,6},{8,9},{9,8},{10,11... | collective-permute-start | bytes 1769480 | tf_op jit(solution)/shard_map/ppermute | solution.py:309
  282.9 6.3 %collective-permute-start.22 = (bf16[562,128]{1,0:T(8,128)(2,1)S(1)}, bf16[562,128]{1,0:T(8,128)(2,1)S(1)}, u32[]{:S(2)}, u32[]{:S(2)}) collective-permute-start(bf16[562,128]{1,0:T(8,128)(2,1)S(1)} %fusion.50), channel_id=1, source_target_pairs={{0,2},{2,0},{4,6},{6,4},{8,10},{10,8},{12,14},{14,12},{1,3},{3,1},... | collective-permute-start | bytes 431624 | tf_op jit(solution)/shard_map/ppermute | solution.py:340
  284.4 10.6 %collective-permute-start.28 = (bf16[562,128]{1,0:T(8,128)(2,1)S(1)}, bf16[562,128]{1,0:T(8,128)(2,1)}, u32[]{:S(2)}, u32[]{:S(2)}) collective-permute-start(bf16[562,128]{1,0:T(8,128)(2,1)S(1)} %add_convert_fusion.3), channel_id=1, source_target_pairs={{0,8},{2,10},{4,12},{6,14},{8,0},{10,2},{12,4},{14,6},{1,9},{3,11}... | collective-permute-start | bytes 431624 | tf_op jit(solution)/shard_map/ppermute | solution.py:340
  289.2 8.0 %collective-permute-start.23 = (bf16[562,128]{1,0:T(8,128)(2,1)S(1)}, bf16[562,128]{1,0:T(8,128)(2,1)}, u32[]{:S(2)}, u32[]{:S(2)}) collective-permute-start(bf16[562,128]{1,0:T(8,128)(2,1)S(1)} %add_convert_fusion.6), channel_id=1, source_target_pairs={{0,4},{2,6},{4,0},{6,2},{8,12},{10,14},{12,8},{14,10},{1,5},{3,7},... | collective-permute-start | bytes 431624 | tf_op jit(solution)/shard_map/ppermute | solution.py:340
  298.1 8.7 %collective-permute-start.24 = (bf16[562,128]{1,0:T(8,128)(2,1)S(1)}, bf16[562,128]{1,0:T(8,128)(2,1)S(1)}, u32[]{:S(2)}, u32[]{:S(2)}) collective-permute-start(bf16[562,128]{1,0:T(8,128)(2,1)S(1)} %add_convert_fusion.5), channel_id=1, source_target_pairs={{0,8},{2,10},{4,12},{6,14},{8,0},{10,2},{12,4},{14,6},{1,9},{3,11}... | collective-permute-start | bytes 431624 | tf_op jit(solution)/shard_map/ppermute | solution.py:340
  (59 other events, 145.0 us)
Sparse Core Ops, SparseCore 0:
  295.1 10.2 all-gather.1

commit v3 on v2

--- a/solution.py
+++ b/solution.py
@@ -37,17 +37,27 @@
     return jnp.dot(a, b, preferred_element_type=F32)
 
 
-def fill_shifted(x_ref, strips_ref, top_ref, right_ref, left_ref, pad_ref, sh_ref):
+def fill_shifted(info_ref, x_ref, strip_refs, top_ref, right_ref, left_ref, pad_ref, sh_ref):
+    full_ref, before_ref, after_ref = strip_refs
+    full_rows, more_rows = full_ref.shape[0], before_ref.shape[0]
+
+    def strip(side):
+        index = info_ref[1 + pl.program_id(0) * 4 + side]
+        local = full_ref[jnp.minimum(index, full_rows - 1)].astype(F32)
+        before = before_ref[jnp.clip(index - full_rows, 0, more_rows - 1)].astype(F32)
+        after = after_ref[jnp.clip(index - full_rows - more_rows, 0, more_rows - 1)].astype(F32)
+        return jnp.where(index < full_rows, local, jnp.where(index < full_rows + more_rows, before, after))
+
     @pl.when(pl.program_id(0) == 0)
     def _():
         pad_ref[...] = jnp.zeros_like(pad_ref)
 
     end = PAD + S
     pad_ref[PAD:end, 8:24] = x_ref[0].astype(F32)
-    pad_ref[0:PAD, 8:24] = mm(top_ref[...], strips_ref[0, 0]).reshape(PAD, S, LANES)
-    pad_ref[end:, 8:24] = strips_ref[0, 2].astype(F32).reshape(PAD, S, LANES)
-    pad_ref[PAD:end, 24:32] = mm(right_ref[...], strips_ref[0, 1]).reshape(S, 8, LANES)
-    pad_ref[PAD:end, 0:8] = mm(left_ref[...], strips_ref[0, 3]).reshape(S, 8, LANES)
+    pad_ref[0:PAD, 8:24] = mm(top_ref[...], strip(0).astype(BF)).reshape(PAD, S, LANES)
+    pad_ref[end:, 8:24] = strip(2).reshape(PAD, S, LANES)
+    pad_ref[PAD:end, 24:32] = mm(right_ref[...], strip(1).astype(BF)).reshape(S, 8, LANES)
+    pad_ref[PAD:end, 0:8] = mm(left_ref[...], strip(3).astype(BF)).reshape(S, 8, LANES)
     for b in range(KS):
         sh_ref[b] = pad_ref[:, 5 + b : 21 + b, :].reshape(S + 2 * PAD, 2, 8, LANES)
 
@@ -78,10 +88,11 @@
 
 
 def forward_kernel(
-    off_ref, x_ref, strips_ref, top_ref, right_ref, left_ref, extract_ref, kern_ref, gain_ref, w_in_ref, w_out_ref,
+    info_ref, x_ref, full_ref, before_ref, after_ref, top_ref, right_ref, left_ref, extract_ref, kern_ref, gain_ref, w_in_ref, w_out_ref,
     hidden_ref, next_ref, next_strips_ref, pad_ref, sh_ref, hid_ref,
 ):
-    fill_shifted(x_ref, strips_ref, top_ref, right_ref, left_ref, pad_ref, sh_ref)
+    strip_refs = (full_ref, before_ref, after_ref)
+    fill_shifted(info_ref, x_ref, strip_refs, top_ref, right_ref, left_ref, pad_ref, sh_ref)
     depthwise(sh_ref, kern_ref, hid_ref)
     hidden = hid_ref[...].reshape(S * S, LANES)
     hidden_ref[0] = hidden
@@ -95,7 +106,7 @@
 
 
 def backward_kernel(
-    first, x_ref, strips_ref, grad_ref, extra_ref, top_ref, right_ref, left_ref, place_ref, top_t_ref,
+    first, info_ref, x_ref, strip_refs, grad_ref, extra_ref, top_ref, right_ref, left_ref, place_ref, top_t_ref,
     right_t_ref, left_t_ref, kern_ref, gain_ref, w_in_ref, w_in_t_ref, w_out_t_ref,
     base_ref, canon_ref, kg_ref, gg_ref, wi_ref, wo_ref,
     pad_ref, sh_ref, hid_ref, gsh_ref, gh_ref, sum_ref, bl_ref, br_ref,
@@ -108,15 +119,16 @@
         wo_ref[...] = jnp.zeros_like(wo_ref)
         gsh_ref[...] = jnp.zeros_like(gsh_ref)
 
-    fill_shifted(x_ref, strips_ref, top_ref, right_ref, left_ref, pad_ref, sh_ref)
+    fill_shifted(info_ref, x_ref, strip_refs, top_ref, right_ref, left_ref, pad_ref, sh_ref)
     if first:
         depthwise(sh_ref, kern_ref, hid_ref)
         hidden = hid_ref[...].reshape(S * S, LANES)
         gradient = grad_ref[0].reshape(S * S, LANES).astype(F32)
     else:
         hidden = extra_ref[0][0]
+        back = (extra_ref[1][...] + extra_ref[2][...].astype(F32)).astype(BF)
         gradient = grad_ref[0].reshape(S * S, LANES) + mm(
-            place_ref[...], extra_ref[1][0].reshape(4 * EDGE, LANES)
+            place_ref[...], back.reshape(4 * EDGE, LANES)
         )
     sum_ref[...] = gradient.reshape(S, S, LANES)
     low = gradient.astype(BF)
@@ -206,7 +218,7 @@
 PARAMS = pltpu.CompilerParams(vmem_limit_bytes=40 * 1024 * 1024)
 
 
-def forward_call(offset, count, x, strips, tables, kern, gain, w_in, w_out):
+def forward_call(info, count, x, strips, tables, kern, gain, w_in, w_out):
     hidden_units = w_in.shape[1]
     return pl.pallas_call(
         forward_kernel,
@@ -215,7 +227,7 @@
             grid=(count,),
             in_specs=[
                 own_tile((S, S, LANES), count),
-                each_tile((4, EDGE, LANES)),
+                *[whole(part.shape) for part in strips],
                 whole((EDGE, EDGE)),
                 whole((S * 8, EDGE)),
                 whole((S * 8, EDGE)),
@@ -239,28 +251,67 @@
         ],
         compiler_params=PARAMS,
         name="block_forward",
-    )(offset, x, strips, *tables, kern, gain, w_in, w_out)
-
-
-def first_backward(off_ref, x_ref, strips_ref, grad_ref, *rest):
-    backward_kernel(True, x_ref, strips_ref, grad_ref, None, *rest)
-
-
-def second_backward(off_ref, x_ref, strips_ref, grad_ref, hidden_ref, returned_ref, *rest):
-    backward_kernel(False, x_ref, strips_ref, grad_ref, (hidden_ref, returned_ref), *rest)
-
-
-def backward_call(first, offset, count, x, strips, grad, extra, tables, kern, gain, w_in, w_in_t, w_out_t):
+    )(info, x, *strips, *tables, kern, gain, w_in, w_out)
+
+
+def first_backward(info_ref, x_ref, full_ref, before_ref, after_ref, grad_ref, *rest):
+    backward_kernel(True, info_ref, x_ref, (full_ref, before_ref, after_ref), grad_ref, None, *rest)
+
+
+def second_backward(
+    info_ref, x_ref, full_ref, before_ref, after_ref, grad_ref, hidden_ref, own_ref, other_ref, *rest
+):
+    strip_refs = (full_ref, before_ref, after_ref)
+    backward_kernel(False, info_ref, x_ref, strip_refs, grad_ref, (hidden_ref, own_ref, other_ref), *rest)
+
+
+def collect_kernel(aims_ref, canon_ref, before_ref, after_ref, total_ref):
+    total_ref[...] = jnp.zeros_like(total_ref)
+    start = 0
+    for source_ref in (canon_ref, before_ref, after_ref):
+
+        def body(k, carry, source_ref=source_ref, start=start):
+            aim = aims_ref[start + k]
+
+            @pl.when(aim >= 0)
+            def _():
+                place = jnp.maximum(aim, 0)
+                total_ref[place] = total_ref[place] + source_ref[k].astype(F32)
+
+            return carry
+
+        lax.fori_loop(0, source_ref.shape[0], body, 0)
+        start += source_ref.shape[0]
+
+
+def collect_call(aims, canon, before, after):
+    rows = 2 * canon.shape[0]
+    return pl.pallas_call(
+        collect_kernel,
+        grid_spec=pltpu.PrefetchScalarGridSpec(
+            num_scalar_prefetch=1,
+            grid=(1,),
+            in_specs=[whole(canon.shape), whole(before.shape), whole(after.shape)],
+            out_specs=whole((rows, EDGE, LANES)),
+        ),
+        out_shape=jax.ShapeDtypeStruct((rows, EDGE, LANES), F32),
+        compiler_params=PARAMS,
+        name="collect_strips",
+    )(aims, canon, before, after)
+
+
+def backward_call(first, info, count, x, strips, grad, extra, tables, kern, gain, w_in, w_in_t, w_out_t):
     hidden_units = w_in.shape[1]
     x_spec = each_tile((S, S, LANES)) if first else own_tile((S, S, LANES), count)
     grad_spec = own_tile((S, S, LANES), count) if first else each_tile((S, S, LANES))
-    extra_specs = [] if first else [each_tile((S * S, LANES)), each_tile((4, EDGE, LANES))]
+    four = pl.BlockSpec((4, EDGE, LANES), lambda t, off: (t, 0, 0))
+    extra_specs = [] if first else [each_tile((S * S, LANES)), four, four]
     return pl.pallas_call(
         first_backward if first else second_backward,
         grid_spec=pltpu.PrefetchScalarGridSpec(
             num_scalar_prefetch=1,
             grid=(count,),
-            in_specs=[x_spec, each_tile((4, EDGE, LANES)), grad_spec]
+            in_specs=[x_spec, *[whole(part.shape) for part in strips], grad_spec]
             + extra_specs
             + [whole(table.shape) for table in tables]
             + [
@@ -297,7 +348,7 @@
         ],
         compiler_params=PARAMS,
         name="block_backward",
-    )(offset, x, strips, grad, *extra, *tables, kern, gain, w_in, w_in_t, w_out_t)
+    )(info, x, *strips, grad, *extra, *tables, kern, gain, w_in, w_in_t, w_out_t)
 
 
 def shifted(value, axis, steps):
@@ -329,6 +380,17 @@
         lambda carry: (carry[0] + 1, body(carry[0], carry[1])),
         (jnp.int32(1), state),
     )[1]
+
+
+def highest(value, axis):
+    count = lax.axis_size(axis)
+    if count & (count - 1):
+        return lax.pmax(value, axis)
+    step = 1
+    while step < count:
+        value = jnp.maximum(value, lax.ppermute(value, axis, [(i, i ^ step) for i in range(count)]))
+        step *= 2
+    return value
 
 
 def reduced(value, axis):
@@ -350,7 +412,6 @@
     position = lax.axis_index("tile")
     groups = lax.axis_size("tile")
     half_units = w_in.shape[2]
-    offset = chan.astype(jnp.int32).reshape(1)
 
     extract, top, right, left = [jnp.asarray(table, BF) for table in permutation_tables()]
     forward_tables = (top, right, left, extract)
@@ -378,12 +439,15 @@
     within = owner == position
     from_before = owner_before == position
     from_after = owner_after == position
-    most = jnp.maximum(jnp.sum(to_before.astype(jnp.int32)), jnp.sum(to_after.astype(jnp.int32)))
-    rounds = (lax.pmax(most, ("parts", "tile", "chan")) + count - 1) // count
+    owners = (neighbours // tile_count).reshape(2, count * 4)
+    before_count = jnp.sum((owners == (position - 1) % groups).astype(jnp.int32), 1)
+    after_count = jnp.sum((owners == (position + 1) % groups).astype(jnp.int32), 1)
+    most = jnp.broadcast_to(jnp.max(jnp.maximum(before_count, after_count)), (LANES,))
+    rounds = (highest(most, "tile")[0] + count - 1) // count
 
     strips0 = jnp.einsum(
         "pk,tkc->tpc", extract, activations.reshape(tile_count, S * S, LANES), preferred_element_type=F32
-    ).astype(BF).reshape(tile_count * 4, EDGE * LANES)
+    ).astype(BF).reshape(tile_count * 4, EDGE, LANES)
 
     def fetch(full, place):
         def ask(index):
@@ -394,32 +458,26 @@
                 shifted(jnp.take(full, for_before, axis=0), "tile", -1),
             )
 
-        got_before, got_after = ask(0)
-        table = jnp.concatenate([full, got_before, got_after], 0)
-        last = count - 1
+        def widened(got):
+            return jnp.pad(got, ((0, 3 * count), (0, 0), (0, 0)))
+
+        def more(index, state):
+            return tuple(
+                lax.dynamic_update_slice_in_dim(held, got, index * count, 0)
+                for held, got in zip(state, ask(index))
+            )
+
+        before, after = in_rounds(rounds, more, tuple(widened(got) for got in ask(0)))
         base = full.shape[0]
-        where_before = base + jnp.minimum(ranked(to_before), last)
-        where_after = base + count + jnp.minimum(ranked(to_after), last)
+        where_before = base + ranked(to_before)
+        where_after = base + 4 * count + ranked(to_after)
         index = jnp.where(within, place(slot), jnp.where(to_before, where_before, where_after))
-        chosen = jnp.take(table, index, axis=0)
-
-        def more(index, chosen):
-            got_before, got_after = ask(index)
-            for mask, got in ((to_before, got_before), (to_after, got_after)):
-                rank = ranked(mask) - index * count
-                here = mask & (rank >= 0) & (rank < count)
-                chosen = jnp.where(
-                    here[:, None], jnp.take(got, jnp.clip(rank, 0, last), axis=0), chosen
-                )
-            return chosen
-
-        return in_rounds(rounds, more, chosen).reshape(count, 4, EDGE, LANES)
-
-    rows = jnp.arange(tile_count * 4, dtype=jnp.int32)[:, None]
-    hot_within = (rows == jnp.where(within, mine_first(slot), -1)[None, :]).astype(BF)
+        return jnp.concatenate([chan.astype(jnp.int32).reshape(1), index]), (full, before, after)
+
+    aim_within = jnp.where(within, mine_first(slot), -1)
 
     def returned(canon):
-        canon = canon.reshape(count * 4, EDGE * LANES)
+        canon = canon.reshape(count * 4, EDGE, LANES)
         numbers = jnp.arange(count * 4, dtype=jnp.int32)
 
         def send(index):
@@ -429,20 +487,18 @@
             aim_after = picked(from_after, mine_first(slot_after), index * count, count, -1)
             got_before = shifted(jnp.take(canon, for_after, axis=0), "tile", 1)
             got_after = shifted(jnp.take(canon, for_before, axis=0), "tile", -1)
-            aims = jnp.concatenate([aim_before, aim_after])
-            return (rows == aims[None, :]).astype(BF), got_before, got_after
-
-        hot, *got = send(0)
-        total = mm(jnp.concatenate([hot_within, hot], 1), jnp.concatenate([canon, *got], 0))
+            return jnp.concatenate([aim_before, aim_after]), got_before, got_after
+
+        aims, got_before, got_after = send(0)
+        total = collect_call(jnp.concatenate([aim_within, aims]), canon, got_before, got_after)
 
         def more(index, total):
-            hot, *got = send(index)
-            return total + mm(hot, jnp.concatenate(got, 0))
+            aims, *got = send(index)
+            aims = jnp.where(aims < 0, tile_count * 4, aims)
+            return total.at[aims].add(jnp.concatenate(got, 0).astype(F32), mode="drop")
 
         total = in_rounds(rounds, more, total)
-        own, other = total[: count * 4], total[count * 4 :]
-        total = own + swapped(other.astype(BF)).astype(F32)
-        return total.astype(BF).reshape(count, 4, EDGE, LANES)
+        return total, swapped(total[count * 4 :].astype(BF))
 
     joined = jnp.stack([w_in[0].T, w_in[1].T, w_out[0], w_out[1]], 0)
     gathered = lax.all_gather(joined, "chan", axis=1, tiled=True)
@@ -454,14 +510,14 @@
         kernels.astype(F32).transpose(0, 2, 1, 3).reshape(2, KS * KS, 1, LANES), (2, KS * KS, 8, LANES)
     )
 
-    chosen0 = fetch(strips0, lambda value: value)
+    info0, chosen0 = fetch(strips0, lambda value: value)
     hidden0, current, strips1 = forward_call(
-        offset, count, activations, chosen0, forward_tables, taps[0], gains[0:1], in_w[0], out_w[0]
-    )
-    strips1 = strips1.reshape(count * 4, EDGE * LANES)
-    chosen1 = fetch(jnp.concatenate([strips1, swapped(strips1)], 0), mine_first)
+        info0, count, activations, chosen0, forward_tables, taps[0], gains[0:1], in_w[0], out_w[0]
+    )
+    strips1 = strips1.reshape(count * 4, EDGE, LANES)
+    info1, chosen1 = fetch(jnp.concatenate([strips1, swapped(strips1)], 0), mine_first)
     base1, canon1, *grads1 = backward_call(
-        True, offset, count, current, chosen1, cotangent, (), backward_tables,
+        True, info1, count, current, chosen1, cotangent, (), backward_tables,
         taps[1], gains[1:2], in_w[1], in_t[1], out_t[1],
     )
 
@@ -494,10 +550,11 @@
     sums1 = split(grads1)
     returned1 = returned(canon1)
     base0, canon0, *grads0 = backward_call(
-        False, offset, count, activations, chosen0, base1, (hidden0, returned1), backward_tables,
+        False, info0, count, activations, chosen0, base1, (hidden0, *returned1), backward_tables,
         taps[0], gains[0:1], in_w[0], in_t[0], out_t[0],
     )
-    returned0 = returned(canon0)
+    own0, other0 = returned(canon0)
+    returned0 = (own0[: count * 4] + other0.astype(F32)).astype(BF)
     sums0 = split(grads0)
     placed = jnp.einsum(
         "kp,tpc->tkc", extract.T, returned0.reshape(count, 4 * EDGE, LANES), preferred_element_type=F32

time: 321 us -> 285 us (0.89)
  blocking collectives: 40.2 us -> 2.18 us
  Pallas kernels: 86.8 us -> 103 us
  waiting for transfers between devices: 37.3 us -> 25.4 us
  matrix products: 6.64 us -> 0.9 us
  local copies, waits for them, and re-layouts: 64.2 us -> 69.8 us
  other arithmetic: 36.9 us -> 33.2 us
    pmax x1 -> x0, blocking collectives: 38 us -> none  [local(): rounds = (lax.pmax(most, ('parts', 'tile', 'chan')) + count - 1) // count]
    ppermute x10, waiting for transfers between devices: 18.9 us -> 3.45 us  [shifted(): lax.ppermute(value, axis, [(i, (i + steps) % count) for i in range(count)])]
    unnamed x149 -> x162, local copies, waits for them, and re-layouts: 21.8 us -> 35 us
    pallas_call x0 -> x2, Pallas kernels: none -> 7.78 us  [collect_call(): pl.pallas_call(collect_kernel, grid_spec=pltpu.PrefetchScalarGridSpec(num...]
    pallas_call x2, Pallas kernels: 66.6 us -> 73 us  [backward_call(): pl.pallas_call(first_backward if first else second_backward, grid_spec=pl...]
    gather x2 -> x0, local copies, waits for them, and re-layouts: 6.04 us -> none  [fetch(): chosen = jnp.take(table, index, axis=0)]
    dot_general x2 -> x0, matrix products: 4.72 us -> none  [mm(): return jnp.dot(a, b, preferred_element_type=F32)]
    pad x0 -> x4, local copies, waits for them, and re-layouts: none -> 3.58 us  [widened(): return jnp.pad(got, ((0, 3 * count), (0, 0), (0, 0)))]
  transfers between devices with their start and end apart: 22 -> 25, of which waited for: 12 -> 10; matrix products, arithmetic and copies ran while one was open for 17% -> 20% of each run, Pallas kernels for 9% -> 14%
where the time goes in v3:
time: 285 us; the launch traced here: 284 us
  Pallas kernels  103 us (36%)
  local copies, waits for them, and re-layouts  69.8 us (24%)
  starting transfers between devices  33.4 us (12%)
  other arithmetic  33.2 us (12%)
  waiting for transfers between devices  25.4 us (9%)
  between operations  15.2 us (5%)
    pallas_call x2, Pallas kernels, backward_call(): pl.pallas_call(first_backward if first else second_backward, grid_spec=pl...  73 us
    unnamed x162, local copies, waits for them, and re-layouts  35 us
    ppermute x10, starting transfers between devices, shifted(): lax.ppermute(value, axis, [(i, (i + steps) % count) for i in range(count)])  25 us
    pallas_call x1, Pallas kernels, forward_call(): pl.pallas_call(forward_kernel, grid_spec=pltpu.PrefetchScalarGridSpec(num...  22.5 us
    ppermute x6, waiting for transfers between devices, reduced(): lax.ppermute(value.astype(BF), axis, [(i, i ^ step) for i in range(count)])  16.6 us
    pallas_call x2, Pallas kernels, collect_call(): pl.pallas_call(collect_kernel, grid_spec=pltpu.PrefetchScalarGridSpec(num...  7.78 us
    ppermute x6, starting transfers between devices, reduced(): lax.ppermute(value.astype(BF), axis, [(i, i ^ step) for i in range(count)])  6.53 us
  transfers between devices with their start and end apart: 25, of which 10 were waited for; matrix products, arithmetic and copies ran while one was open for 20% of the time, Pallas kernels for 14%

profile of v3, /device:TPU:0, one launch (start us, length us, event | category | flops | bytes accessed | tf_op | source)
XLA Modules:
  0.0 283.6 jit_solution(14254525757246187194)
XLA Ops:
  7.9 3.0 %collective-permute-start.10 = (s32[24,8]{0,1:T(8,128)S(1)}, s32[24,8]{0,1:T(8,128)S(1)}, u32[]{:S(2)}, u32[]{:S(2)}) collective-permute-start(s32[24,8]{0,1:T(8,128)S(1)} %pad_add_fusion), channel_id=1, source_target_pairs={{0,2},{2,4},{4,6},{6,8},{8,10},{10,12},{12,14},{14,0},{1,3},{3,5},... | collective-permute-start | bytes 2312 | tf_op jit(solution)/shard_map/ppermute | solution.py:356
  10.9 3.1 %collective-permute-start.8 = (s32[24,8]{0,1:T(8,128)S(1)}, s32[24,8]{0,1:T(8,128)S(1)}, u32[]{:S(2)}, u32[]{:S(2)}) collective-permute-start(s32[24,8]{0,1:T(8,128)S(1)} %pad_add_fusion), channel_id=1, source_target_pairs={{0,14},{2,0},{4,2},{6,4},{8,6},{10,8},{12,10},{14,12},{1,15},{3,1}... | collective-permute-start | bytes 2312 | tf_op jit(solution)/shard_map/ppermute | solution.py:356
  24.1 2.2 all_gather.6
  34.6 1.5 collective-permute-start.9
  36.9 3.2 %collective-permute-start.11 = (bf16[12,48,128]{2,1,0:T(8,128)(2,1)}, bf16[12,48,128]{2,1,0:T(8,128)(2,1)S(1)}, u32[]{:S(2)}, u32[]{:S(2)}) collective-permute-start(bf16[12,48,128]{2,1,0:T(8,128)(2,1)} %broadcast_select_fusion.14), channel_id=1, source_target_pairs={{0,14},{2,0},{4,2},{6,4},{8,6},{10,8},{12,10},{14,12},{1,15},{3,1}... | collective-permute-start | bytes 442376 | tf_op jit(solution)/shard_map/ppermute | solution.py:356
  41.8 3.4 %collective-permute-done.14 = s32[128]{0:T(128)S(1)} collective-permute-done((s32[128]{0:T(128)S(1)}, s32[128]{0:T(128)S(1)}, u32[]{:S(2)}, u32[]{:S(2)}) %collective-permute-start.14) | collective-permute-done | bytes 544 | tf_op jit(solution)/shard_map/ppermute | solution.py:391
  50.8 22.5 %block_forward.1 = (f32[12,256,128]{2,1,0:T(8,128)S(1)}, bf16[12,16,16,128]{3,2,1,0:T(8,128)(2,1)S(1)}, bf16[12,4,48,128]{3,2,1,0:T(8,128)(2,1)S(1)}) custom-call(s32[49]{0:T(128)S(1)} %pad_add_fusion.1.info_ref, bf16[24,16,16,128]{3,2,1,0:T(8,128)(2,1)S(1)} %copy-done, bf16[96,48,128]{2,1,0:T(8,128)(2,1)} %copy-done.47, ...), custom_call_target="tpu_custom_call" | custom-call | tf_op jit(solution)/shard_map/block_forward/pallas_call | solution.py:223
  74.5 2.0 collective-permute-done.15
  77.6 1.8 gather_fusion.11
  79.4 1.8 gather_fusion.10
  81.6 4.8 %collective-permute-start.17 = (bf16[12,48,128]{2,1,0:T(8,128)(2,1)S(1)}, bf16[12,48,128]{2,1,0:T(8,128)(2,1)S(1)}, u32[]{:S(2)}, u32[]{:S(2)}) collective-permute-start(bf16[12,48,128]{2,1,0:T(8,128)(2,1)S(1)} %broadcast_select_fusion.12), channel_id=1, source_target_pairs={{0,14},{2,0},{4,2},{6,4},{8,6},{10,8},{12,10},{14,12},{1,15},{3,1}... | collective-permute-start | bytes 442376 | tf_op jit(solution)/shard_map/ppermute | solution.py:356
  89.0 1.6 collective-permute-done.17
  101.4 41.0 %block_backward.2 = (f32[12,16,16,128]{3,2,1,0:T(8,128)S(1)}, bf16[12,4,48,128]{3,2,1,0:T(8,128)(2,1)}, f32[49,8,128]{2,1,0:T(8,128)S(1)}, f32[8,128]{1,0:T(8,12...) custom-call(s32[49]{0:T(128)S(1)} %copy-done.46, bf16[12,16,16,128]{3,2,1,0:T(8,128)(2,1)S(1)} %copy-done.15, ...), custom_call_target="tpu_custom_call" | custom-call | tf_op jit(solution)/shard_map/block_backward/pallas_call | solution.py:309
  147.0 1.8 gather_fusion.13
  148.8 1.8 gather_fusion.12
  153.3 4.7 %collective-permute-start.19 = (bf16[12,48,128]{2,1,0:T(8,128)(2,1)}, bf16[12,48,128]{2,1,0:T(8,128)(2,1)S(1)}, u32[]{:S(2)}, u32[]{:S(2)}) collective-permute-start(bf16[12,48,128]{2,1,0:T(8,128)(2,1)} %broadcast_select_fusion.9), channel_id=1, source_target_pairs={{0,14},{2,0},{4,2},{6,4},{8,6},{10,8},{12,10},{14,12},{1,15},{3,1}... | collective-permute-start | bytes 442376 | tf_op jit(solution)/shard_map/ppermute | solution.py:356
  162.2 4.4 %collect_strips.2 = f32[96,48,128]{2,1,0:T(8,128)} custom-call(s32[72]{0:T(128)S(1)} %copy-done.37, bf16[48,48,128]{2,1,0:T(8,128)(2,1)} %bitcast.194, bf16[12,48,128]{2,1,0:T(8,128)(2,1)S(1)} %collective-permute-done.18.before_ref, bf16[12,48,128]{2,1,0:T(8,128)(2,1)S(1)} %collective-permute-done.19.after_ref), custom_call_target="tpu_custom_call" | custom-call | tf_op jit(solution)/shard_map/collect_strips/pallas_call | solution.py:289
  166.9 2.2 slice.202
  171.0 5.4 %collective-permute-done.29 = bf16[562,128]{1,0:T(8,128)(2,1)S(1)} collective-permute-done((bf16[562,128]{1,0:T(8,128)(2,1)S(1)}, bf16[562,128]{1,0:T(8,128)(2,1)S(1)}, u32[]{:S(2)}, u32[]{:S(2)}) %collective-permute-start.29) | collective-permute-done | bytes 143904 | tf_op jit(solution)/shard_map/ppermute | solution.py:402
  187.8 32.0 %block_backward.3 = (f32[12,16,16,128]{3,2,1,0:T(8,128)S(1)}, bf16[12,4,48,128]{3,2,1,0:T(8,128)(2,1)}, f32[49,8,128]{2,1,0:T(8,128)S(1)}, f32[8,128]{1,0:T(8,12...) custom-call(s32[49]{0:T(128)S(1)} %copy-done.45, bf16[24,16,16,128]{3,2,1,0:T(8,128)(2,1)S(1)} %copy-done, ...), custom_call_target="tpu_custom_call" | custom-call | tf_op jit(solution)/shard_map/block_backward/pallas_call | solution.py:309
  222.5 1.8 gather_fusion.15
  224.3 1.8 gather_fusion.14
  229.9 4.4 %collective-permute-start.22 = (bf16[12,48,128]{2,1,0:T(8,128)(2,1)}, bf16[12,48,128]{2,1,0:T(8,128)(2,1)S(1)}, u32[]{:S(2)}, u32[]{:S(2)}) collective-permute-start(bf16[12,48,128]{2,1,0:T(8,128)(2,1)} %broadcast_select_fusion.8), channel_id=1, source_target_pairs={{0,14},{2,0},{4,2},{6,4},{8,6},{10,8},{12,10},{14,12},{1,15},{3,1}... | collective-permute-start | bytes 442376 | tf_op jit(solution)/shard_map/ppermute | solution.py:356
  239.0 3.4 %collect_strips.3 = f32[96,48,128]{2,1,0:T(8,128)} custom-call(s32[72]{0:T(128)S(1)} %copy-done.38, bf16[48,48,128]{2,1,0:T(8,128)(2,1)S(1)} %bitcast.190, bf16[12,48,128]{2,1,0:T(8,128)(2,1)S(1)} %collective-permute-done.21.before_ref, bf16[12,48,128]{2,1,0:T(8,128)(2,1)S(1)} %collective-permute-done.22.after_ref), custom_call_target="tpu_custom_call" | custom-call | tf_op jit(solution)/shard_map/collect_strips/pallas_call | solution.py:289
  242.5 1.5 slice.201
  246.2 3.5 %collective-permute-start.31 = (bf16[562,128]{1,0:T(8,128)(2,1)S(1)}, bf16[562,128]{1,0:T(8,128)(2,1)}, u32[]{:S(2)}, u32[]{:S(2)}) collective-permute-start(bf16[562,128]{1,0:T(8,128)(2,1)S(1)} %add_convert_fusion.2), channel_id=1, source_target_pairs={{0,8},{2,10},{4,12},{6,14},{8,0},{10,2},{12,4},{14,6},{1,9},{3,11}... | collective-permute-start | bytes 431624 | tf_op jit(solution)/shard_map/ppermute | solution.py:402
  249.7 1.6 collective-permute-done.25
  252.0 1.5 collective-permute-start.26
  254.1 1.6 copy.179
  255.7 2.5 add_convert_fusion
  262.3 8.5 %collective-permute-done.27 = bf16[562,128]{1,0:T(8,128)(2,1)S(1)} collective-permute-done((bf16[562,128]{1,0:T(8,128)(2,1)S(1)}, bf16[562,128]{1,0:T(8,128)(2,1)S(1)}, u32[]{:S(2)}, u32[]{:S(2)}) %collective-permute-start.27) | collective-permute-done | bytes 143904 | tf_op jit(solution)/shard_map/ppermute | solution.py:402
  273.7 3.0 %copy.251 = bf16[24,16,16,128]{3,2,1,0:T(8,128)(2,1)} copy(bf16[24,16,16,128]{3,2,1,0:T(8,128)(2,1)} %all-gather.2.cloned.1.call-done) | data formatting | bytes 3145728
  (361 shorter events, 89.1 us)
Async XLA Ops:
  7.2 266.6 %all-gather.2.cloned.1.call-start = ((), (), s32[]{:S(2)}) async-start(), calls=%async_computation | async-start | bytes 2359296 | tf_op jit(solution)/shard_map/all_gather | solution.py:563
  7.9 22.4 %collective-permute-start.10 = (s32[24,8]{0,1:T(8,128)S(1)}, s32[24,8]{0,1:T(8,128)S(1)}, u32[]{:S(2)}, u32[]{:S(2)}) collective-permute-start(s32[24,8]{0,1:T(8,128)S(1)} %pad_add_fusion), channel_id=1, source_target_pairs={{0,2},{2,4},{4,6},{6,8},{8,10},{10,12},{12,14},{14,0},{1,3},{3,5},... | collective-permute-start | bytes 2312 | tf_op jit(solution)/shard_map/ppermute | solution.py:356
  10.9 19.5 %collective-permute-start.8 = (s32[24,8]{0,1:T(8,128)S(1)}, s32[24,8]{0,1:T(8,128)S(1)}, u32[]{:S(2)}, u32[]{:S(2)}) collective-permute-start(s32[24,8]{0,1:T(8,128)S(1)} %pad_add_fusion), channel_id=1, source_target_pairs={{0,14},{2,0},{4,2},{6,4},{8,6},{10,8},{12,10},{14,12},{1,15},{3,1}... | collective-permute-start | bytes 2312 | tf_op jit(solution)/shard_map/ppermute | solution.py:356
  16.3 12.8 %collective-permute-start.12 = (s32[128]{0:T(128)S(1)}, s32[128]{0:T(128)S(1)}, u32[]{:S(2)}, u32[]{:S(2)}) collective-permute-start(s32[128]{0:T(128)S(1)} %broadcast_in_dim.441), channel_id=1, source_target_pairs={{0,2},{2,0},{4,6},{6,4},{8,10},{10,8},{12,14},{14,12},{1,3},{3,1},... | collective-permute-start | bytes 1544 | tf_op jit(solution)/shard_map/ppermute | solution.py:391
  17.0 19.2 %copy-start.61 = (pred[48]{0:T(512)(128)(4,1)}, pred[48]{0:T(512)(128)(4,1)S(1)}, u32[]{:S(2)}) copy-start(pred[48]{0:T(512)(128)(4,1)S(1)} %eq.632) | copy-start | bytes 148
  19.8 30.0 %copy-start.39 = (f32[1,128]{1,0:T(1,128)}, f32[1,128]{1,0:T(1,128)S(1)}, u32[]{:S(2)}) copy-start(f32[1,128]{1,0:T(1,128)S(1)} %get-tuple-element.1132.gain_ref.rest_8_) | copy-start | bytes 1540
  29.7 10.4 %collective-permute-start.13 = (s32[128]{0:T(128)S(1)}, s32[128]{0:T(128)S(1)}, u32[]{:S(2)}, u32[]{:S(2)}) collective-permute-start(s32[128]{0:T(128)S(1)} %broadcast_maximum_fusion), channel_id=1, source_target_pairs={{0,4},{2,6},{4,0},{6,2},{8,12},{10,14},{12,8},{14,10},{1,5},{3,7},... | collective-permute-start | bytes 1544 | tf_op jit(solution)/shard_map/ppermute | solution.py:391
  30.8 16.9 %copy-start.77 = (s32[12,4]{1,0:T(8,128)}, s32[12,4]{1,0:T(8,128)S(1)}, u32[]{:S(2)}) copy-start(s32[12,4]{1,0:T(8,128)S(1)} %copy.167) | copy-start | bytes 580
  30.9 16.8 %copy-start.67 = (s32[48]{0:T(128)}, s32[48]{0:T(128)S(1)}, u32[]{:S(2)}) copy-start(s32[48]{0:T(128)S(1)} %broadcast_in_dim.439) | copy-start | bytes 580
  31.0 16.7 %copy-start.78 = (s32[12,4]{1,0:T(8,128)}, s32[12,4]{1,0:T(8,128)S(1)}, u32[]{:S(2)}) copy-start(s32[12,4]{1,0:T(8,128)S(1)} %copy.163) | copy-start | bytes 580
  31.1 16.6 %copy-start.70 = (s32[48]{0:T(128)}, s32[48]{0:T(128)S(1)}, u32[]{:S(2)}) copy-start(s32[48]{0:T(128)S(1)} %broadcast_in_dim.436) | copy-start | bytes 580
  34.6 12.2 %collective-permute-start.9 = (bf16[12,48,128]{2,1,0:T(8,128)(2,1)}, bf16[12,48,128]{2,1,0:T(8,128)(2,1)S(1)}, u32[]{:S(2)}, u32[]{:S(2)}) collective-permute-start(bf16[12,48,128]{2,1,0:T(8,128)(2,1)} %broadcast_select_fusion.15), channel_id=1, source_target_pairs={{0,2},{2,4},{4,6},{6,8},{8,10},{10,12},{12,14},{14,0},{1,3},{3,5},... | collective-permute-start | bytes 442376 | tf_op jit(solution)/shard_map/ppermute | solution.py:356
  36.9 9.0 %collective-permute-start.11 = (bf16[12,48,128]{2,1,0:T(8,128)(2,1)}, bf16[12,48,128]{2,1,0:T(8,128)(2,1)S(1)}, u32[]{:S(2)}, u32[]{:S(2)}) collective-permute-start(bf16[12,48,128]{2,1,0:T(8,128)(2,1)} %broadcast_select_fusion.14), channel_id=1, source_target_pairs={{0,14},{2,0},{4,2},{6,4},{8,6},{10,8},{12,10},{14,12},{1,15},{3,1}... | collective-permute-start | bytes 442376 | tf_op jit(solution)/shard_map/ppermute | solution.py:356
  40.7 4.5 %collective-permute-start.14 = (s32[128]{0:T(128)S(1)}, s32[128]{0:T(128)S(1)}, u32[]{:S(2)}, u32[]{:S(2)}) collective-permute-start(s32[128]{0:T(128)S(1)} %fusion.71), channel_id=1, source_target_pairs={{0,8},{2,10},{4,12},{6,14},{8,0},{10,2},{12,4},{14,6},{1,9},{3,11}... | collective-permute-start | bytes 1544 | tf_op jit(solution)/shard_map/ppermute | solution.py:391
  74.5 2.0 collective-permute-start.15
  81.4 10.2 %collective-permute-start.16 = (bf16[12,48,128]{2,1,0:T(8,128)(2,1)S(1)}, bf16[12,48,128]{2,1,0:T(8,128)(2,1)S(1)}, u32[]{:S(2)}, u32[]{:S(2)}) collective-permute-start(bf16[12,48,128]{2,1,0:T(8,128)(2,1)S(1)} %broadcast_select_fusion.13), channel_id=1, source_target_pairs={{0,2},{2,4},{4,6},{6,8},{8,10},{10,12},{12,14},{14,0},{1,3},{3,5},... | collective-permute-start | bytes 442376 | tf_op jit(solution)/shard_map/ppermute | solution.py:356
  81.6 9.1 %collective-permute-start.17 = (bf16[12,48,128]{2,1,0:T(8,128)(2,1)S(1)}, bf16[12,48,128]{2,1,0:T(8,128)(2,1)S(1)}, u32[]{:S(2)}, u32[]{:S(2)}) collective-permute-start(bf16[12,48,128]{2,1,0:T(8,128)(2,1)S(1)} %broadcast_select_fusion.12), channel_id=1, source_target_pairs={{0,14},{2,0},{4,2},{6,4},{8,6},{10,8},{12,10},{14,12},{1,15},{3,1}... | collective-permute-start | bytes 442376 | tf_op jit(solution)/shard_map/ppermute | solution.py:356
  151.9 9.6 %collective-permute-start.18 = (bf16[12,48,128]{2,1,0:T(8,128)(2,1)}, bf16[12,48,128]{2,1,0:T(8,128)(2,1)S(1)}, u32[]{:S(2)}, u32[]{:S(2)}) collective-permute-start(bf16[12,48,128]{2,1,0:T(8,128)(2,1)} %broadcast_select_fusion.11), channel_id=1, source_target_pairs={{0,2},{2,4},{4,6},{6,8},{8,10},{10,12},{12,14},{14,0},{1,3},{3,5},... | collective-permute-start | bytes 442376 | tf_op jit(solution)/shard_map/ppermute | solution.py:356
  153.3 9.0 %collective-permute-start.19 = (bf16[12,48,128]{2,1,0:T(8,128)(2,1)}, bf16[12,48,128]{2,1,0:T(8,128)(2,1)S(1)}, u32[]{:S(2)}, u32[]{:S(2)}) collective-permute-start(bf16[12,48,128]{2,1,0:T(8,128)(2,1)} %broadcast_select_fusion.9), channel_id=1, source_target_pairs={{0,14},{2,0},{4,2},{6,4},{8,6},{10,8},{12,10},{14,12},{1,15},{3,1}... | collective-permute-start | bytes 442376 | tf_op jit(solution)/shard_map/ppermute | solution.py:356
  161.4 7.7 %collective-permute-start.28 = (bf16[562,128]{1,0:T(8,128)(2,1)S(1)}, bf16[562,128]{1,0:T(8,128)(2,1)}, u32[]{:S(2)}, u32[]{:S(2)}) collective-permute-start(bf16[562,128]{1,0:T(8,128)(2,1)S(1)} %pad_maximum_fusion.5), channel_id=1, source_target_pairs={{0,1},{1,0},{2,3},{3,2},{4,5},{5,4},{6,7},{7,6},{8,9},{9,8},{10,11... | collective-permute-start | bytes 431624 | tf_op jit(solution)/shard_map/ppermute | solution.py:360
  169.1 8.5 %collective-permute-start.20 = (bf16[48,48,128]{2,1,0:T(8,128)(2,1)}, bf16[48,48,128]{2,1,0:T(8,128)(2,1)S(1)}, u32[]{:S(2)}, u32[]{:S(2)}) collective-permute-start(bf16[48,48,128]{2,1,0:T(8,128)(2,1)} %slice.202), channel_id=1, source_target_pairs={{0,1},{1,0},{2,3},{3,2},{4,5},{5,4},{6,7},{7,6},{8,9},{9,8},{10,11... | collective-permute-start | bytes 1769480 | tf_op jit(solution)/shard_map/ppermute | solution.py:360
  170.1 6.3 %collective-permute-start.29 = (bf16[562,128]{1,0:T(8,128)(2,1)S(1)}, bf16[562,128]{1,0:T(8,128)(2,1)S(1)}, u32[]{:S(2)}, u32[]{:S(2)}) collective-permute-start(bf16[562,128]{1,0:T(8,128)(2,1)S(1)} %fusion.23), channel_id=1, source_target_pairs={{0,2},{2,0},{4,6},{6,4},{8,10},{10,8},{12,14},{14,12},{1,3},{3,1},... | collective-permute-start | bytes 431624 | tf_op jit(solution)/shard_map/ppermute | solution.py:402
  177.1 68.1 %collective-permute-start.30 = (bf16[562,128]{1,0:T(8,128)(2,1)}, bf16[562,128]{1,0:T(8,128)(2,1)}, u32[]{:S(2)}, u32[]{:S(2)}) collective-permute-start(bf16[562,128]{1,0:T(8,128)(2,1)} %add_convert_fusion.3), channel_id=1, source_target_pairs={{0,4},{2,6},{4,0},{6,2},{8,12},{10,14},{12,8},{14,10},{1,5},{3,7},... | collective-permute-start | bytes 431624 | tf_op jit(solution)/shard_map/ppermute | solution.py:402
  222.5 13.5 %copy-start.29 = (f32[49,8,128]{2,1,0:T(8,128)S(1)}, f32[49,8,128]{2,1,0:T(8,128)}, u32[]{:S(2)}) copy-start(f32[49,8,128]{2,1,0:T(8,128)} %copy-done.28) | copy-start | bytes 602116
  229.6 9.0 %collective-permute-start.21 = (bf16[12,48,128]{2,1,0:T(8,128)(2,1)}, bf16[12,48,128]{2,1,0:T(8,128)(2,1)S(1)}, u32[]{:S(2)}, u32[]{:S(2)}) collective-permute-start(bf16[12,48,128]{2,1,0:T(8,128)(2,1)} %broadcast_select_fusion.10), channel_id=1, source_target_pairs={{0,2},{2,4},{4,6},{6,8},{8,10},{10,12},{12,14},{14,0},{1,3},{3,5},... | collective-permute-start | bytes 442376 | tf_op jit(solution)/shard_map/ppermute | solution.py:356
  229.9 9.1 %collective-permute-start.22 = (bf16[12,48,128]{2,1,0:T(8,128)(2,1)}, bf16[12,48,128]{2,1,0:T(8,128)(2,1)S(1)}, u32[]{:S(2)}, u32[]{:S(2)}) collective-permute-start(bf16[12,48,128]{2,1,0:T(8,128)(2,1)} %broadcast_select_fusion.8), channel_id=1, source_target_pairs={{0,14},{2,0},{4,2},{6,4},{8,6},{10,8},{12,10},{14,12},{1,15},{3,1}... | collective-permute-start | bytes 442376 | tf_op jit(solution)/shard_map/ppermute | solution.py:356
  238.5 5.6 %collective-permute-start.24 = (bf16[562,128]{1,0:T(8,128)(2,1)}, bf16[562,128]{1,0:T(8,128)(2,1)}, u32[]{:S(2)}, u32[]{:S(2)}) collective-permute-start(bf16[562,128]{1,0:T(8,128)(2,1)} %pad_maximum_fusion.4), channel_id=1, source_target_pairs={{0,1},{1,0},{2,3},{3,2},{4,5},{5,4},{6,7},{7,6},{8,9},{9,8},{10,11... | collective-permute-start | bytes 431624 | tf_op jit(solution)/shard_map/ppermute | solution.py:360
  244.0 9.6 %collective-permute-start.23 = (bf16[48,48,128]{2,1,0:T(8,128)(2,1)S(1)}, bf16[48,48,128]{2,1,0:T(8,128)(2,1)S(1)}, u32[]{:S(2)}, u32[]{:S(2)}) collective-permute-start(bf16[48,48,128]{2,1,0:T(8,128)(2,1)S(1)} %slice.201), channel_id=1, source_target_pairs={{0,1},{1,0},{2,3},{3,2},{4,5},{5,4},{6,7},{7,6},{8,9},{9,8},{10,11... | collective-permute-start | bytes 1769480 | tf_op jit(solution)/shard_map/ppermute | solution.py:360
  245.1 6.2 %collective-permute-start.25 = (bf16[562,128]{1,0:T(8,128)(2,1)S(1)}, bf16[562,128]{1,0:T(8,128)(2,1)S(1)}, u32[]{:S(2)}, u32[]{:S(2)}) collective-permute-start(bf16[562,128]{1,0:T(8,128)(2,1)S(1)} %fusion.22), channel_id=1, source_target_pairs={{0,2},{2,0},{4,6},{6,4},{8,10},{10,8},{12,14},{14,12},{1,3},{3,1},... | collective-permute-start | bytes 431624 | tf_op jit(solution)/shard_map/ppermute | solution.py:402
  246.2 12.0 %collective-permute-start.31 = (bf16[562,128]{1,0:T(8,128)(2,1)S(1)}, bf16[562,128]{1,0:T(8,128)(2,1)}, u32[]{:S(2)}, u32[]{:S(2)}) collective-permute-start(bf16[562,128]{1,0:T(8,128)(2,1)S(1)} %add_convert_fusion.2), channel_id=1, source_target_pairs={{0,8},{2,10},{4,12},{6,14},{8,0},{10,2},{12,4},{14,6},{1,9},{3,11}... | collective-permute-start | bytes 431624 | tf_op jit(solution)/shard_map/ppermute | solution.py:402
  252.0 8.2 %collective-permute-start.26 = (bf16[562,128]{1,0:T(8,128)(2,1)}, bf16[562,128]{1,0:T(8,128)(2,1)}, u32[]{:S(2)}, u32[]{:S(2)}) collective-permute-start(bf16[562,128]{1,0:T(8,128)(2,1)} %add_convert_fusion.5), channel_id=1, source_target_pairs={{0,4},{2,6},{4,0},{6,2},{8,12},{10,14},{12,8},{14,10},{1,5},{3,7},... | collective-permute-start | bytes 431624 | tf_op jit(solution)/shard_map/ppermute | solution.py:402
  261.3 9.5 %collective-permute-start.27 = (bf16[562,128]{1,0:T(8,128)(2,1)S(1)}, bf16[562,128]{1,0:T(8,128)(2,1)S(1)}, u32[]{:S(2)}, u32[]{:S(2)}) collective-permute-start(bf16[562,128]{1,0:T(8,128)(2,1)S(1)} %add_convert_fusion.4), channel_id=1, source_target_pairs={{0,8},{2,10},{4,12},{6,14},{8,0},{10,2},{12,4},{14,6},{1,9},{3,11}... | collective-permute-start | bytes 431624 | tf_op jit(solution)/shard_map/ppermute | solution.py:402
  (72 other events, 263.7 us)
Sparse Core Ops, SparseCore 0:
  258.3 9.5 all-gather.1

commit v4 on v3

--- a/solution.py
+++ b/solution.py
@@ -215,7 +215,7 @@
     ]
 
 
-PARAMS = pltpu.CompilerParams(vmem_limit_bytes=40 * 1024 * 1024)
+PARAMS = pltpu.CompilerParams(vmem_limit_bytes=58 * 1024 * 1024)
 
 
 def forward_call(info, count, x, strips, tables, kern, gain, w_in, w_out):

time: 285 us -> 251 us (0.88)
  local copies, waits for them, and re-layouts: 69.8 us -> 36.3 us
  waiting for transfers between devices: 25.4 us -> 22.3 us
    unnamed x162 -> x60, local copies, waits for them, and re-layouts: 35 us -> 8.92 us
  transfers between devices with their start and end apart: 25 -> 25, of which waited for: 10 -> 11; matrix products, arithmetic and copies ran while one was open for 20% -> 24% of each run, Pallas kernels for 14% -> 15%
where the time goes in v4:
time: 251 us; the launch traced here: 250 us
  Pallas kernels  102 us (41%)
  local copies, waits for them, and re-layouts  36.3 us (14%)
  other arithmetic  36 us (14%)
  starting transfers between devices  34.4 us (14%)
  waiting for transfers between devices  22.3 us (9%)
  between operations  15 us (6%)
    pallas_call x2, Pallas kernels, backward_call(): pl.pallas_call(first_backward if first else second_backward, grid_spec=pl...  74 us
    ppermute x10, starting transfers between devices, shifted(): lax.ppermute(value, axis, [(i, (i + steps) % count) for i in range(count)])  25.3 us
    pallas_call x1, Pallas kernels, forward_call(): pl.pallas_call(forward_kernel, grid_spec=pltpu.PrefetchScalarGridSpec(num...  22.3 us
    ppermute x6, waiting for transfers between devices, reduced(): lax.ppermute(value.astype(BF), axis, [(i, i ^ step) for i in range(count)])  15.3 us
    unnamed x60, local copies, waits for them, and re-layouts  8.92 us
    ppermute x6, starting transfers between devices, reduced(): lax.ppermute(value.astype(BF), axis, [(i, i ^ step) for i in range(count)])  7.06 us
    convert_element_type x6, other arithmetic, reduced(): value = value.astype(BF).astype(F32) + got.astype(F32)  6.44 us
    pallas_call x2, Pallas kernels, collect_call(): pl.pallas_call(collect_kernel, grid_spec=pltpu.PrefetchScalarGridSpec(num...  6.09 us
  transfers between devices with their start and end apart: 25, of which 11 were waited for; matrix products, arithmetic and copies ran while one was open for 24% of the time, Pallas kernels for 15%

profile of v4, /device:TPU:0, one launch (start us, length us, event | category | flops | bytes accessed | tf_op | source)
XLA Modules:
  0.0 249.7 jit_solution(5909735673527528379)
XLA Ops:
  7.9 3.0 %collective-permute-start.10 = (s32[24,8]{0,1:T(8,128)S(1)}, s32[24,8]{0,1:T(8,128)S(1)}, u32[]{:S(2)}, u32[]{:S(2)}) collective-permute-start(s32[24,8]{0,1:T(8,128)S(1)} %pad_add_fusion), channel_id=1, source_target_pairs={{0,2},{2,4},{4,6},{6,8},{8,10},{10,12},{12,14},{14,0},{1,3},{3,5},... | collective-permute-start | bytes 2312 | tf_op jit(solution)/shard_map/ppermute | solution.py:356
  10.9 3.1 %collective-permute-start.8 = (s32[24,8]{0,1:T(8,128)S(1)}, s32[24,8]{0,1:T(8,128)S(1)}, u32[]{:S(2)}, u32[]{:S(2)}) collective-permute-start(s32[24,8]{0,1:T(8,128)S(1)} %pad_add_fusion), channel_id=1, source_target_pairs={{0,14},{2,0},{4,2},{6,4},{8,6},{10,8},{12,10},{14,12},{1,15},{3,1}... | collective-permute-start | bytes 2312 | tf_op jit(solution)/shard_map/ppermute | solution.py:356
  18.6 1.3 fusion.66
  24.2 2.2 all_gather.6
  34.6 1.3 select_reduce_fusion.10
  36.4 1.2 select_reduce_fusion.11
  39.1 1.6 collective-permute-start.9
  41.9 3.2 %collective-permute-start.11 = (bf16[12,48,128]{2,1,0:T(8,128)(2,1)S(1)}, bf16[12,48,128]{2,1,0:T(8,128)(2,1)S(1)}, u32[]{:S(2)}, u32[]{:S(2)}) collective-permute-start(bf16[12,48,128]{2,1,0:T(8,128)(2,1)S(1)} %broadcast_select_fusion.14), channel_id=1, source_target_pairs={{0,14},{2,0},{4,2},{6,4},{8,6},{10,8},{12,10},{14,12},{1,15},{3,1}... | collective-permute-start | bytes 442376 | tf_op jit(solution)/shard_map/ppermute | solution.py:356
  47.4 2.9 %collective-permute-done.14 = s32[128]{0:T(128)S(1)} collective-permute-done((s32[128]{0:T(128)S(1)}, s32[128]{0:T(128)S(1)}, u32[]{:S(2)}, u32[]{:S(2)}) %collective-permute-start.14) | collective-permute-done | bytes 544 | tf_op jit(solution)/shard_map/ppermute | solution.py:391
  51.6 22.3 %block_forward.1 = (f32[12,256,128]{2,1,0:T(8,128)}, bf16[12,16,16,128]{3,2,1,0:T(8,128)(2,1)}, bf16[12,4,48,128]{3,2,1,0:T(8,128)(2,1)}) custom-call(s32[49]{0:T(128)} %pad_add_fusion.1.info_ref, bf16[24,16,16,128]{3,2,1,0:T(8,128)(2,1)} %x_ref.3, bf16[96,48,128]{2,1,0:T(8,128)(2,1)S(1)} %get-tuple-element.1746, ...), custom_call_target="tpu_custom_call" | custom-call | tf_op jit(solution)/shard_map/block_forward/pallas_call | solution.py:223
  74.6 1.6 collective-permute-done.15
  79.5 4.8 %collective-permute-start.17 = (bf16[12,48,128]{2,1,0:T(8,128)(2,1)S(1)}, bf16[12,48,128]{2,1,0:T(8,128)(2,1)S(1)}, u32[]{:S(2)}, u32[]{:S(2)}) collective-permute-start(bf16[12,48,128]{2,1,0:T(8,128)(2,1)S(1)} %broadcast_select_fusion.12), channel_id=1, source_target_pairs={{0,14},{2,0},{4,2},{6,4},{8,6},{10,8},{12,10},{14,12},{1,15},{3,1}... | collective-permute-start | bytes 442376 | tf_op jit(solution)/shard_map/ppermute | solution.py:356
  84.2 1.3 pad_add_fusion.2.info_ref
  92.0 41.6 %block_backward.2 = (f32[12,16,16,128]{3,2,1,0:T(8,128)}, bf16[12,4,48,128]{3,2,1,0:T(8,128)(2,1)S(1)}, f32[49,8,128]{2,1,0:T(8,128)}, f32[8,128]{1,0:T(8,128)}, f32[128,512]{1,0:T(8,128)}, /*index=5*/f32[128,512]{1,0:T(8,128)}) custom-call(s32[49]{0:T(128)} %pad_add_fusion.2.info_ref, bf16[12,16,16,128]{3,2,1,0:T(8,128)(2,1)} %get-tuple-element.781.x_ref, ...), custom_call_target="tpu_custom_call" | custom-call | tf_op jit(solution)/shard_map/block_backward/pallas_call | solution.py:309
  136.1 4.8 %collective-permute-start.19 = (bf16[12,48,128]{2,1,0:T(8,128)(2,1)S(1)}, bf16[12,48,128]{2,1,0:T(8,128)(2,1)S(1)}, u32[]{:S(2)}, u32[]{:S(2)}) collective-permute-start(bf16[12,48,128]{2,1,0:T(8,128)(2,1)S(1)} %broadcast_select_fusion.9), channel_id=1, source_target_pairs={{0,14},{2,0},{4,2},{6,4},{8,6},{10,8},{12,10},{14,12},{1,15},{3,1}... | collective-permute-start | bytes 442376 | tf_op jit(solution)/shard_map/ppermute | solution.py:356
  145.5 3.0 %collect_strips.2 = f32[96,48,128]{2,1,0:T(8,128)S(1)} custom-call(s32[72]{0:T(128)} %pad_add_fusion.3.aims_ref, bf16[48,48,128]{2,1,0:T(8,128)(2,1)S(1)} %bitcast.184, bf16[12,48,128]{2,1,0:T(8,128)(2,1)} %copy-done.20, bf16[12,48,128]{2,1,0:T(8,128)(2,1)} %copy-done.22), custom_call_target="tpu_custom_call" | custom-call | tf_op jit(solution)/shard_map/collect_strips/pallas_call | solution.py:289
  150.0 1.7 fusion.23
  152.0 1.6 copy.178.rest_10_
  153.6 4.2 %collective-permute-done.29 = bf16[562,128]{1,0:T(8,128)(2,1)} collective-permute-done((bf16[562,128]{1,0:T(8,128)(2,1)}, bf16[562,128]{1,0:T(8,128)(2,1)}, u32[]{:S(2)}, u32[]{:S(2)}) %collective-permute-start.29) | collective-permute-done | bytes 143904 | tf_op jit(solution)/shard_map/ppermute | solution.py:402
  157.9 1.7 add_convert_fusion.3
  159.6 32.4 %block_backward.3 = (f32[12,16,16,128]{3,2,1,0:T(8,128)}, bf16[12,4,48,128]{3,2,1,0:T(8,128)(2,1)}, f32[49,8,128]{2,1,0:T(8,128)}, f32[8,128]{1,0:T(8,128)}, f32[128,512]{1,0:T(8,128)}, /*index=5*/f32[128,512]{1,0:T(8,128)}) custom-call(s32[49]{0:T(128)} %pad_add_fusion.1.info_ref, bf16[24,16,16,128]{3,2,1,0:T(8,128)(2,1)} %x_ref.3, ...), custom_call_target="tpu_custom_call" | custom-call | tf_op jit(solution)/shard_map/block_backward/pallas_call | solution.py:309
  192.0 1.8 gather_fusion.15
  193.8 1.8 gather_fusion.14
  198.6 4.1 %collective-permute-start.22 = (bf16[12,48,128]{2,1,0:T(8,128)(2,1)S(1)}, bf16[12,48,128]{2,1,0:T(8,128)(2,1)S(1)}, u32[]{:S(2)}, u32[]{:S(2)}) collective-permute-start(bf16[12,48,128]{2,1,0:T(8,128)(2,1)S(1)} %broadcast_select_fusion.8), channel_id=1, source_target_pairs={{0,14},{2,0},{4,2},{6,4},{8,6},{10,8},{12,10},{14,12},{1,15},{3,1}... | collective-permute-start | bytes 442376 | tf_op jit(solution)/shard_map/ppermute | solution.py:356
  205.9 1.4 collective-permute-done.22.after_ref
  207.9 3.0 %collect_strips.3 = f32[96,48,128]{2,1,0:T(8,128)S(1)} custom-call(s32[72]{0:T(128)} %pad_add_fusion.3.aims_ref, bf16[48,48,128]{2,1,0:T(8,128)(2,1)S(1)} %bitcast.180, bf16[12,48,128]{2,1,0:T(8,128)(2,1)} %copy-done.19, bf16[12,48,128]{2,1,0:T(8,128)(2,1)} %copy-done.21), custom_call_target="tpu_custom_call" | custom-call | tf_op jit(solution)/shard_map/collect_strips/pallas_call | solution.py:289
  213.5 4.6 %collective-permute-start.31 = (bf16[562,128]{1,0:T(8,128)(2,1)S(1)}, bf16[562,128]{1,0:T(8,128)(2,1)}, u32[]{:S(2)}, u32[]{:S(2)}) collective-permute-start(bf16[562,128]{1,0:T(8,128)(2,1)S(1)} %add_convert_fusion.2), channel_id=1, source_target_pairs={{0,8},{2,10},{4,12},{6,14},{8,0},{10,2},{12,4},{14,6},{1,9},{3,11}... | collective-permute-start | bytes 431624 | tf_op jit(solution)/shard_map/ppermute | solution.py:402
  218.5 1.5 collective-permute-start.26
  221.1 2.5 %add_convert_fusion = bf16[12,16,16,128]{3,2,1,0:T(8,128)(2,1)} fusion(f32[12,16,16,128]{3,2,1,0:T(8,128)} %get-tuple-element.789, f32[12,16,16,128]{3,2,1,0:T(8,128)S(1)} %bitcast.186), kind=kLoop, calls=%fused_computation.138 | loop fusion | flops 786432 | bytes 3932160 | tf_op jit(solution)/shard_map/convert_element_type | solution.py:562
  223.6 1.4 collective-permute-done.31
  228.7 8.1 %collective-permute-done.27 = bf16[562,128]{1,0:T(8,128)(2,1)S(1)} collective-permute-done((bf16[562,128]{1,0:T(8,128)(2,1)S(1)}, bf16[562,128]{1,0:T(8,128)(2,1)S(1)}, u32[]{:S(2)}, u32[]{:S(2)}) %collective-permute-start.27) | collective-permute-done | bytes 143904 | tf_op jit(solution)/shard_map/ppermute | solution.py:402
  239.9 3.0 %copy.251 = bf16[24,16,16,128]{3,2,1,0:T(8,128)(2,1)} copy(bf16[24,16,16,128]{3,2,1,0:T(8,128)(2,1)} %all-gather.2.cloned.1.call-done) | data formatting | bytes 3145728
  (259 shorter events, 60.6 us)
Async XLA Ops:
  7.2 232.7 %all-gather.2.cloned.1.call-start = ((), (), s32[]{:S(2)}) async-start(), calls=%async_computation | async-start | bytes 2359296 | tf_op jit(solution)/shard_map/all_gather | solution.py:563
  7.9 23.1 %collective-permute-start.10 = (s32[24,8]{0,1:T(8,128)S(1)}, s32[24,8]{0,1:T(8,128)S(1)}, u32[]{:S(2)}, u32[]{:S(2)}) collective-permute-start(s32[24,8]{0,1:T(8,128)S(1)} %pad_add_fusion), channel_id=1, source_target_pairs={{0,2},{2,4},{4,6},{6,8},{8,10},{10,12},{12,14},{14,0},{1,3},{3,5},... | collective-permute-start | bytes 2312 | tf_op jit(solution)/shard_map/ppermute | solution.py:356
  10.9 20.2 %collective-permute-start.8 = (s32[24,8]{0,1:T(8,128)S(1)}, s32[24,8]{0,1:T(8,128)S(1)}, u32[]{:S(2)}, u32[]{:S(2)}) collective-permute-start(s32[24,8]{0,1:T(8,128)S(1)} %pad_add_fusion), channel_id=1, source_target_pairs={{0,14},{2,0},{4,2},{6,4},{8,6},{10,8},{12,10},{14,12},{1,15},{3,1}... | collective-permute-start | bytes 2312 | tf_op jit(solution)/shard_map/ppermute | solution.py:356
  16.4 13.5 %collective-permute-start.12 = (s32[128]{0:T(128)S(1)}, s32[128]{0:T(128)S(1)}, u32[]{:S(2)}, u32[]{:S(2)}) collective-permute-start(s32[128]{0:T(128)S(1)} %broadcast_in_dim.441), channel_id=1, source_target_pairs={{0,2},{2,0},{4,6},{6,4},{8,10},{10,8},{12,14},{14,12},{1,3},{3,1},... | collective-permute-start | bytes 1544 | tf_op jit(solution)/shard_map/ppermute | solution.py:391
  30.5 14.6 %collective-permute-start.13 = (s32[128]{0:T(128)S(1)}, s32[128]{0:T(128)S(1)}, u32[]{:S(2)}, u32[]{:S(2)}) collective-permute-start(s32[128]{0:T(128)S(1)} %broadcast_maximum_fusion), channel_id=1, source_target_pairs={{0,4},{2,6},{4,0},{6,2},{8,12},{10,14},{12,8},{14,10},{1,5},{3,7},... | collective-permute-start | bytes 1544 | tf_op jit(solution)/shard_map/ppermute | solution.py:391
  32.2 18.6 %copy-start.24 = (s32[12,4]{1,0:T(8,128)}, s32[12,4]{1,0:T(8,128)S(1)}, u32[]{:S(2)}) copy-start(s32[12,4]{1,0:T(8,128)S(1)} %copy.167) | copy-start | bytes 580
  32.9 17.9 %copy-start.25 = (s32[12,4]{1,0:T(8,128)}, s32[12,4]{1,0:T(8,128)S(1)}, u32[]{:S(2)}) copy-start(s32[12,4]{1,0:T(8,128)S(1)} %copy.163) | copy-start | bytes 580
  39.1 11.6 %collective-permute-start.9 = (bf16[12,48,128]{2,1,0:T(8,128)(2,1)S(1)}, bf16[12,48,128]{2,1,0:T(8,128)(2,1)S(1)}, u32[]{:S(2)}, u32[]{:S(2)}) collective-permute-start(bf16[12,48,128]{2,1,0:T(8,128)(2,1)S(1)} %broadcast_select_fusion.15), channel_id=1, source_target_pairs={{0,2},{2,4},{4,6},{6,8},{8,10},{10,12},{12,14},{14,0},{1,3},{3,5},... | collective-permute-start | bytes 442376 | tf_op jit(solution)/shard_map/ppermute | solution.py:356
  41.9 8.7 %collective-permute-start.11 = (bf16[12,48,128]{2,1,0:T(8,128)(2,1)S(1)}, bf16[12,48,128]{2,1,0:T(8,128)(2,1)S(1)}, u32[]{:S(2)}, u32[]{:S(2)}) collective-permute-start(bf16[12,48,128]{2,1,0:T(8,128)(2,1)S(1)} %broadcast_select_fusion.14), channel_id=1, source_target_pairs={{0,14},{2,0},{4,2},{6,4},{8,6},{10,8},{12,10},{14,12},{1,15},{3,1}... | collective-permute-start | bytes 442376 | tf_op jit(solution)/shard_map/ppermute | solution.py:356
  45.8 4.5 %collective-permute-start.14 = (s32[128]{0:T(128)S(1)}, s32[128]{0:T(128)S(1)}, u32[]{:S(2)}, u32[]{:S(2)}) collective-permute-start(s32[128]{0:T(128)S(1)} %fusion.71), channel_id=1, source_target_pairs={{0,8},{2,10},{4,12},{6,14},{8,0},{10,2},{12,4},{14,6},{1,9},{3,11}... | collective-permute-start | bytes 1544 | tf_op jit(solution)/shard_map/ppermute | solution.py:391
  50.9 23.1 %copy-start = (bf16[96,48,128]{2,1,0:T(8,128)(2,1)}, bf16[96,48,128]{2,1,0:T(8,128)(2,1)S(1)}, u32[]{:S(2)}) copy-start(bf16[96,48,128]{2,1,0:T(8,128)(2,1)S(1)} %get-tuple-element.1746) | copy-start | bytes 3538948
  50.9 39.7 %copy-start.4 = (bf16[48,48,128]{2,1,0:T(8,128)(2,1)}, bf16[48,48,128]{2,1,0:T(8,128)(2,1)S(1)}, u32[]{:S(2)}) copy-start(bf16[48,48,128]{2,1,0:T(8,128)(2,1)S(1)} %get-tuple-element.780.after_ref) | copy-start | bytes 1769476
  50.9 39.7 %copy-start.5 = (bf16[48,48,128]{2,1,0:T(8,128)(2,1)}, bf16[48,48,128]{2,1,0:T(8,128)(2,1)S(1)}, u32[]{:S(2)}) copy-start(bf16[48,48,128]{2,1,0:T(8,128)(2,1)S(1)} %get-tuple-element.779.before_ref) | copy-start | bytes 1769476
  73.9 2.3 collective-permute-start.15
  78.7 11.0 %collective-permute-start.16 = (bf16[12,48,128]{2,1,0:T(8,128)(2,1)S(1)}, bf16[12,48,128]{2,1,0:T(8,128)(2,1)S(1)}, u32[]{:S(2)}, u32[]{:S(2)}) collective-permute-start(bf16[12,48,128]{2,1,0:T(8,128)(2,1)S(1)} %broadcast_select_fusion.13), channel_id=1, source_target_pairs={{0,2},{2,4},{4,6},{6,8},{8,10},{10,12},{12,14},{14,0},{1,3},{3,5},... | collective-permute-start | bytes 442376 | tf_op jit(solution)/shard_map/ppermute | solution.py:356
  79.5 10.1 %collective-permute-start.17 = (bf16[12,48,128]{2,1,0:T(8,128)(2,1)S(1)}, bf16[12,48,128]{2,1,0:T(8,128)(2,1)S(1)}, u32[]{:S(2)}, u32[]{:S(2)}) collective-permute-start(bf16[12,48,128]{2,1,0:T(8,128)(2,1)S(1)} %broadcast_select_fusion.12), channel_id=1, source_target_pairs={{0,14},{2,0},{4,2},{6,4},{8,6},{10,8},{12,10},{14,12},{1,15},{3,1}... | collective-permute-start | bytes 442376 | tf_op jit(solution)/shard_map/ppermute | solution.py:356
  92.0 43.8 %copy-start.26 = (pred[12]{0:T(512)(128)(4,1)S(1)}, pred[12]{0:T(512)(128)(4,1)}, u32[]{:S(2)}) copy-start(pred[12]{0:T(512)(128)(4,1)} %get-tuple-element.1141) | copy-start | bytes 40
  92.0 44.0 %copy-start.27 = (pred[12]{0:T(512)(128)(4,1)S(1)}, pred[12]{0:T(512)(128)(4,1)}, u32[]{:S(2)}) copy-start(pred[12]{0:T(512)(128)(4,1)} %get-tuple-element.1140) | copy-start | bytes 40
  136.0 8.2 %collective-permute-start.18 = (bf16[12,48,128]{2,1,0:T(8,128)(2,1)S(1)}, bf16[12,48,128]{2,1,0:T(8,128)(2,1)S(1)}, u32[]{:S(2)}, u32[]{:S(2)}) collective-permute-start(bf16[12,48,128]{2,1,0:T(8,128)(2,1)S(1)} %broadcast_select_fusion.11), channel_id=1, source_target_pairs={{0,2},{2,4},{4,6},{6,8},{8,10},{10,12},{12,14},{14,0},{1,3},{3,5},... | collective-permute-start | bytes 442376 | tf_op jit(solution)/shard_map/ppermute | solution.py:356
  136.1 8.5 %collective-permute-start.19 = (bf16[12,48,128]{2,1,0:T(8,128)(2,1)S(1)}, bf16[12,48,128]{2,1,0:T(8,128)(2,1)S(1)}, u32[]{:S(2)}, u32[]{:S(2)}) collective-permute-start(bf16[12,48,128]{2,1,0:T(8,128)(2,1)S(1)} %broadcast_select_fusion.9), channel_id=1, source_target_pairs={{0,14},{2,0},{4,2},{6,4},{8,6},{10,8},{12,10},{14,12},{1,15},{3,1}... | collective-permute-start | bytes 442376 | tf_op jit(solution)/shard_map/ppermute | solution.py:356
  144.0 6.0 %collective-permute-start.28 = (bf16[562,128]{1,0:T(8,128)(2,1)}, bf16[562,128]{1,0:T(8,128)(2,1)}, u32[]{:S(2)}, u32[]{:S(2)}) collective-permute-start(bf16[562,128]{1,0:T(8,128)(2,1)} %pad_maximum_fusion.5), channel_id=1, source_target_pairs={{0,1},{1,0},{2,3},{3,2},{4,5},{5,4},{6,7},{7,6},{8,9},{9,8},{10,11... | collective-permute-start | bytes 431624 | tf_op jit(solution)/shard_map/ppermute | solution.py:360
  149.6 9.9 %collective-permute-start.20 = (bf16[48,48,128]{2,1,0:T(8,128)(2,1)}, bf16[48,48,128]{2,1,0:T(8,128)(2,1)}, u32[]{:S(2)}, u32[]{:S(2)}) collective-permute-start(bf16[48,48,128]{2,1,0:T(8,128)(2,1)} %slice.202), channel_id=1, source_target_pairs={{0,1},{1,0},{2,3},{3,2},{4,5},{5,4},{6,7},{7,6},{8,9},{9,8},{10,11... | collective-permute-start | bytes 1769480 | tf_op jit(solution)/shard_map/ppermute | solution.py:360
  151.8 6.1 %collective-permute-start.29 = (bf16[562,128]{1,0:T(8,128)(2,1)}, bf16[562,128]{1,0:T(8,128)(2,1)}, u32[]{:S(2)}, u32[]{:S(2)}) collective-permute-start(bf16[562,128]{1,0:T(8,128)(2,1)} %fusion.23), channel_id=1, source_target_pairs={{0,2},{2,0},{4,6},{6,4},{8,10},{10,8},{12,14},{14,12},{1,3},{3,1},... | collective-permute-start | bytes 431624 | tf_op jit(solution)/shard_map/ppermute | solution.py:402
  159.5 52.9 %collective-permute-start.30 = (bf16[562,128]{1,0:T(8,128)(2,1)}, bf16[562,128]{1,0:T(8,128)(2,1)}, u32[]{:S(2)}, u32[]{:S(2)}) collective-permute-start(bf16[562,128]{1,0:T(8,128)(2,1)} %add_convert_fusion.3), channel_id=1, source_target_pairs={{0,4},{2,6},{4,0},{6,2},{8,12},{10,14},{12,8},{14,10},{1,5},{3,7},... | collective-permute-start | bytes 431624 | tf_op jit(solution)/shard_map/ppermute | solution.py:402
  197.9 8.0 %collective-permute-start.21 = (bf16[12,48,128]{2,1,0:T(8,128)(2,1)S(1)}, bf16[12,48,128]{2,1,0:T(8,128)(2,1)S(1)}, u32[]{:S(2)}, u32[]{:S(2)}) collective-permute-start(bf16[12,48,128]{2,1,0:T(8,128)(2,1)S(1)} %broadcast_select_fusion.10), channel_id=1, source_target_pairs={{0,2},{2,4},{4,6},{6,8},{8,10},{10,12},{12,14},{14,0},{1,3},{3,5},... | collective-permute-start | bytes 442376 | tf_op jit(solution)/shard_map/ppermute | solution.py:356
  198.6 8.7 %collective-permute-start.22 = (bf16[12,48,128]{2,1,0:T(8,128)(2,1)S(1)}, bf16[12,48,128]{2,1,0:T(8,128)(2,1)S(1)}, u32[]{:S(2)}, u32[]{:S(2)}) collective-permute-start(bf16[12,48,128]{2,1,0:T(8,128)(2,1)S(1)} %broadcast_select_fusion.8), channel_id=1, source_target_pairs={{0,14},{2,0},{4,2},{6,4},{8,6},{10,8},{12,10},{14,12},{1,15},{3,1}... | collective-permute-start | bytes 442376 | tf_op jit(solution)/shard_map/ppermute | solution.py:356
  205.8 5.3 %collective-permute-start.24 = (bf16[562,128]{1,0:T(8,128)(2,1)}, bf16[562,128]{1,0:T(8,128)(2,1)}, u32[]{:S(2)}, u32[]{:S(2)}) collective-permute-start(bf16[562,128]{1,0:T(8,128)(2,1)} %pad_maximum_fusion.4), channel_id=1, source_target_pairs={{0,1},{1,0},{2,3},{3,2},{4,5},{5,4},{6,7},{7,6},{8,9},{9,8},{10,11... | collective-permute-start | bytes 431624 | tf_op jit(solution)/shard_map/ppermute | solution.py:360
  211.1 9.0 %collective-permute-start.23 = (bf16[48,48,128]{2,1,0:T(8,128)(2,1)S(1)}, bf16[48,48,128]{2,1,0:T(8,128)(2,1)S(1)}, u32[]{:S(2)}, u32[]{:S(2)}) collective-permute-start(bf16[48,48,128]{2,1,0:T(8,128)(2,1)S(1)} %slice.201), channel_id=1, source_target_pairs={{0,1},{1,0},{2,3},{3,2},{4,5},{5,4},{6,7},{7,6},{8,9},{9,8},{10,11... | collective-permute-start | bytes 1769480 | tf_op jit(solution)/shard_map/ppermute | solution.py:360
  212.2 6.3 %collective-permute-start.25 = (bf16[562,128]{1,0:T(8,128)(2,1)S(1)}, bf16[562,128]{1,0:T(8,128)(2,1)S(1)}, u32[]{:S(2)}, u32[]{:S(2)}) collective-permute-start(bf16[562,128]{1,0:T(8,128)(2,1)S(1)} %fusion.22), channel_id=1, source_target_pairs={{0,2},{2,0},{4,6},{6,4},{8,10},{10,8},{12,14},{14,12},{1,3},{3,1},... | collective-permute-start | bytes 431624 | tf_op jit(solution)/shard_map/ppermute | solution.py:402
  213.5 11.5 %collective-permute-start.31 = (bf16[562,128]{1,0:T(8,128)(2,1)S(1)}, bf16[562,128]{1,0:T(8,128)(2,1)}, u32[]{:S(2)}, u32[]{:S(2)}) collective-permute-start(bf16[562,128]{1,0:T(8,128)(2,1)S(1)} %add_convert_fusion.2), channel_id=1, source_target_pairs={{0,8},{2,10},{4,12},{6,14},{8,0},{10,2},{12,4},{14,6},{1,9},{3,11}... | collective-permute-start | bytes 431624 | tf_op jit(solution)/shard_map/ppermute | solution.py:402
  218.5 8.6 %collective-permute-start.26 = (bf16[562,128]{1,0:T(8,128)(2,1)S(1)}, bf16[562,128]{1,0:T(8,128)(2,1)}, u32[]{:S(2)}, u32[]{:S(2)}) collective-permute-start(bf16[562,128]{1,0:T(8,128)(2,1)S(1)} %add_convert_fusion.5), channel_id=1, source_target_pairs={{0,4},{2,6},{4,0},{6,2},{8,12},{10,14},{12,8},{14,10},{1,5},{3,7},... | collective-permute-start | bytes 431624 | tf_op jit(solution)/shard_map/ppermute | solution.py:402
  228.1 8.8 %collective-permute-start.27 = (bf16[562,128]{1,0:T(8,128)(2,1)S(1)}, bf16[562,128]{1,0:T(8,128)(2,1)S(1)}, u32[]{:S(2)}, u32[]{:S(2)}) collective-permute-start(bf16[562,128]{1,0:T(8,128)(2,1)S(1)} %add_convert_fusion.4), channel_id=1, source_target_pairs={{0,8},{2,10},{4,12},{6,14},{8,0},{10,2},{12,4},{14,6},{1,9},{3,11}... | collective-permute-start | bytes 431624 | tf_op jit(solution)/shard_map/ppermute | solution.py:402
  (21 other events, 112.4 us)
Sparse Core Ops, SparseCore 0:
  223.7 10.6 all-gather.1
